TPU v7x, 256 devices: a whole 4x4x8 slice. The times are simulated.
256 devices in a mesh: row: 8 (over z), col: 32 (over x, y, core).
Axes of the slice: x: 4, y: 4, z: 8, core: 2. Of those that a mesh axis runs over, the one named last changes fastest.
Arguments:
- schur_blocks: bfloat16 [8, 32, 2048, 2048], P('row', 'col'), as said below
- rigid_modes: float32 [8, 32, 6, 2048], P('row', 'col'), may hold values from -0.125 to 0.125
- floating: int32 [8, 32], P('row', 'col'), may hold values 0 or 1
- block_order: int32 [8, 32, 16], P('row', 'col'), may hold values from 0 to 15, each once within a row
- coarse_inverse: float32 [6, 8, 32, 6, 8, 32], P(None, 'row', None, None, None, 'col'), may hold values from -4 to 4
- right_side: float32 [8, 32, 2, 128, 512], P('row', 'col')
Outputs:
- multipliers: float32 [8, 32, 2, 128, 512], P('row', 'col')
- residual: float32 [8, 32, 2, 128, 512], P('row', 'col')
Inputs may be any that keep to these rules, and one draw needn't show every extreme that they name: `schur_blocks`: each subdomain's matrix is symmetric. `block_order`: each subdomain's 16 entries name every block of its face order once.
All inputs are finite; a program needn't handle non-finite values. No bound on the sum of `floating` on one device may be relied on, other than what follows from the above.
Results may differ from a plain program's by a relative error of at most 0.0003.
Values sent between devices are 32-bit elements; how exact they have to be, the bound alone decides.
No kernel may reach another device: no remote copies, remote signals or barrier semaphores. Data moves between devices by JAX's collectives and lax.ppermute only.
A program may use at most 128 MiB of HBM per device.

v0:
```python
import jax
import jax.numpy as jnp
from jax import lax
from jax.sharding import PartitionSpec as P

M = 512
NS = 2048
BLK = 128
NB = 16
ITERS = 3


highest = lax.Precision.HIGHEST


def shifted(value, axis, steps):
    count = lax.axis_size(axis)
    initial, last = (max(0, -steps), min(count, count - steps))
    return lax.ppermute(value, axis, [(source, source + steps) for source in range(initial, last)])


def per_device(schur_blocks, rigid_modes, floating, block_order, coarse_inverse, right_side):
    matrix = schur_blocks[0, 0].astype(jnp.float32)
    order_row = block_order[0, 0]
    count_rhs = right_side.shape[3]
    labels = jnp.arange(NB, dtype=jnp.int32)
    inverse = jnp.sum(
        labels[:, None] * (order_row[:, None] == labels[None, :]).astype(jnp.int32), axis=0
    )
    mode_all = rigid_modes[0, 0] * floating[0, 0].astype(jnp.float32)
    weights = jnp.transpose(coarse_inverse[:, 0, :, :, :, 0], (1, 0, 2, 3))

    def coarse_solve(coarse_rhs):
        gathered = lax.all_gather(coarse_rhs[None], "row", axis=0, tiled=True)
        return lax.psum_scatter(
            jnp.einsum("cabr,rbk->cak", weights, gathered, precision=highest),
            "col",
            scatter_dimension=0,
            tiled=True,
        )[0]

    def mode_product(modes_block, faces):
        return jnp.einsum("an,kn->ak", modes_block, faces, precision=highest)

    def mode_spread(coarse_values, modes_block):
        return jnp.einsum("ak,an->kn", coarse_values, modes_block, precision=highest)

    def correction(vector):
        north_copy = shifted(vector[0], "row", 1)
        west_copy = shifted(vector[1], "col", 1)
        copies = jnp.stack([-north_copy, vector[0], -west_copy, vector[1]], axis=1).reshape(
            count_rhs, NS
        )
        coarse_values = coarse_solve(mode_product(mode_all, copies))
        spread = mode_spread(coarse_values, mode_all).reshape(count_rhs, 4, M)
        south_edge = spread[:, 1] - shifted(spread[:, 0], "row", -1)
        east_edge = spread[:, 3] - shifted(spread[:, 2], "col", -1)
        return jnp.stack([south_edge, east_edge], axis=0)

    start_side = right_side[0, 0]
    residual = start_side - correction(start_side)
    multipliers = jnp.zeros_like(start_side)
    direction = residual
    norm_now = lax.psum(jnp.sum(residual * residual, axis=(0, 2)), ("row", "col"))
    for iteration in range(ITERS):
        south_part = direction[0]
        east_part = direction[1]
        north_face = shifted(south_part, "row", 1)
        west_face = shifted(east_part, "col", 1)
        stacked = jnp.stack([-north_face, south_part, -west_face, east_part], axis=1).reshape(
            count_rhs, NB, BLK
        )
        permuted = jnp.take(stacked, order_row, axis=1).reshape(count_rhs, NS)
        product = jnp.dot(
            permuted, matrix, precision=highest, preferred_element_type=jnp.float32
        ).reshape(count_rhs, NB, BLK)
        restored = jnp.take(product, inverse, axis=1).reshape(count_rhs, 4, M)
        apply_south_edge = restored[:, 1] - shifted(restored[:, 0], "row", -1)
        apply_east_edge = restored[:, 3] - shifted(restored[:, 2], "col", -1)
        schur_image = jnp.stack([apply_south_edge, apply_east_edge], axis=0)
        curvature = lax.psum(jnp.sum(direction * schur_image, axis=(0, 2)), ("row", "col"))
        projected = schur_image - correction(schur_image)
        step_size = (norm_now / curvature)[None, :, None]
        multipliers = multipliers + step_size * direction
        residual = residual - step_size * projected
        if iteration + 1 < ITERS:
            norm_later = lax.psum(jnp.sum(residual * residual, axis=(0, 2)), ("row", "col"))
            direction = residual + (norm_later / norm_now)[None, :, None] * direction
            norm_now = norm_later
    return (multipliers[None, None], residual[None, None])


def solution(mesh):
    placed = (
        P("row", "col", None, None),
        P("row", "col", None, None),
        P("row", "col"),
        P("row", "col", None),
        P(None, "row", None, None, None, "col"),
        P("row", "col", None, None, None),
    )
    return jax.shard_map(
        per_device,
        mesh=mesh,
        in_specs=placed,
        out_specs=(P("row", "col", None, None, None), P("row", "col", None, None, None)),
        check_vma=False,
    )
```

profile of v0, /device:TPU:1, one launch (start us, length us, event | category | flops | bytes accessed | tf_op | source)
XLA Modules:
  0.0 1231.4 jit_solution(7125695766259366308)
XLA Ops:
  8.5 4.6 collective-permute-start.1
  13.3 3.6 collective-permute-start
  19.0 3.0 collective-permute-done
  22.8 22.0 %all-gather.4 = f32[8,6,128]{2,1,0:T(8,128)S(1)} all-gather(f32[1,6,128]{2,1,0:T(8,128)S(1)} %convolution_bitcast_fusion.7), channel_id=2, replica_groups=mesh['row'=8,'col'=32] {'row'}, dimensions={0}, use_global_device_ids=true | all-gather | bytes 27648 | tf_op jit(solution)/shard_map/all_gather | solution.py:34
  47.9 112.9 %all-reduce.10.cloned.1.call-done = f32[32,6,128]{2,0,1:T(8,128)} async-done(((f32[32,6,128]{2,0,1:T(8,128)}), f32[32,6,128]{2,0,1:T(8,128)}) %all-reduce.10.cloned.1.call-update) | async-done | bytes 98320
  164.5 2.8 collective-permute-start.3
  167.5 4.5 collective-permute-done.2
  173.7 4.1 collective-permute-start.5
  177.9 3.2 collective-permute-start.4
  181.1 12.4 %copy.203 = bf16[2048,2048]{1,0:T(8,128)(2,1)} copy(bf16[2048,2048]{0,1:T(8,128)(2,1)} %bitcast.357) | data formatting | bytes 16777216 | tf_op jit(solution)/shard_map/dot_general | solution.py:74
  196.0 2.5 copy.147
  201.4 2.5 copy.148
  204.0 11.3 fusion.67
  225.2 4.6 collective-permute-done.7
  232.8 3.2 collective-permute-start.8
  236.1 6.1 collective-permute-done.8
  245.4 20.5 %all-gather.5 = f32[8,6,128]{2,1,0:T(8,128)S(1)} all-gather(f32[1,6,128]{2,1,0:T(8,128)S(1)} %convolution_bitcast_fusion.6), channel_id=3, replica_groups=mesh['row'=8,'col'=32] {'row'}, dimensions={0}, use_global_device_ids=true | all-gather | bytes 27648 | tf_op jit(solution)/shard_map/all_gather | solution.py:34
  267.2 114.5 %all-reduce.12.cloned.1.call-done = f32[32,6,128]{2,0,1:T(8,128)} async-done(((f32[32,6,128]{2,0,1:T(8,128)}), f32[32,6,128]{2,0,1:T(8,128)}) %all-reduce.12.cloned.1.call-update) | async-done | bytes 98320
  386.2 2.8 collective-permute-start.11
  389.2 78.2 %all-reduce.4 = (f32[128]{0:T(128)S(1)}, f32[128]{0:T(128)S(1)}) all-reduce(f32[128]{0:T(128)S(1)} %get-tuple-element.4, f32[128]{0:T(128)S(1)} %get-tuple-element.3), channel_id=1, replica_groups=mesh['row'=8,'col'=32] {'row','col'}, use_global_device_ids=true, to_apply=%region_2.0 | all-reduce | flops 256 | bytes 2048 | tf_op jit(solution)/shard_map/psum | solution.py:64
  469.6 73.2 %psum.44 = f32[128]{0:T(128)S(1)} all-reduce(f32[128]{0:T(128)S(1)} %get-tuple-element.9), channel_id=1, replica_groups=mesh['row'=8,'col'=32] {'row','col'}, use_global_device_ids=true, to_apply=%region_8.10 | all-reduce | flops 128 | bytes 1024 | tf_op jit(solution)/shard_map/psum | solution.py:87
  543.1 3.2 collective-permute-start.13
  546.3 3.7 collective-permute-start.12
  550.0 5.8 collective-permute-done.12
  556.8 2.5 copy.159
  559.4 2.5 copy.160
  561.9 2.8 gather_fusion.2
  564.7 2.3 select_bitcast_fusion.3
  567.0 2.5 copy.161
  569.6 12.1 fusion.68
  581.6 2.8 gather_fusion.3
  584.4 2.3 select_bitcast_fusion.2
  586.8 2.5 copy.164
  599.2 2.2 collective-permute-done.15
  607.6 3.8 collective-permute-start.16
  611.4 5.2 collective-permute-done.16
  617.7 2.5 copy.169
  622.1 19.1 %all-gather.6 = f32[8,6,128]{2,1,0:T(8,128)S(1)} all-gather(f32[1,6,128]{2,1,0:T(8,128)S(1)} %convolution_bitcast_fusion.5), channel_id=4, replica_groups=mesh['row'=8,'col'=32] {'row'}, dimensions={0}, use_global_device_ids=true | all-gather | bytes 27648 | tf_op jit(solution)/shard_map/all_gather | solution.py:34
  642.3 112.8 %all-reduce.14.cloned.1.call-done = f32[32,6,128]{2,0,1:T(8,128)} async-done(((f32[32,6,128]{2,0,1:T(8,128)}), f32[32,6,128]{2,0,1:T(8,128)}) %all-reduce.14.cloned.1.call-update) | async-done | bytes 98320
  760.8 2.8 collective-permute-start.19
  763.8 78.2 %psum.45 = f32[128]{0:T(128)S(1)} all-reduce(f32[128]{0:T(128)S(1)} %multiply_reduce_fusion.1), channel_id=1, replica_groups=mesh['row'=8,'col'=32] {'row','col'}, use_global_device_ids=true, to_apply=%region_10.12 | all-reduce | flops 128 | bytes 1024 | tf_op jit(solution)/shard_map/psum | solution.py:81
  845.1 73.2 %psum.46 = f32[128]{0:T(128)S(1)} all-reduce(f32[128]{0:T(128)S(1)} %get-tuple-element.7), channel_id=1, replica_groups=mesh['row'=8,'col'=32] {'row','col'}, use_global_device_ids=true, to_apply=%region_13.15 | all-reduce | flops 128 | bytes 1024 | tf_op jit(solution)/shard_map/psum | solution.py:87
  919.6 3.2 collective-permute-start.21
  922.8 3.7 collective-permute-start.20
  926.5 5.8 collective-permute-done.20
  933.4 2.5 copy.172
  935.9 2.5 copy.173
  938.4 2.8 gather_fusion.4
  941.3 2.3 select_bitcast_fusion.1
  943.6 2.5 copy.174
  946.1 12.1 fusion.69
  958.2 2.8 gather_fusion.5
  961.0 2.4 select_bitcast_fusion
  963.4 2.6 copy.177
  975.9 2.2 collective-permute-done.23
  984.3 3.8 collective-permute-start.24
  988.1 5.2 collective-permute-done.24
  994.4 2.6 copy.182
  998.8 19.1 %all-gather.7 = f32[8,6,128]{2,1,0:T(8,128)S(1)} all-gather(f32[1,6,128]{2,1,0:T(8,128)S(1)} %convolution_bitcast_fusion.4), channel_id=5, replica_groups=mesh['row'=8,'col'=32] {'row'}, dimensions={0}, use_global_device_ids=true | all-gather | bytes 27648 | tf_op jit(solution)/shard_map/all_gather | solution.py:34
  1019.0 112.8 %all-reduce.16.cloned.1.call-done = f32[32,6,128]{2,0,1:T(8,128)} async-done(((f32[32,6,128]{2,0,1:T(8,128)}), f32[32,6,128]{2,0,1:T(8,128)}) %all-reduce.16.cloned.1.call-update) | async-done | bytes 98320
  1137.4 2.8 collective-permute-start.27
  1140.3 78.2 %psum.47 = f32[128]{0:T(128)S(1)} all-reduce(f32[128]{0:T(128)S(1)} %fusion.6), channel_id=1, replica_groups=mesh['row'=8,'col'=32] {'row','col'}, use_global_device_ids=true, to_apply=%region_15.17 | all-reduce | flops 128 | bytes 1024 | tf_op jit(solution)/shard_map/psum | solution.py:81
  1218.5 2.4 multiply_add_fusion
  1222.2 2.3 fusion.10
  (151 shorter events, 101.9 us)
Async XLA Ops:
  7.2 37.6 %copy-start = (f32[6,1,32,6,8,1]{2,5,4,3,1,0:T(1,128)S(1)}, f32[6,1,32,6,8,1]{2,5,4,3,1,0:T(1,128)}, u32[]{:S(2)}) copy-start(f32[6,1,32,6,8,1]{2,5,4,3,1,0:T(1,128)} %param.12) | copy-start | bytes 110596
  7.2 165.5 %copy-start.1 = (f32[1,1,2,128,512]{4,3,2,1,0:T(8,128)S(1)}, f32[1,1,2,128,512]{4,3,2,1,0:T(8,128)}, u32[]{:S(2)}) copy-start(f32[1,1,2,128,512]{4,3,2,1,0:T(8,128)} %param.13) | copy-start | bytes 1572868
  7.2 160.2 %copy-start.4 = (s32[1,1,16]{2,1,0:T(1,128)S(1)}, s32[1,1,16]{2,1,0:T(1,128)}, u32[]{:S(2)}) copy-start(s32[1,1,16]{2,1,0:T(1,128)} %param.11) | copy-start | bytes 196
  7.2 153.6 %all-reduce.10.cloned.1.call-start = ((), (), s32[]{:S(2)}) async-start(), calls=%async_computation | async-start | bytes 196608
  8.5 10.4 collective-permute-start.1
  13.3 8.8 collective-permute-start
  45.9 335.8 %all-reduce.12.cloned.1.call-start = ((), (), s32[]{:S(2)}) async-start(), calls=%async_computation.1 | async-start | bytes 196608
  163.2 8.8 collective-permute-start.2
  164.5 8.1 collective-permute-start.3
  173.7 19.7 %collective-permute-start.5 = (f32[128,512]{1,0:T(8,128)S(1)}, f32[128,512]{1,0:T(8,128)S(1)}, u32[]{:S(2)}, u32[]{:S(2)}) collective-permute-start(f32[128,512]{1,0:T(8,128)S(1)} %get-tuple-element.61), channel_id=1, source_target_pairs={{0,1},{1,2},{2,3},{3,4},{4,5},{5,6},{6,7},{7,8},{8,9},{9,10},{10,1... | collective-permute-start | bytes 786440 | tf_op jit(solution)/shard_map/ppermute | solution.py:19
  177.9 15.6 %collective-permute-start.4 = (f32[128,512]{1,0:T(8,128)S(1)}, f32[128,512]{1,0:T(8,128)S(1)}, u32[]{:S(2)}, u32[]{:S(2)}) collective-permute-start(f32[128,512]{1,0:T(8,128)S(1)} %get-tuple-element.59), channel_id=1, source_target_pairs={{0,32},{32,64},{64,96},{96,128},{128,160},{160,192},{192,224},{1,3... | collective-permute-start | bytes 786440 | tf_op jit(solution)/shard_map/ppermute | solution.py:19
  221.6 8.2 collective-permute-start.7
  223.7 9.1 collective-permute-start.6
  229.8 6.2 collective-permute-start.9
  232.8 9.3 collective-permute-start.8
  266.9 488.2 %all-reduce.14.cloned.1.call-start = ((), (), s32[]{:S(2)}) async-start(), calls=%async_computation.2 | async-start | bytes 196608
  384.9 82.5 %collective-permute-start.10 = (f32[128,512]{1,0:T(8,128)}, f32[128,512]{1,0:T(8,128)}, u32[]{:S(2)}, u32[]{:S(2)}) collective-permute-start(f32[128,512]{1,0:T(8,128)} %get-tuple-element.43), channel_id=1, source_target_pairs={{32,0},{64,32},{96,64},{128,96},{160,128},{192,160},{224,192},{33,... | collective-permute-start | bytes 786440 | tf_op jit(solution)/shard_map/ppermute | solution.py:19
  386.2 81.2 %collective-permute-start.11 = (f32[128,512]{1,0:T(8,128)}, f32[128,512]{1,0:T(8,128)}, u32[]{:S(2)}, u32[]{:S(2)}) collective-permute-start(f32[128,512]{1,0:T(8,128)} %get-tuple-element.44), channel_id=1, source_target_pairs={{1,0},{2,1},{3,2},{4,3},{5,4},{6,5},{7,6},{8,7},{9,8},{10,9},{11,1... | collective-permute-start | bytes 786440 | tf_op jit(solution)/shard_map/ppermute | solution.py:19
  543.1 6.9 collective-permute-start.13
  546.3 9.5 collective-permute-start.12
  593.1 8.3 collective-permute-start.15
  596.0 10.5 collective-permute-start.14
  602.4 9.0 collective-permute-start.17
  607.6 9.1 collective-permute-start.16
  642.3 489.5 %all-reduce.16.cloned.1.call-start = ((), (), s32[]{:S(2)}) async-start(), calls=%async_computation.3 | async-start | bytes 196608
  757.5 1.0 copy-start.3
  759.3 82.7 %collective-permute-start.18 = (f32[128,512]{1,0:T(8,128)}, f32[128,512]{1,0:T(8,128)}, u32[]{:S(2)}, u32[]{:S(2)}) collective-permute-start(f32[128,512]{1,0:T(8,128)} %get-tuple-element.37), channel_id=1, source_target_pairs={{32,0},{64,32},{96,64},{128,96},{160,128},{192,160},{224,192},{33,... | collective-permute-start | bytes 786440 | tf_op jit(solution)/shard_map/ppermute | solution.py:19
  760.8 81.2 %collective-permute-start.19 = (f32[128,512]{1,0:T(8,128)}, f32[128,512]{1,0:T(8,128)}, u32[]{:S(2)}, u32[]{:S(2)}) collective-permute-start(f32[128,512]{1,0:T(8,128)} %get-tuple-element.38), channel_id=1, source_target_pairs={{1,0},{2,1},{3,2},{4,3},{5,4},{6,5},{7,6},{8,7},{9,8},{10,9},{11,1... | collective-permute-start | bytes 786440 | tf_op jit(solution)/shard_map/ppermute | solution.py:19
  919.6 6.9 collective-permute-start.21
  922.8 9.5 collective-permute-start.20
  969.8 8.3 collective-permute-start.23
  972.7 10.5 collective-permute-start.22
  979.1 9.0 collective-permute-start.25
  984.3 9.1 collective-permute-start.24
  1134.2 1.0 copy-start.2
  1136.1 84.8 %collective-permute-start.26 = (f32[128,512]{1,0:T(8,128)}, f32[128,512]{1,0:T(8,128)}, u32[]{:S(2)}, u32[]{:S(2)}) collective-permute-start(f32[128,512]{1,0:T(8,128)} %get-tuple-element.25), channel_id=1, source_target_pairs={{32,0},{64,32},{96,64},{128,96},{160,128},{192,160},{224,192},{33,... | collective-permute-start | bytes 786440 | tf_op jit(solution)/shard_map/ppermute | solution.py:19
  1137.4 83.5 %collective-permute-start.27 = (f32[128,512]{1,0:T(8,128)}, f32[128,512]{1,0:T(8,128)}, u32[]{:S(2)}, u32[]{:S(2)}) collective-permute-start(f32[128,512]{1,0:T(8,128)} %get-tuple-element.26), channel_id=1, source_target_pairs={{1,0},{2,1},{3,2},{4,3},{5,4},{6,5},{7,6},{8,7},{9,8},{10,9},{11,1... | collective-permute-start | bytes 786440 | tf_op jit(solution)/shard_map/ppermute | solution.py:19
Sparse Core Ops, SparseCore 0:
  46.0 114.7 all-reduce.9
  267.1 114.5 all-reduce.11
  642.4 112.6 all-reduce.13
  1019.1 112.6 all-reduce.15
where the time goes:
time: 1240 us; the launch traced here: 1230 us
  waiting for transfers between devices  504 us (41%)
  blocking collectives  462 us (37%)
  local copies, waits for them, and re-layouts  90.9 us (7%)
  starting transfers between devices  72.6 us (6%)
  matrix products  49.9 us (4%)
  other arithmetic  37.2 us (3%)
  between operations  15.5 us (1%)
    unnamed x8, waiting for transfers between devices  453 us
    psum x3, blocking collectives, per_device(): lax.psum(jnp.sum(residual * residual, axis=(0, 2)), ('row', 'col'))  225 us
    psum x2, blocking collectives, per_device(): lax.psum(jnp.sum(direction * schur_image, axis=(0, 2)), ('row', 'col'))  156 us
    all_gather x4, blocking collectives, coarse_solve(): gathered = lax.all_gather(coarse_rhs[None], 'row', axis=0, tiled=True)  80.7 us
    ppermute x28, starting transfers between devices, shifted(): lax.ppermute(value, axis, [(source, source + steps) for source in range(i...  72.2 us
    ppermute x28, waiting for transfers between devices, shifted(): lax.ppermute(value, axis, [(source, source + steps) for source in range(i...  50.7 us
    dot_general x3, matrix products, per_device(): jnp.dot(permuted, matrix, precision=highest, preferred_element_type=jnp.f...  35.4 us
  transfers between devices with their start and end apart: 32, of which 18 were waited for; matrix products, arithmetic and copies ran while one was open for 2% of the time, Pallas kernels for 0%

commit v1 on v0

v1 whole, which is shorter than its diff:
```python
import functools

import jax
import jax.numpy as jnp
from jax import lax
from jax.experimental import pallas as pl
from jax.experimental.pallas import tpu as pltpu
from jax.sharding import PartitionSpec as P

M = 512
NS = 2048
BLK = 128
NB = 16
K = 128
ROWS = 8
COLS = 32
MODES = 6
ITERS = 3
SLOT = 8
SLOTS = 5
PAY = 48
TERMS = ((0, 0), (0, 1), (1, 0), (1, 1), (0, 2), (2, 0))
TALL = 1024
CHIPS = 16

f32 = jnp.float32
bf16 = jnp.bfloat16
VM = pl.BlockSpec(memory_space=pltpu.VMEM)
SM = pl.BlockSpec(memory_space=pltpu.SMEM)
HB = pl.BlockSpec(memory_space=pltpu.HBM)
LIMIT = pltpu.CompilerParams(vmem_limit_bytes=56 * 1024 * 1024)
SMALL = pltpu.CompilerParams(vmem_limit_bytes=8 * 1024 * 1024)


def cyclic(value, axis, steps):
    count = lax.axis_size(axis)
    return lax.ppermute(value, axis, [(s, (s + steps) % count) for s in range(count)])


def shifted(value, axis, steps):
    count = lax.axis_size(axis)
    initial, last = (max(0, -steps), min(count, count - steps))
    return lax.ppermute(value, axis, [(s, s + steps) for s in range(initial, last)])


def swapped(value, partner):
    return lax.ppermute(value, "col", [(s, partner(s)) for s in range(COLS)])


def parts_of(value, count):
    pieces = []
    for _ in range(count):
        piece = value.astype(bf16)
        pieces.append(piece)
        value = value - piece.astype(f32)
    return pieces


class Copies:
    def __init__(self, sems):
        self.sems, self.used, self.open = sems, 0, []

    def start(self, source, target):
        copy = pltpu.make_async_copy(source, target, self.sems.at[self.used])
        copy.start()
        self.used += 1
        return copy

    def out(self, source, target):
        self.open.append(self.start(source, target))

    def close(self):
        for copy in self.open:
            copy.wait()


def wait(copies):
    for copy in copies:
        copy.wait()


def own_modes(full, own, masks):
    for block in range(NB):
        face = block // (M // BLK)
        value = own[block] * masks[face] if face % 2 == 0 else own[block]
        full[0:SLOT, BLK * block : BLK * (block + 1)] = value


def start_kernel(
    masks, own, side, from_n, from_w, local, pay,
    own_v, side_v, near_v, local_v, full, halves, pay_v, sems,
):
    copies = Copies(sems)
    ready = [copies.start(own, own_v), copies.start(side.at[0], side_v.at[0]), copies.start(side.at[1], side_v.at[1])]
    near = [copies.start(from_n, near_v.at[0]), copies.start(from_w, near_v.at[1])]
    full[...] = jnp.zeros_like(full)
    wait(ready)
    own_modes(full, own_v, masks)
    for pair in range(2):
        wait(near[pair : pair + 1])
        for kind in range(2):
            face = 2 * pair + kind
            for block in range(M // BLK):
                inside = slice(BLK * block, BLK * (block + 1))
                rows = slice(M * face + BLK * block, M * face + BLK * (block + 1))
                if kind:
                    turned = side_v[pair, :, inside].T
                else:
                    turned = near_v[pair, :, inside].T * -masks[face]
                local_v[rows, :] = turned
                high, low = parts_of(turned, 2)
                halves[rows, :K] = high
                halves[rows, K:] = low
        wide = pl.ds(2 * M * pair, 2 * M)
        copies.out(local_v.at[wide], local.at[wide])
    pieces = jnp.concatenate(parts_of(full[...], 2), axis=0)
    d = jnp.dot(pieces, halves[...], preferred_element_type=f32)
    value = d[0:16, :K] + d[0:16, K:] + d[16:32, :K] + d[16:32, K:]
    pay_v[...] = jnp.zeros_like(pay_v)
    pay_v[0:SLOT, :] = value[0:SLOT]
    for index in range(ROWS):
        copies.out(pay_v, pay.at[index])
    copies.close()


def setup_kernel(
    order, masks, core, own, mine, down, up, right, left, far, bgt, bgc, parts,
    own_v, mine_v, down_v, up_v, right_v, left_v, far_v, full, turned, table, bgt_v, bgc_v, parts_v, sems,
):
    copies = Copies(sems)
    pairs = ((own, own_v), (mine, mine_v), (down, down_v), (up, up_v), (right, right_v), (left, left_v), (far, far_v))
    ready = [copies.start(source, target) for source, target in pairs]
    full[...] = jnp.zeros_like(full)
    wait(ready)
    own_modes(full, own_v, masks)
    for slot, (near, at) in enumerate(((down_v, COLS), (up_v, COLS), (right_v, 3 * COLS), (left_v, 3 * COLS))):
        rows = slice(SLOT * (slot + 1), SLOT * (slot + 2))
        for block in range(M // BLK):
            lanes = slice(M * slot + BLK * block, M * slot + BLK * (block + 1))
            full[rows, lanes] = near[at + block] * -masks[slot]
    pieces = parts_of(full[...], 3)
    for index, (which, _) in enumerate(TERMS):
        turned[40 * index : 40 * (index + 1), :] = pieces[which][0:40].astype(f32)
    turned[240:256, :] = jnp.zeros((16, NS), f32)
    for block in range(NB):
        for half in range(2):
            piece = turned[BLK * half : BLK * (half + 1), BLK * block : BLK * (block + 1)].T
            bgc_v[BLK * block : BLK * (block + 1), BLK * half : BLK * (half + 1)] = piece.astype(bf16)
    copies.out(bgc_v, bgc)
    for block in range(NB):
        at = pl.multiple_of(order[block] * BLK, BLK)
        for index, piece in enumerate(parts_of(full[:, pl.ds(at, BLK)], 2)):
            bgt_v[PAY * index : PAY * (index + 1), BLK * block : BLK * (block + 1)] = piece
    copies.out(bgt_v, bgt)

    first = core[0] == 0
    half = lax.broadcasted_iota(jnp.int32, (SLOT, BLK), 1) < SLOT * ROWS

    @pl.loop(0, CHIPS)
    def _(target):
        at = 2 * target + core[0]
        picks = ((0, at), (1, at), (2, at), (0, jnp.maximum(at - 1, 0)), (0, jnp.minimum(at + 1, COLS - 1)))
        for slot, (line, column) in enumerate(picks):
            w, e, f = (ref[COLS * line + column] for ref in (right_v, left_v, far_v))
            m = (mine_v[column], down_v[column], up_v[column])[line]
            inner = jnp.where(half, jnp.where(first, w, f), jnp.where(first, m, w))
            outer = jnp.where(half, jnp.where(first, e, m), jnp.where(first, f, e))
            rows = pl.ds(pl.multiple_of((target * SLOTS + slot) * SLOT, SLOT), SLOT)
            table[rows, :K] = inner
            table[rows, K:] = outer

    for index, piece in enumerate(parts_of(table[...], 2)):
        parts_v[index] = piece
        copies.out(parts_v.at[index], parts.at[index])
    copies.close()


def coarse_kernel(core, parts, own_v, other_v, out, parts_v, entries, out_v, sems):
    copies = Copies(sems)
    table = [copies.start(parts.at[index], parts_v.at[index]) for index in range(2)]
    first = core[0] == 0

    def tile(which, line, slot):
        here = slice(SLOT * slot, SLOT * (slot + 1))
        a, b = own_v[line, here, :], other_v[line, here, :]
        return jnp.where(first, a, b) if which == 0 else jnp.where(first, b, a)

    total = jnp.zeros((SLOT, K), f32)
    for line in range(ROWS):
        for which in range(2):
            value = tile(which, line, 0)
            if line > 0:
                value = value + tile(which, line - 1, 2)
            if line < ROWS - 1:
                value = value + tile(which, line + 1, 1)
            value = value + tile(1 - which, line, 3 + which)
            at = SLOT * (ROWS * (which + 1) + line)
            entries[at : at + SLOT, :] = value
        entries[SLOT * line : SLOT * (line + 1), :] = tile(0, line, 3)
        at = SLOT * (ROWS * 3 + line)
        entries[at : at + SLOT, :] = tile(1, line, 4)
        total = total + own_v[line, SLOT * SLOTS :, :] + other_v[line, SLOT * SLOTS :, :]
    both = jnp.concatenate(parts_of(entries[...], 2), axis=1)
    wait(table)
    d = jnp.dot(parts_v[0], both, preferred_element_type=f32)
    e = jnp.dot(parts_v[1], both, preferred_element_type=f32)
    value = e[:, K:] + e[:, :K] + d[:, K:] + d[:, :K]
    for target in range(CHIPS):
        out_v[target] = value[SLOTS * SLOT * target : SLOTS * SLOT * (target + 1)]
        out_v[target, 6:8, :] = total[0:2]
        out_v[target, 14:15, :] = total[2:3]
    copies.out(out_v, out)
    copies.close()


def take_values(came, stack):
    value = came[0]
    for index in range(1, CHIPS):
        value = value + came[index]
    spare = lax.broadcasted_iota(jnp.int32, (SLOT * SLOTS, K), 0) % SLOT >= MODES
    pieces = parts_of(jnp.where(spare, 0.0, value), 3)
    for index, (_, right) in enumerate(TERMS):
        stack[40 * index : 40 * (index + 1), :] = pieces[right].astype(f32)
    stack[240:256, :] = jnp.zeros((16, K), f32)
    return stack[...].astype(bf16), (value[6:7], value[7:8], value[14:15])


def folded(value):
    return jnp.sum(value.reshape(-1, SLOT, K), axis=0)


def schur_product(order, copies, matrix, turn, bgt, residual, halves, product):
    wait(turn)

    def tall(step, carry):
        value, energy = carry
        matrix.wait(step)
        rows = matrix.held[pl.ds(pl.multiple_of(step * TALL, TALL), TALL), :]
        both = jnp.dot(rows, halves[...], preferred_element_type=f32)
        both = both[:, :K] + both[:, K:]
        d = jnp.dot(
            bgt[:, pl.ds(pl.multiple_of(step * TALL, TALL), TALL)],
            jnp.concatenate(parts_of(both, 2), axis=1),
            preferred_element_type=f32,
        )
        value = value + d[:PAY, :K] + d[:PAY, K:] + d[PAY:, :K] + d[PAY:, K:]
        for piece in range(TALL // BLK):
            at = pl.multiple_of(order[step * (TALL // BLK) + piece] * BLK, BLK)
            y = both[BLK * piece : BLK * (piece + 1)]
            product[pl.ds(at, BLK), :] = y
            energy = energy + folded(residual[pl.ds(at, BLK), :] * y)
        return value, energy

    return lax.fori_loop(0, NS // TALL, tall, (jnp.zeros((PAY, K), f32), jnp.zeros((SLOT, K), f32)))


class Matrix:
    def __init__(self, source, held, sems):
        self.source, self.held, self.sems = source, held, sems

    def copy(self, step):
        rows = pl.ds(TALL * step if isinstance(step, int) else pl.multiple_of(step * TALL, TALL), TALL)
        return pltpu.make_async_copy(self.source.at[rows], self.held.at[rows], self.sems.at[step])

    def start(self, step):
        self.copy(step).start()

    def wait(self, step):
        self.copy(step).wait()


def put_halves(value, halves, at):
    high, low = parts_of(value, 2)
    halves[pl.ds(pl.multiple_of(at * BLK, BLK), BLK), :K] = high
    halves[pl.ds(pl.multiple_of(at * BLK, BLK), BLK), K:] = low


def invert(order, inverse):
    for block in range(NB):
        inverse[order[block]] = block


def close_product(value, norm, energy, cross, product, pay, faces, copies, pay_held):
    for face in range(4):
        copies.out(product.at[pl.ds(M * face, M)], faces[face])
    pay_held[0:PAY, :] = value
    pay_held[40:41, :] = jnp.sum(norm, axis=0, keepdims=True)
    pay_held[41:42, :] = jnp.sum(energy, axis=0, keepdims=True)
    pay_held[42:43, :] = jnp.sum(cross, axis=0, keepdims=True)
    for index in range(ROWS):
        copies.out(pay_held, pay.at[index])
    copies.close()


def begin_kernel(
    order, matrix, bgt, bgc, came, local, residual, yn, ys, yw, ye, pay,
    inverse, held, bgt_v, bgc_v, came_v, r_v, halves, product, spread, stack, pay_v, sems, tall_sems,
):
    copies, matrix = Copies(sems), Matrix(matrix, held, tall_sems)
    head = [copies.start(came, came_v), copies.start(bgc, bgc_v)]
    body = [copies.start(local.at[pl.ds(M * face, M)], r_v.at[pl.ds(M * face, M)]) for face in range(4)]
    matrix.start(0)
    turn = [copies.start(bgt, bgt_v)]
    invert(order, inverse)
    wait(head)
    matrix.start(1)
    stacked, _ = take_values(came_v, stack)
    norm = jnp.zeros((SLOT, K), f32)
    for face in range(4):
        inner = slice(M * face, M * (face + 1))
        spread[0:M, :] = jnp.dot(bgc_v[inner, :], stacked, preferred_element_type=f32)
        wait(body[face : face + 1])

        def block(index, norm, face=face):
            rows = pl.ds(pl.multiple_of(M * face + BLK * index, BLK), BLK)
            r = r_v[rows, :] - spread[pl.ds(pl.multiple_of(BLK * index, BLK), BLK), :]
            r_v[rows, :] = r
            put_halves(r, halves, inverse[M // BLK * face + index])
            return norm + folded(r * r) if face % 2 else norm

        norm = lax.fori_loop(0, M // BLK, block, norm)
        copies.out(r_v.at[inner], residual.at[inner])
    value, energy = schur_product(order, copies, matrix, turn, bgt_v, r_v, halves, product)
    close_product(value, norm, energy, jnp.zeros_like(norm), product, pay, (yn, ys, yw, ye), copies, pay_v)


def scalars(first, sums, past):
    norm, energy, cross = sums
    if first:
        return norm, energy, None, norm / energy
    ratio = norm / past[0:1, :]
    curvature = energy + 2.0 * ratio * cross + ratio * ratio * past[1:2, :]
    return norm, curvature, ratio, norm / curvature


def step_kernel(first, *refs):
    order, masks, matrix, bgt, bgc, came, residual = refs[:7]
    near, faces = refs[7:11], refs[11:15]
    refs = refs[15:]
    if not first:
        past, along, moved, image, done = refs[:5]
        refs = refs[5:]
    new_residual, new_along, new_moved, new_image, new_done, new_past = refs[:6]
    new_faces, pay, refs = refs[6:10], refs[10], refs[11:]
    (inverse, held, bgt_v, bgc_v, came_v, r_v, halves, product, spread, stack, pay_v, sems, tall_sems,
     y_v, near_v, moved_v, image_v, along_v, done_v, past_v, new_past_v) = refs

    copies, matrix = Copies(sems), Matrix(matrix, held, tall_sems)
    head = [copies.start(came, came_v)]
    if not first:
        head.append(copies.start(past, past_v))
    head.append(copies.start(bgc, bgc_v))
    def fetch(pair):
        wide, own = pl.ds(2 * M * pair, 2 * M), pl.ds(M * pair, M)
        part = [copies.start(residual.at[wide], r_v.at[wide])]
        for face in (2 * pair, 2 * pair + 1):
            rows = pl.ds(M * face, M)
            part += [copies.start(faces[face], y_v.at[rows]), copies.start(near[face], near_v.at[rows])]
        if not first:
            part.append(copies.start(moved.at[wide], moved_v.at[wide]))
            for source, target in ((image, image_v), (along, along_v), (done, done_v)):
                part.append(copies.start(source.at[own], target.at[own]))
        return part

    body = [fetch(0)]
    matrix.start(0)
    invert(order, inverse)

    wait(head)
    stacked, sums = take_values(came_v, stack)
    norm, curvature, ratio, step = scalars(first, sums, past_v)
    new_past_v[...] = jnp.zeros_like(new_past_v)
    new_past_v[0:1, :] = norm
    new_past_v[1:2, :] = curvature
    copies.out(new_past_v, new_past)
    carry = (jnp.zeros((SLOT, K), f32), jnp.zeros((SLOT, K), f32))
    for pair in range(2):
        wide, own = pl.ds(2 * M * pair, 2 * M), pl.ds(M * pair, M)
        spread[...] = jnp.dot(bgc_v[2 * M * pair : 2 * M * (pair + 1), :], stacked, preferred_element_type=f32)
        wait(body[pair])
        if pair == 0:
            body.append(fetch(1))
            turn = [copies.start(bgt, bgt_v)]

        def block(index, carry, pair=pair):
            norm, cross = carry
            for kind in range(2):
                face = 2 * pair + kind
                rows = pl.ds(pl.multiple_of(M * face + BLK * index, BLK), BLK)
                mine = pl.ds(pl.multiple_of(M * pair + BLK * index, BLK), BLK)
                if kind:
                    q = y_v[rows, :] - masks[face] * near_v[rows, :]
                    f = q if first else q + ratio * image_v[mine, :]
                    image_v[mine, :] = f
                else:
                    q = masks[face] * (y_v[rows, :] - near_v[rows, :])
                q = q - spread[pl.ds(pl.multiple_of(M * kind + BLK * index, BLK), BLK), :]
                if not first:
                    q = q + ratio * moved_v[rows, :]
                moved_v[rows, :] = q
                r = r_v[rows, :]
                if kind:
                    if first:
                        along_v[mine, :] = r
                        done_v[mine, :] = step * r
                    else:
                        d = r + ratio * along_v[mine, :]
                        along_v[mine, :] = d
                        done_v[mine, :] = done_v[mine, :] + step * d
                r = r - step * q
                r_v[rows, :] = r
                put_halves(r, halves, inverse[M // BLK * face + index])
                if kind:
                    norm = norm + folded(r * r)
                    cross = cross + folded(r * f)
            return norm, cross

        carry = lax.fori_loop(0, M // BLK, block, carry)
        if pair == 0:
            matrix.start(1)
        for source, target in ((r_v, new_residual), (moved_v, new_moved)):
            copies.out(source.at[wide], target.at[wide])
        for source, target in ((image_v, new_image), (along_v, new_along), (done_v, new_done)):
            copies.out(source.at[own], target.at[own])
    value, energy = schur_product(order, copies, matrix, turn, bgt_v, r_v, halves, product)
    close_product(value, carry[0], energy, carry[1], product, pay, new_faces, copies, pay_v)


def end_kernel(
    masks, bgc, came, residual, ns, ne, ys, ye, past, along, moved, done, out_done, out_residual,
    stack, bgc_v, came_v, past_v, r_v, near_v, y_v, along_v, moved_v, done_v, x_v, s_v, sems,
):
    copies = Copies(sems)
    head = [copies.start(came, came_v), copies.start(past, past_v)]
    body = []
    for pair, near, mine in ((0, ns, ys), (1, ne, ye)):
        rows, own = pl.ds(M * (2 * pair + 1), M), pl.ds(M * pair, M)
        part = [copies.start(bgc.at[rows], bgc_v.at[own]), copies.start(near, near_v.at[own])]
        part += [copies.start(mine, y_v.at[own]), copies.start(residual.at[rows], r_v.at[own])]
        part += [copies.start(moved.at[rows], moved_v.at[own]), copies.start(along.at[own], along_v.at[own])]
        body.append(part + [copies.start(done.at[own], done_v.at[own])])
    wait(head)
    stacked, sums = take_values(came_v, stack)
    _, _, ratio, step = scalars(False, sums, past_v)
    for pair in range(2):
        wait(body[pair])
        for block in range(M // BLK):
            inside = slice(BLK * block, BLK * (block + 1))
            own = slice(M * pair + BLK * block, M * pair + BLK * (block + 1))
            q = y_v[own, :] - masks[2 * pair + 1] * near_v[own, :]
            q = q - jnp.dot(bgc_v[own, :], stacked, preferred_element_type=f32)
            q = q + ratio * moved_v[own, :]
            r = r_v[own, :]
            d = r + ratio * along_v[own, :]
            s_v[pair, :, inside] = (r - step * q).T
            x_v[pair, :, inside] = (done_v[own, :] + step * d).T
        copies.out(s_v.at[pair], out_residual.at[pair])
        copies.out(x_v.at[pair], out_done.at[pair])
    copies.close()


def shape(*dims, kind=f32):
    return jax.ShapeDtypeStruct(dims, kind)


WORK = [
    pltpu.SMEM((NB,), jnp.int32),
    pltpu.VMEM((NS, NS), bf16),
    pltpu.VMEM((2 * PAY, NS), bf16),
    pltpu.VMEM((NS, 2 * K), bf16),
    pltpu.VMEM((CHIPS, SLOTS * SLOT, K), f32),
    pltpu.VMEM((NS, K), f32),
    pltpu.VMEM((NS, 2 * K), bf16),
    pltpu.VMEM((NS, K), f32),
    pltpu.VMEM((2 * M, K), f32),
    pltpu.VMEM((256, K), f32),
    pltpu.VMEM((PAY, K), f32),
    pltpu.SemaphoreType.DMA((64,)),
    pltpu.SemaphoreType.DMA((NS // TALL,)),
]
MORE = [pltpu.VMEM((NS, K), f32)] * 3 + [pltpu.VMEM((2 * M, K), f32)] * 3 + [pltpu.VMEM((SLOT, K), f32)] * 2
LAST = (
    [pltpu.VMEM((256, K), f32), pltpu.VMEM((2 * M, 2 * K), bf16), pltpu.VMEM((CHIPS, SLOTS * SLOT, K), f32)]
    + [pltpu.VMEM((SLOT, K), f32)]
    + [pltpu.VMEM((2 * M, K), f32)] * 6
    + [pltpu.VMEM((2, K, M), f32)] * 2
    + [pltpu.SemaphoreType.DMA((32,))]
)
FACES = [shape(M, K)] * 4


def call(kernel, specs, outs, scratch, flops, place, limit=LIMIT):
    return pl.pallas_call(
        kernel,
        in_specs=specs,
        out_specs=[place] * len(outs),
        out_shape=outs,
        scratch_shapes=scratch,
        compiler_params=limit,
        cost_estimate=pl.CostEstimate(flops=flops, bytes_accessed=1 << 20, transcendentals=0),
    )


def coarse_phase(pay, parts, core):
    own = lax.all_to_all(pay, "row", 0, 0, tiled=True)
    other = swapped(own, lambda c: c ^ 1)
    (terms,) = call(
        coarse_kernel,
        [SM, HB, VM, VM],
        [shape(CHIPS, SLOTS * SLOT, K)],
        [
            pltpu.VMEM((2, CHIPS * SLOTS * SLOT, 2 * K), bf16),
            pltpu.VMEM((2 * K, K), f32),
            pltpu.VMEM((CHIPS, SLOTS * SLOT, K), f32),
            pltpu.SemaphoreType.DMA((8,)),
        ],
        10**8,
        HB,
        SMALL,
    )(core, parts, own, other)
    groups = [[2 * chip + which for chip in range(CHIPS)] for which in range(2)]
    return lax.all_to_all(terms, "col", 0, 0, axis_index_groups=groups, tiled=True)


def per_device(schur_blocks, rigid_modes, floating, block_order, coarse_inverse, right_side):
    order = block_order[0, 0]
    row, col = lax.axis_index("row"), lax.axis_index("col")
    core = (col % 2).astype(jnp.int32).reshape(1)
    masks = jnp.stack([row > 0, row < ROWS - 1, col > 0, col < COLS - 1]).astype(f32)
    side = right_side[0, 0]

    from_n = cyclic(side[0], "row", 1)
    from_w = cyclic(side[1], "col", 1)
    modes = (rigid_modes[0, 0] * floating[0, 0].astype(f32)).reshape(MODES, NB, BLK)
    modes = jnp.pad(jnp.transpose(modes, (1, 0, 2)), ((0, 0), (0, SLOT - MODES), (0, 0)))
    local, pay = call(
        start_kernel,
        [SM] + [HB] * 4,
        [shape(NS, K), shape(ROWS, PAY, K)],
        [
            pltpu.VMEM((NB, SLOT, BLK), f32),
            pltpu.VMEM((2, K, M), f32),
            pltpu.VMEM((2, K, M), f32),
            pltpu.VMEM((NS, K), f32),
            pltpu.VMEM((16, NS), f32),
            pltpu.VMEM((NS, 2 * K), bf16),
            pltpu.VMEM((PAY, K), f32),
            pltpu.SemaphoreType.DMA((16,)),
        ],
        10**8,
        HB,
    )(masks, modes, side, from_n, from_w)

    mine = jnp.transpose(coarse_inverse[:, 0, :, :, :, 0], (1, 0, 3, 2))
    mine = jnp.pad(mine, ((0, 0), (0, SLOT - MODES), (0, 0), (0, SLOT - MODES))).reshape(COLS, SLOT, SLOT * ROWS)
    mine = jnp.concatenate([mine, mine], axis=2)
    down = cyclic(jnp.concatenate([mine, modes[4:8]], axis=0), "row", 1)
    up = cyclic(jnp.concatenate([mine, modes[0:4]], axis=0), "row", -1)
    down, up, pay = lax.optimization_barrier((down, up, pay))
    lines = jnp.concatenate([mine, down[:COLS], up[:COLS]], axis=0)
    right = cyclic(jnp.concatenate([lines, modes[12:16]], axis=0), "col", 1)
    left = cyclic(jnp.concatenate([lines, modes[8:12]], axis=0), "col", -1)
    far = swapped(jnp.where(core[0] == 0, right[: 3 * COLS], left[: 3 * COLS]), lambda c: c ^ 1)
    bgt, bgc, parts = call(
        setup_kernel,
        [SM] * 3 + [HB] * 7,
        [shape(2 * PAY, NS, kind=bf16), shape(NS, 2 * K, kind=bf16), shape(2, CHIPS * SLOTS * SLOT, 2 * K, kind=bf16)],
        [pltpu.VMEM((tiles, SLOT, BLK), f32) for tiles in (NB, COLS, COLS + 4, COLS + 4, 3 * COLS + 4, 3 * COLS + 4, 3 * COLS)]
        + [
            pltpu.VMEM((PAY, NS), f32),
            pltpu.VMEM((256, NS), f32),
            pltpu.VMEM((CHIPS * SLOTS * SLOT, 2 * K), f32),
            pltpu.VMEM((2 * PAY, NS), bf16),
            pltpu.VMEM((NS, 2 * K), bf16),
            pltpu.VMEM((2, CHIPS * SLOTS * SLOT, 2 * K), bf16),
            pltpu.SemaphoreType.DMA((16,)),
        ],
        10**8,
        HB,
    )(order, masks, core, modes, mine, down, up, right, left, far)
    came = coarse_phase(pay, parts, core)

    matrix = schur_blocks[0, 0]
    residual, *faces, pay = call(
        begin_kernel,
        [SM] + [HB] * 5,
        [shape(NS, K)] + FACES + [shape(ROWS, PAY, K)],
        WORK,
        2 * 10**9,
        HB,
    )(order, matrix, bgt, bgc, came, local)

    state = ()
    for iteration in range(ITERS):
        north, south = cyclic(faces[1], "row", 1), cyclic(faces[0], "row", -1)
        west, east = cyclic(faces[3], "col", 1), cyclic(faces[2], "col", -1)
        near = (north, south, west, east)
        came = coarse_phase(pay, parts, core)
        if iteration + 1 == ITERS:
            break
        first = iteration == 0
        given = (order, masks, matrix, bgt, bgc, came, residual, *near, *faces, *state)
        residual, along, moved, image, done, past, *faces, pay = call(
            functools.partial(step_kernel, first),
            [SM, SM] + [HB] * (len(given) - 2),
            [shape(NS, K), shape(2 * M, K), shape(NS, K), shape(2 * M, K), shape(2 * M, K), shape(SLOT, K)]
            + FACES
            + [shape(ROWS, PAY, K)],
            WORK + MORE,
            2 * 10**9,
            HB,
        )(*given)
        state = (past, along, moved, image, done)

    past, along, moved, image, done = state
    done, residual = call(
        end_kernel,
        [SM] + [HB] * 11,
        [shape(2, K, M)] * 2,
        LAST,
        10**8,
        HB,
    )(masks, bgc, came, residual, near[1], near[3], faces[1], faces[3], past, along, moved, done)
    return (done[None, None], residual[None, None])


def solution(mesh):
    placed = (
        P("row", "col", None, None),
        P("row", "col", None, None),
        P("row", "col"),
        P("row", "col", None),
        P(None, "row", None, None, None, "col"),
        P("row", "col", None, None, None),
    )
    return jax.shard_map(
        per_device,
        mesh=mesh,
        in_specs=placed,
        out_specs=(P("row", "col", None, None, None), P("row", "col", None, None, None)),
        check_vma=False,
    )
```

time: 1240 us -> 198 us (0.16)
  waiting for transfers between devices: 504 us -> 27 us
  blocking collectives: 462 us -> 49.7 us
  local copies, waits for them, and re-layouts: 90.9 us -> 7.85 us
  matrix products: 49.9 us -> 0 us
  Pallas kernels: 0 us -> 44.9 us
  other arithmetic: 37.2 us -> 2.43 us
  between operations: 15.5 us -> 1.76 us
    unnamed x8 -> x0, waiting for transfers between devices: 453 us -> none
    psum x5 -> x0, blocking collectives: 381 us -> none  [the longest x3 225 us: per_device(): lax.psum(jnp.sum(residual * residual, axis=(0, 2)), ('row', 'col'))]
    all_gather x4 -> x0, blocking collectives: 80.7 us -> none  [coarse_solve(): gathered = lax.all_gather(coarse_rhs[None], 'row', axis=0, tiled=True)]
    dot_general x15 -> x0, matrix products: 49.9 us -> none  [the longest x3 35.4 us: per_device(): jnp.dot(permuted, matrix, precision=highest, preferred_element_type=jnp.f...]
    all_to_all x0 -> x4, blocking collectives: none -> 49.7 us  [the longest x3 36 us: coarse_phase(): own = lax.all_to_all(pay, 'row', 0, 0, tiled=True)]
    pallas_call x0 -> x10, Pallas kernels: none -> 44.9 us  [the longest x2 20.2 us: per_device(): call(functools.partial(step_kernel, first), [SM, SM] + [HB] * (len(given)...]
    ppermute x28 -> x21, starting transfers between devices: 72.2 us -> 41.9 us  [the longest x16 21.5 us: cyclic(): lax.ppermute(value, axis, [(s, (s + steps) % count) for s in range(count)])]
    ppermute x28 -> x21, waiting for transfers between devices: 50.7 us -> 26.4 us  [the longest x16 23.1 us: cyclic(): lax.ppermute(value, axis, [(s, (s + steps) % count) for s in range(count)])]
  transfers between devices with their start and end apart: 32 -> 25, of which waited for: 18 -> 14; matrix products, arithmetic and copies ran while one was open for 2% -> 2% of each run, Pallas kernels for 0% -> 4%
where the time goes in v1:
time: 198 us; the launch traced here: 197 us
  starting transfers between devices  63.3 us (32%)
  blocking collectives  49.7 us (25%)
  Pallas kernels  44.9 us (23%)
  waiting for transfers between devices  27 us (14%)
  local copies, waits for them, and re-layouts  7.85 us (4%)
  other arithmetic  2.43 us (1%)
    all_to_all x3, blocking collectives, coarse_phase(): own = lax.all_to_all(pay, 'row', 0, 0, tiled=True)  36 us
    ppermute x16, waiting for transfers between devices, cyclic(): lax.ppermute(value, axis, [(s, (s + steps) % count) for s in range(count)])  23.1 us
    ppermute x16, starting transfers between devices, cyclic(): lax.ppermute(value, axis, [(s, (s + steps) % count) for s in range(count)])  21.5 us
    ppermute x5, starting transfers between devices, swapped(): return lax.ppermute(value, 'col', [(s, partner(s)) for s in range(COLS)])  20.3 us
    pallas_call x2, Pallas kernels, per_device(): call(functools.partial(step_kernel, first), [SM, SM] + [HB] * (len(given)...  20.2 us
    all_to_all x3, starting transfers between devices, coarse_phase(): lax.all_to_all(terms, 'col', 0, 0, axis_index_groups=groups, tiled=True)  15.9 us
    all_to_all x1, blocking collectives, coarse_phase(): lax.all_to_all(terms, 'col', 0, 0, axis_index_groups=groups, tiled=True)  13.8 us
    pallas_call x1, Pallas kernels, per_device(): call(begin_kernel, [SM] + [HB] * 5, [shape(NS, K)] + FACES + [shape(ROWS,...  8.41 us
  transfers between devices with their start and end apart: 25, of which 14 were waited for; matrix products, arithmetic and copies ran while one was open for 2% of the time, Pallas kernels for 4%

profile of v1, /device:TPU:1, one launch (start us, length us, event | category | flops | bytes accessed | tf_op | source)
XLA Modules:
  0.0 196.9 jit_solution(9686345478608217600)
XLA Ops:
  0.6 1.1 slice_bitcast_fusion
  1.7 2.8 %collective-permute-start.3 = (f32[128,512]{1,0:T(8,128)S(1)}, f32[128,512]{1,0:T(8,128)S(1)}, u32[]{:S(2)}, u32[]{:S(2)}) collective-permute-start(f32[128,512]{1,0:T(8,128)S(1)} %get-tuple-element.76), channel_id=1, source_target_pairs={{0,1},{1,2},{2,3},{3,4},{4,5},{5,6},{6,7},{7,8},{8,9},{9,10},{10,1... | collective-permute-start | bytes 786440 | tf_op jit(solution)/shard_map/ppermute | solution.py:37
  4.5 1.6 collective-permute-start.2
  6.8 0.8 broadcast_multiply_fusion
  7.6 1.0 copy.13
  8.6 0.1 copy.11
  8.9 4.0 %collective-permute-start.1 = (f32[36,8,128]{2,1,0:T(8,128)S(1)}, f32[36,8,128]{2,1,0:T(8,128)S(1)}, u32[]{:S(2)}, u32[]{:S(2)}) collective-permute-start(f32[36,8,128]{2,1,0:T(8,128)S(1)} %get-tuple-element.80), channel_id=1, source_target_pairs={{0,224},{32,0},{64,32},{96,64},{128,96},{160,128},{192,160},{224,1... | collective-permute-start | bytes 442376 | tf_op jit(solution)/shard_map/ppermute | solution.py:37
  12.9 0.6 pad.8.own
  13.5 0.6 add_convert_fusion.masks.refs_1_
  14.1 1.6 collective-permute-done.2.from_n
  15.7 0.7 copy-done.17
  16.4 3.3 %shard_map.77 = (f32[2048,128]{1,0:T(8,128)}, f32[8,48,128]{2,1,0:T(8,128)}) custom-call(f32[4]{0:T(128)} %add_convert_fusion.masks.refs_1_, f32[16,8,128]{2,1,0:T(8,128)} %pad.8.own, f32[2,128,512]{2,1,0:T(8,128)} %bitcast.27, f32[128,512]{1,0:T(8,128)} %copy-done.17, f32[128,512]{1,0:T(8,128)} %copy-done.16), custom_call_target="tpu_custom_call" | custom-call | flops 100000000 | bytes 1048576 | tf_op jit(solution)/shard_map/pallas_call | solution.py:536
  19.8 0.1 pad_maximum_fusion.2
  20.0 1.7 collective-permute-start.4
  21.7 5.6 %all-to-all-start = ((f32[8,48,128]{2,1,0:T(8,128)}), f32[8,48,128]{2,1,0:T(8,128)S(1)}, u32[]{:S(2)}, u32[]{:S(2)}) async-start(f32[8,48,128]{2,1,0:T(8,128)} %get-tuple-element.45), calls=%async_computation | async-start | bytes 393216 | tf_op jit(solution)/shard_map/all_to_all | solution.py:505
  27.4 8.0 %collective-permute-start.6 = (f32[96,8,128]{2,1,0:T(8,128)S(1)}, f32[96,8,128]{2,1,0:T(8,128)S(1)}, u32[]{:S(2)}, u32[]{:S(2)}) collective-permute-start(f32[96,8,128]{2,1,0:T(8,128)S(1)} %slice_select_fusion), channel_id=1, source_target_pairs={{0,1},{1,0},{2,3},{3,2},{4,5},{5,4},{6,7},{7,6},{8,9},{9,8},{10,11... | collective-permute-start | bytes 1179656 | tf_op jit(solution)/shard_map/ppermute | solution.py:47
  35.4 0.6 all-to-all-done.own_v
  36.0 3.6 %collective-permute-start.7 = (f32[8,48,128]{2,1,0:T(8,128)S(1)}, f32[8,48,128]{2,1,0:T(8,128)S(1)}, u32[]{:S(2)}, u32[]{:S(2)}) collective-permute-start(f32[8,48,128]{2,1,0:T(8,128)S(1)} %all-to-all-done.own_v), channel_id=1, source_target_pairs={{0,1},{1,0},{2,3},{3,2},{4,5},{5,4},{6,7},{7,6},{8,9},{9,8},{10,11... | collective-permute-start | bytes 589832 | tf_op jit(solution)/shard_map/ppermute | solution.py:47
  39.6 0.8 pad_maximum_fusion.6.mine
  40.4 0.7 copy-done.9
  41.1 4.0 %shard_map.78 = (bf16[96,2048]{1,0:T(8,128)(2,1)}, bf16[2048,256]{1,0:T(8,128)(2,1)}, bf16[2,640,256]{2,1,0:T(8,128)(2,1)}) custom-call(s32[16]{0:T(128)} %bitcast.32, f32[4]{0:T(128)} %add_convert_fusion.masks.refs_1_, s32[1]{0:T(128)} %bitcast.5.core, f32[16,8,128]{2,1,0:T(8,128)} %pad.8.own, f32[32,8,128]{2,1,0:T(8,128)} %pad_maximum_fusion.6.mine, ...), custom_call_target="tpu_custom_call" | custom-call | flops 100000000 | bytes 1048576 | tf_op jit(solution)/shard_map/pallas_call | solution.py:564
  45.2 1.1 copy-done
  46.2 0.7 shard_map.79
  47.0 13.8 %all_to_all.40.came = f32[16,40,128]{2,1,0:T(8,128)} all-to-all(f32[16,40,128]{2,1,0:T(8,128)S(1)} %shard_map.79), channel_id=1, replica_groups={{0,2,4,6,8,10,12,14,16,18,20,22,24,26,28,30},{1,3,5,7,9,11,13,15,17,19,..., dimensions={0} | all-to-all | bytes 655360 | tf_op jit(solution)/shard_map/all_to_all | solution.py:522
  60.8 8.4 %shard_map.80 = (f32[2048,128]{1,0:T(8,128)}, f32[512,128]{1,0:T(8,128)}, f32[512,128]{1,0:T(8,128)}, f32[512,128]{1,0:T(8,128)}, f32[512,128]{1,0:T(8,128)}, /*index=5*/f32[8,48,128]{2,1,0:T(8,128)}) custom-call(s32[16]{0:T(128)} %bitcast.33, bf16[2048,2048]{1,0:T(8,128)(2,1)} %bitcast.24, bf16[96,2048]{1,0:T(8,128)(2,1)} %get-tuple-element.44.bgt.refs_3_, ...), custom_call_target="tpu_custom_call" | custom-call | flops 2000000000 | bytes 1048576 | tf_op jit(solution)/shard_map/pallas_call | solution.py:584
  69.2 12.0 %all_to_all.41.own_v = f32[8,48,128]{2,1,0:T(8,128)S(1)} all-to-all(f32[8,48,128]{2,1,0:T(8,128)} %get-tuple-element.47), channel_id=1, replica_groups=mesh['row'=8,'col'=32] {'row'}, dimensions={0} | all-to-all | bytes 393216 | tf_op jit(solution)/shard_map/all_to_all | solution.py:505
  81.2 3.0 %collective-permute-start.8 = (f32[8,48,128]{2,1,0:T(8,128)S(1)}, f32[8,48,128]{2,1,0:T(8,128)S(1)}, u32[]{:S(2)}, u32[]{:S(2)}) collective-permute-start(f32[8,48,128]{2,1,0:T(8,128)S(1)} %all_to_all.41.own_v), channel_id=1, source_target_pairs={{0,1},{1,0},{2,3},{3,2},{4,5},{5,4},{6,7},{7,6},{8,9},{9,8},{10,11... | collective-permute-start | bytes 589832 | tf_op jit(solution)/shard_map/ppermute | solution.py:47
  84.2 1.1 collective-permute-done.8.other_v
  85.3 1.4 shard_map.81
  86.6 3.8 %all-to-all-start.3 = ((f32[16,40,128]{2,1,0:T(8,128)}), f32[16,40,128]{2,1,0:T(8,128)S(1)}, u32[]{:S(2)}, u32[]{:S(2)}) async-start(f32[16,40,128]{2,1,0:T(8,128)} %shard_map.81), calls=%async_computation.3 | async-start | bytes 655360 | tf_op jit(solution)/shard_map/all_to_all | solution.py:522
  90.4 0.6 collective-permute-start.9
  91.0 2.4 %collective-permute-start.10 = (f32[512,128]{1,0:T(8,128)}, f32[512,128]{1,0:T(8,128)S(1)}, u32[]{:S(2)}, u32[]{:S(2)}) collective-permute-start(f32[512,128]{1,0:T(8,128)} %get-tuple-element.50.refs_11_), channel_id=1, source_target_pairs={{0,224},{32,0},{64,32},{96,64},{128,96},{160,128},{192,160},{224,1... | collective-permute-start | bytes 786440 | tf_op jit(solution)/shard_map/ppermute | solution.py:37
  93.4 2.5 %collective-permute-start.11 = (f32[512,128]{1,0:T(8,128)}, f32[512,128]{1,0:T(8,128)S(1)}, u32[]{:S(2)}, u32[]{:S(2)}) collective-permute-start(f32[512,128]{1,0:T(8,128)} %get-tuple-element.51.refs_14_), channel_id=1, source_target_pairs={{0,1},{1,2},{2,3},{3,4},{4,5},{5,6},{6,7},{7,8},{8,9},{9,10},{10,1... | collective-permute-start | bytes 786440 | tf_op jit(solution)/shard_map/ppermute | solution.py:37
  95.9 3.5 %collective-permute-done.9.refs_7_ = f32[512,128]{1,0:T(8,128)S(1)} collective-permute-done((f32[512,128]{1,0:T(8,128)}, f32[512,128]{1,0:T(8,128)S(1)}, u32[]{:S(2)}, u32[]{:S(2)}) %collective-permute-start.9) | collective-permute-done | bytes 262176 | tf_op jit(solution)/shard_map/ppermute | solution.py:37
  99.3 0.4 collective-permute-done.11.refs_9_
  99.7 2.4 %collective-permute-done.12.refs_10_ = f32[512,128]{1,0:T(8,128)S(1)} collective-permute-done((f32[512,128]{1,0:T(8,128)}, f32[512,128]{1,0:T(8,128)S(1)}, u32[]{:S(2)}, u32[]{:S(2)}) %collective-permute-start.12) | collective-permute-done | bytes 262176 | tf_op jit(solution)/shard_map/ppermute | solution.py:37
  102.2 0.7 copy-done.21
  102.9 0.1 copy-done.6
  103.0 9.7 %shard_map.82 = (f32[2048,128]{1,0:T(8,128)}, f32[1024,128]{1,0:T(8,128)}, f32[2048,128]{1,0:T(8,128)}, f32[1024,128]{1,0:T(8,128)}, f32[1024,128]{1,0:T(8,128)}...) custom-call(s32[16]{0:T(128)} %bitcast.34, ...), custom_call_target="tpu_custom_call" | custom-call | flops 2000000000 | bytes 1048576 | tf_op jit(solution)/shard_map/pallas_call | solution.py:603
  112.7 12.0 %all_to_all.42.own_v = f32[8,48,128]{2,1,0:T(8,128)S(1)} all-to-all(f32[8,48,128]{2,1,0:T(8,128)} %get-tuple-element.53), channel_id=1, replica_groups=mesh['row'=8,'col'=32] {'row'}, dimensions={0} | all-to-all | bytes 393216 | tf_op jit(solution)/shard_map/all_to_all | solution.py:505
  124.7 2.9 %collective-permute-start.13 = (f32[8,48,128]{2,1,0:T(8,128)S(1)}, f32[8,48,128]{2,1,0:T(8,128)S(1)}, u32[]{:S(2)}, u32[]{:S(2)}) collective-permute-start(f32[8,48,128]{2,1,0:T(8,128)S(1)} %all_to_all.42.own_v), channel_id=1, source_target_pairs={{0,1},{1,0},{2,3},{3,2},{4,5},{5,4},{6,7},{7,6},{8,9},{9,8},{10,11... | collective-permute-start | bytes 589832 | tf_op jit(solution)/shard_map/ppermute | solution.py:47
  127.6 1.1 collective-permute-done.13.other_v
  128.7 1.4 shard_map.83
  130.1 5.9 %all-to-all-start.5 = ((f32[16,40,128]{2,1,0:T(8,128)}), f32[16,40,128]{2,1,0:T(8,128)S(1)}, u32[]{:S(2)}, u32[]{:S(2)}) async-start(f32[16,40,128]{2,1,0:T(8,128)} %shard_map.83), calls=%async_computation.5 | async-start | bytes 655360 | tf_op jit(solution)/shard_map/all_to_all | solution.py:522
  135.9 0.4 collective-permute-start.14
  136.3 2.4 %collective-permute-start.15 = (f32[512,128]{1,0:T(8,128)}, f32[512,128]{1,0:T(8,128)S(1)}, u32[]{:S(2)}, u32[]{:S(2)}) collective-permute-start(f32[512,128]{1,0:T(8,128)} %get-tuple-element.56.refs_11_), channel_id=1, source_target_pairs={{0,224},{32,0},{64,32},{96,64},{128,96},{160,128},{192,160},{224,1... | collective-permute-start | bytes 786440 | tf_op jit(solution)/shard_map/ppermute | solution.py:37
  138.7 2.5 %collective-permute-start.16 = (f32[512,128]{1,0:T(8,128)}, f32[512,128]{1,0:T(8,128)S(1)}, u32[]{:S(2)}, u32[]{:S(2)}) collective-permute-start(f32[512,128]{1,0:T(8,128)} %get-tuple-element.57.refs_14_), channel_id=1, source_target_pairs={{0,1},{1,2},{2,3},{3,4},{4,5},{5,6},{6,7},{7,8},{8,9},{9,10},{10,1... | collective-permute-start | bytes 786440 | tf_op jit(solution)/shard_map/ppermute | solution.py:37
  141.2 3.6 %collective-permute-done.14.refs_7_ = f32[512,128]{1,0:T(8,128)S(1)} collective-permute-done((f32[512,128]{1,0:T(8,128)}, f32[512,128]{1,0:T(8,128)S(1)}, u32[]{:S(2)}, u32[]{:S(2)}) %collective-permute-start.14) | collective-permute-done | bytes 262176 | tf_op jit(solution)/shard_map/ppermute | solution.py:37
  144.8 0.3 collective-permute-done.16.refs_9_
  145.1 2.4 %collective-permute-done.17.refs_10_ = f32[512,128]{1,0:T(8,128)S(1)} collective-permute-done((f32[512,128]{1,0:T(8,128)}, f32[512,128]{1,0:T(8,128)S(1)}, u32[]{:S(2)}, u32[]{:S(2)}) %collective-permute-start.17) | collective-permute-done | bytes 262176 | tf_op jit(solution)/shard_map/ppermute | solution.py:37
  147.6 0.7 copy-done.13
  148.2 0.1 copy-done.5
  148.4 10.5 %shard_map.84 = (f32[2048,128]{1,0:T(8,128)}, f32[1024,128]{1,0:T(8,128)}, f32[2048,128]{1,0:T(8,128)}, f32[1024,128]{1,0:T(8,128)}, f32[1024,128]{1,0:T(8,128)}...) custom-call(s32[16]{0:T(128)} %bitcast.35, ...), custom_call_target="tpu_custom_call" | custom-call | flops 2000000000 | bytes 1048576 | tf_op jit(solution)/shard_map/pallas_call | solution.py:603
  158.9 11.9 %all_to_all.43.own_v = f32[8,48,128]{2,1,0:T(8,128)S(1)} all-to-all(f32[8,48,128]{2,1,0:T(8,128)} %get-tuple-element.64), channel_id=1, replica_groups=mesh['row'=8,'col'=32] {'row'}, dimensions={0} | all-to-all | bytes 393216 | tf_op jit(solution)/shard_map/all_to_all | solution.py:505
  170.8 2.8 %collective-permute-start.18 = (f32[8,48,128]{2,1,0:T(8,128)S(1)}, f32[8,48,128]{2,1,0:T(8,128)S(1)}, u32[]{:S(2)}, u32[]{:S(2)}) collective-permute-start(f32[8,48,128]{2,1,0:T(8,128)S(1)} %all_to_all.43.own_v), channel_id=1, source_target_pairs={{0,1},{1,0},{2,3},{3,2},{4,5},{5,4},{6,7},{7,6},{8,9},{9,8},{10,11... | collective-permute-start | bytes 589832 | tf_op jit(solution)/shard_map/ppermute | solution.py:47
  173.6 1.1 collective-permute-done.18.other_v
  174.7 1.4 shard_map.85
  176.0 6.2 %all-to-all-start.7 = ((f32[16,40,128]{2,1,0:T(8,128)}), f32[16,40,128]{2,1,0:T(8,128)S(1)}, u32[]{:S(2)}, u32[]{:S(2)}) async-start(f32[16,40,128]{2,1,0:T(8,128)} %shard_map.85), calls=%async_computation.7 | async-start | bytes 655360 | tf_op jit(solution)/shard_map/all_to_all | solution.py:522
  182.4 0.5 collective-permute-start.20
  182.9 7.1 %collective-permute-done.19.ns = f32[512,128]{1,0:T(8,128)S(1)} collective-permute-done((f32[512,128]{1,0:T(8,128)}, f32[512,128]{1,0:T(8,128)S(1)}, u32[]{:S(2)}, u32[]{:S(2)}) %collective-permute-start.19) | collective-permute-done | bytes 262176 | tf_op jit(solution)/shard_map/ppermute | solution.py:37
  190.0 1.8 collective-permute-done.20.ne
  191.8 0.7 copy-done.15
  192.5 0.1 copy-done.4
  192.6 4.2 %shard_map.86 = (f32[2,128,512]{2,1,0:T(8,128)}, f32[2,128,512]{2,1,0:T(8,128)}) custom-call(f32[4]{0:T(128)} %add_convert_fusion.masks.refs_1_, bf16[2048,256]{1,0:T(8,128)(2,1)} %get-tuple-element.42.bgc.refs_4_, f32[16,40,128]{2,1,0:T(8,128)} %copy-done.4, f32[2048,128]{1,0:T(8,128)} %get-tuple-element.65.residual, f32[512,128]{1,0:T(8,128)} %copy-done.14, ...), custom_call_target="tpu_custom_call" | custom-call | flops 100000000 | bytes 1048576 | tf_op jit(solution)/shard_map/pallas_call | solution.py:616
  (59 shorter events, 0.6 us)
Async XLA Ops:
  1.7 12.4 %collective-permute-start.3 = (f32[128,512]{1,0:T(8,128)S(1)}, f32[128,512]{1,0:T(8,128)S(1)}, u32[]{:S(2)}, u32[]{:S(2)}) collective-permute-start(f32[128,512]{1,0:T(8,128)S(1)} %get-tuple-element.76), channel_id=1, source_target_pairs={{0,1},{1,2},{2,3},{3,4},{4,5},{5,6},{6,7},{7,8},{8,9},{9,10},{10,1... | collective-permute-start | bytes 786440 | tf_op jit(solution)/shard_map/ppermute | solution.py:37
  4.5 11.2 %collective-permute-start.2 = (f32[128,512]{1,0:T(8,128)S(1)}, f32[128,512]{1,0:T(8,128)S(1)}, u32[]{:S(2)}, u32[]{:S(2)}) collective-permute-start(f32[128,512]{1,0:T(8,128)S(1)} %get-tuple-element.77), channel_id=1, source_target_pairs={{0,32},{32,64},{64,96},{96,128},{128,160},{160,192},{192,224},{224... | collective-permute-start | bytes 786440 | tf_op jit(solution)/shard_map/ppermute | solution.py:37
  8.9 10.8 %collective-permute-start.1 = (f32[36,8,128]{2,1,0:T(8,128)S(1)}, f32[36,8,128]{2,1,0:T(8,128)S(1)}, u32[]{:S(2)}, u32[]{:S(2)}) collective-permute-start(f32[36,8,128]{2,1,0:T(8,128)S(1)} %get-tuple-element.80), channel_id=1, source_target_pairs={{0,224},{32,0},{64,32},{96,64},{128,96},{160,128},{192,160},{224,1... | collective-permute-start | bytes 442376 | tf_op jit(solution)/shard_map/ppermute | solution.py:37
  12.9 6.8 %collective-permute-start = (f32[36,8,128]{2,1,0:T(8,128)S(1)}, f32[36,8,128]{2,1,0:T(8,128)S(1)}, u32[]{:S(2)}, u32[]{:S(2)}) collective-permute-start(f32[36,8,128]{2,1,0:T(8,128)S(1)} %get-tuple-element.81), channel_id=1, source_target_pairs={{0,32},{32,64},{64,96},{96,128},{128,160},{160,192},{192,224},{224... | collective-permute-start | bytes 442376 | tf_op jit(solution)/shard_map/ppermute | solution.py:37
  14.1 1.6 copy-start.16
  15.7 0.7 copy-start.17
  19.7 20.7 %copy-start.7 = (f32[36,8,128]{2,1,0:T(8,128)}, f32[36,8,128]{2,1,0:T(8,128)S(1)}, u32[]{:S(2)}) copy-start(f32[36,8,128]{2,1,0:T(8,128)S(1)} %collective-permute-done.1.up) | copy-start | bytes 442372
  19.7 20.7 %copy-start.8 = (f32[36,8,128]{2,1,0:T(8,128)}, f32[36,8,128]{2,1,0:T(8,128)S(1)}, u32[]{:S(2)}) copy-start(f32[36,8,128]{2,1,0:T(8,128)S(1)} %collective-permute-done.down) | copy-start | bytes 442372
  19.9 7.5 %collective-permute-start.5 = (f32[100,8,128]{2,1,0:T(8,128)S(1)}, f32[100,8,128]{2,1,0:T(8,128)S(1)}, u32[]{:S(2)}, u32[]{:S(2)}) collective-permute-start(f32[100,8,128]{2,1,0:T(8,128)S(1)} %get-tuple-element.78), channel_id=1, source_target_pairs={{0,31},{1,0},{2,1},{3,2},{4,3},{5,4},{6,5},{7,6},{8,7},{9,8},{10,9... | collective-permute-start | bytes 1228808 | tf_op jit(solution)/shard_map/ppermute | solution.py:37
  20.0 7.4 %collective-permute-start.4 = (f32[100,8,128]{2,1,0:T(8,128)S(1)}, f32[100,8,128]{2,1,0:T(8,128)S(1)}, u32[]{:S(2)}, u32[]{:S(2)}) collective-permute-start(f32[100,8,128]{2,1,0:T(8,128)S(1)} %get-tuple-element.79), channel_id=1, source_target_pairs={{0,1},{1,2},{2,3},{3,4},{4,5},{5,6},{6,7},{7,8},{8,9},{9,10},{10,1... | collective-permute-start | bytes 1228808 | tf_op jit(solution)/shard_map/ppermute | solution.py:37
  21.7 14.3 %all-to-all-start = ((f32[8,48,128]{2,1,0:T(8,128)}), f32[8,48,128]{2,1,0:T(8,128)S(1)}, u32[]{:S(2)}, u32[]{:S(2)}) async-start(f32[8,48,128]{2,1,0:T(8,128)} %get-tuple-element.45), calls=%async_computation | async-start | bytes 393216 | tf_op jit(solution)/shard_map/all_to_all | solution.py:505
  27.3 13.1 %copy-start.2 = (f32[100,8,128]{2,1,0:T(8,128)}, f32[100,8,128]{2,1,0:T(8,128)S(1)}, u32[]{:S(2)}) copy-start(f32[100,8,128]{2,1,0:T(8,128)S(1)} %collective-permute-done.5.left) | copy-start | bytes 1228804
  27.3 13.1 %copy-start.3 = (f32[100,8,128]{2,1,0:T(8,128)}, f32[100,8,128]{2,1,0:T(8,128)S(1)}, u32[]{:S(2)}) copy-start(f32[100,8,128]{2,1,0:T(8,128)S(1)} %collective-permute-done.4.right) | copy-start | bytes 1228804
  27.4 13.0 %collective-permute-start.6 = (f32[96,8,128]{2,1,0:T(8,128)S(1)}, f32[96,8,128]{2,1,0:T(8,128)S(1)}, u32[]{:S(2)}, u32[]{:S(2)}) collective-permute-start(f32[96,8,128]{2,1,0:T(8,128)S(1)} %slice_select_fusion), channel_id=1, source_target_pairs={{0,1},{1,0},{2,3},{3,2},{4,5},{5,4},{6,7},{7,6},{8,9},{9,8},{10,11... | collective-permute-start | bytes 1179656 | tf_op jit(solution)/shard_map/ppermute | solution.py:47
  36.0 9.1 %collective-permute-start.7 = (f32[8,48,128]{2,1,0:T(8,128)S(1)}, f32[8,48,128]{2,1,0:T(8,128)S(1)}, u32[]{:S(2)}, u32[]{:S(2)}) collective-permute-start(f32[8,48,128]{2,1,0:T(8,128)S(1)} %all-to-all-done.own_v), channel_id=1, source_target_pairs={{0,1},{1,0},{2,3},{3,2},{4,5},{5,4},{6,7},{7,6},{8,9},{9,8},{10,11... | collective-permute-start | bytes 589832 | tf_op jit(solution)/shard_map/ppermute | solution.py:47
  40.4 0.8 copy-start.9
  45.2 1.1 copy-start
  46.2 39.0 %copy-start.1 = (bf16[2,640,256]{2,1,0:T(8,128)(2,1)S(1)}, bf16[2,640,256]{2,1,0:T(8,128)(2,1)}, u32[]{:S(2)}) copy-start(bf16[2,640,256]{2,1,0:T(8,128)(2,1)} %get-tuple-element.43.parts) | copy-start | bytes 1966084
  81.2 4.0 %collective-permute-start.8 = (f32[8,48,128]{2,1,0:T(8,128)S(1)}, f32[8,48,128]{2,1,0:T(8,128)S(1)}, u32[]{:S(2)}, u32[]{:S(2)}) collective-permute-start(f32[8,48,128]{2,1,0:T(8,128)S(1)} %all_to_all.41.own_v), channel_id=1, source_target_pairs={{0,1},{1,0},{2,3},{3,2},{4,5},{5,4},{6,7},{7,6},{8,9},{9,8},{10,11... | collective-permute-start | bytes 589832 | tf_op jit(solution)/shard_map/ppermute | solution.py:47
  86.6 15.5 %all-to-all-start.3 = ((f32[16,40,128]{2,1,0:T(8,128)}), f32[16,40,128]{2,1,0:T(8,128)S(1)}, u32[]{:S(2)}, u32[]{:S(2)}) async-start(f32[16,40,128]{2,1,0:T(8,128)} %shard_map.81), calls=%async_computation.3 | async-start | bytes 655360 | tf_op jit(solution)/shard_map/all_to_all | solution.py:522
  90.4 8.9 %collective-permute-start.9 = (f32[512,128]{1,0:T(8,128)}, f32[512,128]{1,0:T(8,128)S(1)}, u32[]{:S(2)}, u32[]{:S(2)}) collective-permute-start(f32[512,128]{1,0:T(8,128)} %get-tuple-element.49.refs_12_), channel_id=1, source_target_pairs={{0,32},{32,64},{64,96},{96,128},{128,160},{160,192},{192,224},{224... | collective-permute-start | bytes 786440 | tf_op jit(solution)/shard_map/ppermute | solution.py:37
  91.0 8.3 %collective-permute-start.10 = (f32[512,128]{1,0:T(8,128)}, f32[512,128]{1,0:T(8,128)S(1)}, u32[]{:S(2)}, u32[]{:S(2)}) collective-permute-start(f32[512,128]{1,0:T(8,128)} %get-tuple-element.50.refs_11_), channel_id=1, source_target_pairs={{0,224},{32,0},{64,32},{96,64},{128,96},{160,128},{192,160},{224,1... | collective-permute-start | bytes 786440 | tf_op jit(solution)/shard_map/ppermute | solution.py:37
  93.4 6.3 %collective-permute-start.11 = (f32[512,128]{1,0:T(8,128)}, f32[512,128]{1,0:T(8,128)S(1)}, u32[]{:S(2)}, u32[]{:S(2)}) collective-permute-start(f32[512,128]{1,0:T(8,128)} %get-tuple-element.51.refs_14_), channel_id=1, source_target_pairs={{0,1},{1,2},{2,3},{3,4},{4,5},{5,6},{6,7},{7,8},{8,9},{9,10},{10,1... | collective-permute-start | bytes 786440 | tf_op jit(solution)/shard_map/ppermute | solution.py:37
  95.9 6.3 %collective-permute-start.12 = (f32[512,128]{1,0:T(8,128)}, f32[512,128]{1,0:T(8,128)S(1)}, u32[]{:S(2)}, u32[]{:S(2)}) collective-permute-start(f32[512,128]{1,0:T(8,128)} %get-tuple-element.52.refs_13_), channel_id=1, source_target_pairs={{0,31},{1,0},{2,1},{3,2},{4,3},{5,4},{6,5},{7,6},{8,7},{9,8},{10,9... | collective-permute-start | bytes 786440 | tf_op jit(solution)/shard_map/ppermute | solution.py:37
  99.3 2.9 %copy-start.18 = (f32[512,128]{1,0:T(8,128)}, f32[512,128]{1,0:T(8,128)S(1)}, u32[]{:S(2)}) copy-start(f32[512,128]{1,0:T(8,128)S(1)} %collective-permute-done.9.refs_7_) | copy-start | bytes 786436
  99.3 2.9 %copy-start.19 = (f32[512,128]{1,0:T(8,128)}, f32[512,128]{1,0:T(8,128)S(1)}, u32[]{:S(2)}) copy-start(f32[512,128]{1,0:T(8,128)S(1)} %collective-permute-done.10.refs_8_) | copy-start | bytes 786436
  99.7 2.5 %copy-start.20 = (f32[512,128]{1,0:T(8,128)}, f32[512,128]{1,0:T(8,128)S(1)}, u32[]{:S(2)}) copy-start(f32[512,128]{1,0:T(8,128)S(1)} %collective-permute-done.11.refs_9_) | copy-start | bytes 786436
  102.2 0.7 copy-start.21
  102.2 0.8 copy-start.6
  124.7 3.9 %collective-permute-start.13 = (f32[8,48,128]{2,1,0:T(8,128)S(1)}, f32[8,48,128]{2,1,0:T(8,128)S(1)}, u32[]{:S(2)}, u32[]{:S(2)}) collective-permute-start(f32[8,48,128]{2,1,0:T(8,128)S(1)} %all_to_all.42.own_v), channel_id=1, source_target_pairs={{0,1},{1,0},{2,3},{3,2},{4,5},{5,4},{6,7},{7,6},{8,9},{9,8},{10,11... | collective-permute-start | bytes 589832 | tf_op jit(solution)/shard_map/ppermute | solution.py:47
  130.1 17.4 %all-to-all-start.5 = ((f32[16,40,128]{2,1,0:T(8,128)}), f32[16,40,128]{2,1,0:T(8,128)S(1)}, u32[]{:S(2)}, u32[]{:S(2)}) async-start(f32[16,40,128]{2,1,0:T(8,128)} %shard_map.83), calls=%async_computation.5 | async-start | bytes 655360 | tf_op jit(solution)/shard_map/all_to_all | solution.py:522
  135.9 8.9 %collective-permute-start.14 = (f32[512,128]{1,0:T(8,128)}, f32[512,128]{1,0:T(8,128)S(1)}, u32[]{:S(2)}, u32[]{:S(2)}) collective-permute-start(f32[512,128]{1,0:T(8,128)} %get-tuple-element.55.refs_12_), channel_id=1, source_target_pairs={{0,32},{32,64},{64,96},{96,128},{128,160},{160,192},{192,224},{224... | collective-permute-start | bytes 786440 | tf_op jit(solution)/shard_map/ppermute | solution.py:37
  136.3 8.5 %collective-permute-start.15 = (f32[512,128]{1,0:T(8,128)}, f32[512,128]{1,0:T(8,128)S(1)}, u32[]{:S(2)}, u32[]{:S(2)}) collective-permute-start(f32[512,128]{1,0:T(8,128)} %get-tuple-element.56.refs_11_), channel_id=1, source_target_pairs={{0,224},{32,0},{64,32},{96,64},{128,96},{160,128},{192,160},{224,1... | collective-permute-start | bytes 786440 | tf_op jit(solution)/shard_map/ppermute | solution.py:37
  138.7 6.4 %collective-permute-start.16 = (f32[512,128]{1,0:T(8,128)}, f32[512,128]{1,0:T(8,128)S(1)}, u32[]{:S(2)}, u32[]{:S(2)}) collective-permute-start(f32[512,128]{1,0:T(8,128)} %get-tuple-element.57.refs_14_), channel_id=1, source_target_pairs={{0,1},{1,2},{2,3},{3,4},{4,5},{5,6},{6,7},{7,8},{8,9},{9,10},{10,1... | collective-permute-start | bytes 786440 | tf_op jit(solution)/shard_map/ppermute | solution.py:37
  141.2 6.3 %collective-permute-start.17 = (f32[512,128]{1,0:T(8,128)}, f32[512,128]{1,0:T(8,128)S(1)}, u32[]{:S(2)}, u32[]{:S(2)}) collective-permute-start(f32[512,128]{1,0:T(8,128)} %get-tuple-element.58.refs_13_), channel_id=1, source_target_pairs={{0,31},{1,0},{2,1},{3,2},{4,3},{5,4},{6,5},{7,6},{8,7},{9,8},{10,9... | collective-permute-start | bytes 786440 | tf_op jit(solution)/shard_map/ppermute | solution.py:37
  144.8 2.7 %copy-start.10 = (f32[512,128]{1,0:T(8,128)}, f32[512,128]{1,0:T(8,128)S(1)}, u32[]{:S(2)}) copy-start(f32[512,128]{1,0:T(8,128)S(1)} %collective-permute-done.14.refs_7_) | copy-start | bytes 786436
  144.8 2.7 %copy-start.11 = (f32[512,128]{1,0:T(8,128)}, f32[512,128]{1,0:T(8,128)S(1)}, u32[]{:S(2)}) copy-start(f32[512,128]{1,0:T(8,128)S(1)} %collective-permute-done.15.refs_8_) | copy-start | bytes 786436
  145.1 2.5 %copy-start.12 = (f32[512,128]{1,0:T(8,128)}, f32[512,128]{1,0:T(8,128)S(1)}, u32[]{:S(2)}) copy-start(f32[512,128]{1,0:T(8,128)S(1)} %collective-permute-done.16.refs_9_) | copy-start | bytes 786436
  147.5 0.7 copy-start.13
  147.5 0.8 copy-start.5
  170.8 3.9 %collective-permute-start.18 = (f32[8,48,128]{2,1,0:T(8,128)S(1)}, f32[8,48,128]{2,1,0:T(8,128)S(1)}, u32[]{:S(2)}, u32[]{:S(2)}) collective-permute-start(f32[8,48,128]{2,1,0:T(8,128)S(1)} %all_to_all.43.own_v), channel_id=1, source_target_pairs={{0,1},{1,0},{2,3},{3,2},{4,5},{5,4},{6,7},{7,6},{8,9},{9,8},{10,11... | collective-permute-start | bytes 589832 | tf_op jit(solution)/shard_map/ppermute | solution.py:47
  176.0 15.7 %all-to-all-start.7 = ((f32[16,40,128]{2,1,0:T(8,128)}), f32[16,40,128]{2,1,0:T(8,128)S(1)}, u32[]{:S(2)}, u32[]{:S(2)}) async-start(f32[16,40,128]{2,1,0:T(8,128)} %shard_map.85), calls=%async_computation.7 | async-start | bytes 655360 | tf_op jit(solution)/shard_map/all_to_all | solution.py:522
  182.3 7.7 %collective-permute-start.19 = (f32[512,128]{1,0:T(8,128)}, f32[512,128]{1,0:T(8,128)S(1)}, u32[]{:S(2)}, u32[]{:S(2)}) collective-permute-start(f32[512,128]{1,0:T(8,128)} %get-tuple-element.66), channel_id=1, source_target_pairs={{0,224},{32,0},{64,32},{96,64},{128,96},{160,128},{192,160},{224,1... | collective-permute-start | bytes 786440 | tf_op jit(solution)/shard_map/ppermute | solution.py:37
  182.4 9.4 %collective-permute-start.20 = (f32[512,128]{1,0:T(8,128)}, f32[512,128]{1,0:T(8,128)S(1)}, u32[]{:S(2)}, u32[]{:S(2)}) collective-permute-start(f32[512,128]{1,0:T(8,128)} %get-tuple-element.67), channel_id=1, source_target_pairs={{0,31},{1,0},{2,1},{3,2},{4,3},{5,4},{6,5},{7,6},{8,7},{9,8},{10,9... | collective-permute-start | bytes 786440 | tf_op jit(solution)/shard_map/ppermute | solution.py:37
  190.0 1.8 copy-start.14
  191.8 0.7 copy-start.15
  191.8 0.8 copy-start.4

commit v2 on v1

--- a/solution.py
+++ b/solution.py
@@ -18,10 +18,12 @@
 ITERS = 3
 SLOT = 8
 SLOTS = 5
-PAY = 48
+PAY = 40
+ROWS16 = 48
 TERMS = ((0, 0), (0, 1), (1, 0), (1, 1), (0, 2), (2, 0))
 TALL = 1024
 CHIPS = 16
+COST = 2 * 10**10
 
 f32 = jnp.float32
 bf16 = jnp.bfloat16
@@ -123,21 +125,24 @@
     copies.close()
 
 
-def setup_kernel(
-    order, masks, core, own, mine, down, up, right, left, far, bgt, bgc, parts,
-    own_v, mine_v, down_v, up_v, right_v, left_v, far_v, full, turned, table, bgt_v, bgc_v, parts_v, sems,
+def modes_kernel(
+    order, masks, own, down, up, right, left, bgt, bgc,
+    own_v, down_v, up_v, right_v, left_v, full, turned, bgt_v, bgc_v, sems,
 ):
     copies = Copies(sems)
-    pairs = ((own, own_v), (mine, mine_v), (down, down_v), (up, up_v), (right, right_v), (left, left_v), (far, far_v))
-    ready = [copies.start(source, target) for source, target in pairs]
+    ready = [copies.start(own, own_v)]
+    for source, target in ((down, down_v), (up, up_v)):
+        ready.append(copies.start(source.at[pl.ds(COLS, 4)], target))
+    for source, target in ((right, right_v), (left, left_v)):
+        ready.append(copies.start(source.at[pl.ds(3 * COLS, 4)], target))
     full[...] = jnp.zeros_like(full)
     wait(ready)
     own_modes(full, own_v, masks)
-    for slot, (near, at) in enumerate(((down_v, COLS), (up_v, COLS), (right_v, 3 * COLS), (left_v, 3 * COLS))):
+    for slot, near in enumerate((down_v, up_v, right_v, left_v)):
         rows = slice(SLOT * (slot + 1), SLOT * (slot + 2))
         for block in range(M // BLK):
             lanes = slice(M * slot + BLK * block, M * slot + BLK * (block + 1))
-            full[rows, lanes] = near[at + block] * -masks[slot]
+            full[rows, lanes] = near[block] * -masks[slot]
     pieces = parts_of(full[...], 3)
     for index, (which, _) in enumerate(TERMS):
         turned[40 * index : 40 * (index + 1), :] = pieces[which][0:40].astype(f32)
@@ -150,9 +155,18 @@
     for block in range(NB):
         at = pl.multiple_of(order[block] * BLK, BLK)
         for index, piece in enumerate(parts_of(full[:, pl.ds(at, BLK)], 2)):
-            bgt_v[PAY * index : PAY * (index + 1), BLK * block : BLK * (block + 1)] = piece
+            bgt_v[ROWS16 * index : ROWS16 * (index + 1), BLK * block : BLK * (block + 1)] = piece
     copies.out(bgt_v, bgt)
-
+    copies.close()
+
+
+def table_kernel(
+    core, mine, down, up, right, left, far, parts,
+    mine_v, down_v, up_v, right_v, left_v, far_v, table, parts_v, sems,
+):
+    copies = Copies(sems)
+    pairs = ((mine, mine_v), (down, down_v), (up, up_v), (right, right_v), (left, left_v), (far, far_v))
+    wait([copies.start(source, target) for source, target in pairs])
     first = core[0] == 0
     half = lax.broadcasted_iota(jnp.int32, (SLOT, BLK), 1) < SLOT * ROWS
 
@@ -185,7 +199,7 @@
         a, b = own_v[line, here, :], other_v[line, here, :]
         return jnp.where(first, a, b) if which == 0 else jnp.where(first, b, a)
 
-    total = jnp.zeros((SLOT, K), f32)
+    total = jnp.zeros((2 * SLOT, K), f32)
     for line in range(ROWS):
         for which in range(2):
             value = tile(which, line, 0)
@@ -199,7 +213,7 @@
         entries[SLOT * line : SLOT * (line + 1), :] = tile(0, line, 3)
         at = SLOT * (ROWS * 3 + line)
         entries[at : at + SLOT, :] = tile(1, line, 4)
-        total = total + own_v[line, SLOT * SLOTS :, :] + other_v[line, SLOT * SLOTS :, :]
+        total = total + own_v[line, : 2 * SLOT, :] + other_v[line, : 2 * SLOT, :]
     both = jnp.concatenate(parts_of(entries[...], 2), axis=1)
     wait(table)
     d = jnp.dot(parts_v[0], both, preferred_element_type=f32)
@@ -207,8 +221,8 @@
     value = e[:, K:] + e[:, :K] + d[:, K:] + d[:, :K]
     for target in range(CHIPS):
         out_v[target] = value[SLOTS * SLOT * target : SLOTS * SLOT * (target + 1)]
-        out_v[target, 6:8, :] = total[0:2]
-        out_v[target, 14:15, :] = total[2:3]
+        out_v[target, 6:8, :] = total[6:8]
+        out_v[target, 14:15, :] = total[14:15]
     copies.out(out_v, out)
     copies.close()
 
@@ -243,7 +257,7 @@
             jnp.concatenate(parts_of(both, 2), axis=1),
             preferred_element_type=f32,
         )
-        value = value + d[:PAY, :K] + d[:PAY, K:] + d[PAY:, :K] + d[PAY:, K:]
+        value = value + d[:ROWS16, :K] + d[:ROWS16, K:] + d[ROWS16:, :K] + d[ROWS16:, K:]
         for piece in range(TALL // BLK):
             at = pl.multiple_of(order[step * (TALL // BLK) + piece] * BLK, BLK)
             y = both[BLK * piece : BLK * (piece + 1)]
@@ -251,7 +265,7 @@
             energy = energy + folded(residual[pl.ds(at, BLK), :] * y)
         return value, energy
 
-    return lax.fori_loop(0, NS // TALL, tall, (jnp.zeros((PAY, K), f32), jnp.zeros((SLOT, K), f32)))
+    return lax.fori_loop(0, NS // TALL, tall, (jnp.zeros((ROWS16, K), f32), jnp.zeros((SLOT, K), f32)))
 
 
 class Matrix:
@@ -283,10 +297,10 @@
 def close_product(value, norm, energy, cross, product, pay, faces, copies, pay_held):
     for face in range(4):
         copies.out(product.at[pl.ds(M * face, M)], faces[face])
-    pay_held[0:PAY, :] = value
-    pay_held[40:41, :] = jnp.sum(norm, axis=0, keepdims=True)
-    pay_held[41:42, :] = jnp.sum(energy, axis=0, keepdims=True)
-    pay_held[42:43, :] = jnp.sum(cross, axis=0, keepdims=True)
+    pay_held[...] = value[0:PAY]
+    pay_held[6:7, :] = jnp.sum(norm, axis=0, keepdims=True)
+    pay_held[7:8, :] = jnp.sum(energy, axis=0, keepdims=True)
+    pay_held[14:15, :] = jnp.sum(cross, axis=0, keepdims=True)
     for index in range(ROWS):
         copies.out(pay_held, pay.at[index])
     copies.close()
@@ -324,6 +338,24 @@
     close_product(value, norm, energy, jnp.zeros_like(norm), product, pay, (yn, ys, yw, ye), copies, pay_v)
 
 
+def image_kernel(which, *refs):
+    masks, refs = refs[0], refs[1:]
+    count = len(which)
+    faces, near, image, (y_v, near_v, sems) = refs[:count], refs[count : 2 * count], refs[2 * count], refs[2 * count + 1 :]
+    copies = Copies(sems)
+    ready = []
+    for index in range(count):
+        ready.append([copies.start(faces[index], y_v.at[index]), copies.start(near[index], near_v.at[index])])
+    for index, face in enumerate(which):
+        wait(ready[index])
+        if face % 2:
+            y_v[index] = y_v[index] - masks[face] * near_v[index]
+        else:
+            y_v[index] = masks[face] * (y_v[index] - near_v[index])
+        copies.out(y_v.at[index], image.at[index])
+    copies.close()
+
+
 def scalars(first, sums, past):
     norm, energy, cross = sums
     if first:
@@ -334,16 +366,15 @@
 
 
 def step_kernel(first, *refs):
-    order, masks, matrix, bgt, bgc, came, residual = refs[:7]
-    near, faces = refs[7:11], refs[11:15]
-    refs = refs[15:]
+    order, matrix, bgt, bgc, came, residual, local = refs[:7]
+    refs = refs[7:]
     if not first:
         past, along, moved, image, done = refs[:5]
         refs = refs[5:]
     new_residual, new_along, new_moved, new_image, new_done, new_past = refs[:6]
     new_faces, pay, refs = refs[6:10], refs[10], refs[11:]
     (inverse, held, bgt_v, bgc_v, came_v, r_v, halves, product, spread, stack, pay_v, sems, tall_sems,
-     y_v, near_v, moved_v, image_v, along_v, done_v, past_v, new_past_v) = refs
+     local_v, moved_v, image_v, along_v, done_v, past_v, new_past_v) = refs
 
     copies, matrix = Copies(sems), Matrix(matrix, held, tall_sems)
     head = [copies.start(came, came_v)]
@@ -353,9 +384,7 @@
     def fetch(pair):
         wide, own = pl.ds(2 * M * pair, 2 * M), pl.ds(M * pair, M)
         part = [copies.start(residual.at[wide], r_v.at[wide])]
-        for face in (2 * pair, 2 * pair + 1):
-            rows = pl.ds(M * face, M)
-            part += [copies.start(faces[face], y_v.at[rows]), copies.start(near[face], near_v.at[rows])]
+        part.append(copies.start(local.at[pl.ds(2 * pair, 2)], local_v.at[pl.ds(2 * pair, 2)]))
         if not first:
             part.append(copies.start(moved.at[wide], moved_v.at[wide]))
             for source, target in ((image, image_v), (along, along_v), (done, done_v)):
@@ -388,12 +417,10 @@
                 face = 2 * pair + kind
                 rows = pl.ds(pl.multiple_of(M * face + BLK * index, BLK), BLK)
                 mine = pl.ds(pl.multiple_of(M * pair + BLK * index, BLK), BLK)
+                q = local_v[face, pl.ds(pl.multiple_of(BLK * index, BLK), BLK), :]
                 if kind:
-                    q = y_v[rows, :] - masks[face] * near_v[rows, :]
                     f = q if first else q + ratio * image_v[mine, :]
                     image_v[mine, :] = f
-                else:
-                    q = masks[face] * (y_v[rows, :] - near_v[rows, :])
                 q = q - spread[pl.ds(pl.multiple_of(M * kind + BLK * index, BLK), BLK), :]
                 if not first:
                     q = q + ratio * moved_v[rows, :]
@@ -427,16 +454,16 @@
 
 
 def end_kernel(
-    masks, bgc, came, residual, ns, ne, ys, ye, past, along, moved, done, out_done, out_residual,
-    stack, bgc_v, came_v, past_v, r_v, near_v, y_v, along_v, moved_v, done_v, x_v, s_v, sems,
+    bgc, came, residual, local, past, along, moved, done, out_done, out_residual,
+    stack, bgc_v, came_v, past_v, r_v, local_v, along_v, moved_v, done_v, x_v, s_v, sems,
 ):
     copies = Copies(sems)
     head = [copies.start(came, came_v), copies.start(past, past_v)]
     body = []
-    for pair, near, mine in ((0, ns, ys), (1, ne, ye)):
+    for pair in range(2):
         rows, own = pl.ds(M * (2 * pair + 1), M), pl.ds(M * pair, M)
-        part = [copies.start(bgc.at[rows], bgc_v.at[own]), copies.start(near, near_v.at[own])]
-        part += [copies.start(mine, y_v.at[own]), copies.start(residual.at[rows], r_v.at[own])]
+        part = [copies.start(bgc.at[rows], bgc_v.at[own]), copies.start(local.at[pair], local_v.at[own])]
+        part.append(copies.start(residual.at[rows], r_v.at[own]))
         part += [copies.start(moved.at[rows], moved_v.at[own]), copies.start(along.at[own], along_v.at[own])]
         body.append(part + [copies.start(done.at[own], done_v.at[own])])
     wait(head)
@@ -447,8 +474,7 @@
         for block in range(M // BLK):
             inside = slice(BLK * block, BLK * (block + 1))
             own = slice(M * pair + BLK * block, M * pair + BLK * (block + 1))
-            q = y_v[own, :] - masks[2 * pair + 1] * near_v[own, :]
-            q = q - jnp.dot(bgc_v[own, :], stacked, preferred_element_type=f32)
+            q = local_v[own, :] - jnp.dot(bgc_v[own, :], stacked, preferred_element_type=f32)
             q = q + ratio * moved_v[own, :]
             r = r_v[own, :]
             d = r + ratio * along_v[own, :]
@@ -466,7 +492,7 @@
 WORK = [
     pltpu.SMEM((NB,), jnp.int32),
     pltpu.VMEM((NS, NS), bf16),
-    pltpu.VMEM((2 * PAY, NS), bf16),
+    pltpu.VMEM((2 * ROWS16, NS), bf16),
     pltpu.VMEM((NS, 2 * K), bf16),
     pltpu.VMEM((CHIPS, SLOTS * SLOT, K), f32),
     pltpu.VMEM((NS, K), f32),
@@ -478,11 +504,11 @@
     pltpu.SemaphoreType.DMA((64,)),
     pltpu.SemaphoreType.DMA((NS // TALL,)),
 ]
-MORE = [pltpu.VMEM((NS, K), f32)] * 3 + [pltpu.VMEM((2 * M, K), f32)] * 3 + [pltpu.VMEM((SLOT, K), f32)] * 2
+MORE = [pltpu.VMEM((4, M, K), f32), pltpu.VMEM((NS, K), f32)] + [pltpu.VMEM((2 * M, K), f32)] * 3 + [pltpu.VMEM((SLOT, K), f32)] * 2
 LAST = (
     [pltpu.VMEM((256, K), f32), pltpu.VMEM((2 * M, 2 * K), bf16), pltpu.VMEM((CHIPS, SLOTS * SLOT, K), f32)]
     + [pltpu.VMEM((SLOT, K), f32)]
-    + [pltpu.VMEM((2 * M, K), f32)] * 6
+    + [pltpu.VMEM((2 * M, K), f32)] * 5
     + [pltpu.VMEM((2, K, M), f32)] * 2
     + [pltpu.SemaphoreType.DMA((32,))]
 )
@@ -501,8 +527,9 @@
     )
 
 
-def coarse_phase(pay, parts, core):
+def coarse_phase(pay, parts, core, *beside):
     own = lax.all_to_all(pay, "row", 0, 0, tiled=True)
+    own, *beside = lax.optimization_barrier((own, *beside))
     other = swapped(own, lambda c: c ^ 1)
     (terms,) = call(
         coarse_kernel,
@@ -519,7 +546,7 @@
         SMALL,
     )(core, parts, own, other)
     groups = [[2 * chip + which for chip in range(CHIPS)] for which in range(2)]
-    return lax.all_to_all(terms, "col", 0, 0, axis_index_groups=groups, tiled=True)
+    return lax.all_to_all(terms, "col", 0, 0, axis_index_groups=groups, tiled=True), *beside
 
 
 def per_device(schur_blocks, rigid_modes, floating, block_order, coarse_inverse, right_side):
@@ -561,24 +588,35 @@
     right = cyclic(jnp.concatenate([lines, modes[12:16]], axis=0), "col", 1)
     left = cyclic(jnp.concatenate([lines, modes[8:12]], axis=0), "col", -1)
     far = swapped(jnp.where(core[0] == 0, right[: 3 * COLS], left[: 3 * COLS]), lambda c: c ^ 1)
-    bgt, bgc, parts = call(
-        setup_kernel,
-        [SM] * 3 + [HB] * 7,
-        [shape(2 * PAY, NS, kind=bf16), shape(NS, 2 * K, kind=bf16), shape(2, CHIPS * SLOTS * SLOT, 2 * K, kind=bf16)],
-        [pltpu.VMEM((tiles, SLOT, BLK), f32) for tiles in (NB, COLS, COLS + 4, COLS + 4, 3 * COLS + 4, 3 * COLS + 4, 3 * COLS)]
+    (parts,) = call(
+        table_kernel,
+        [SM] + [HB] * 6,
+        [shape(2, CHIPS * SLOTS * SLOT, 2 * K, kind=bf16)],
+        [pltpu.VMEM((tiles, SLOT, BLK), f32) for tiles in (COLS, COLS + 4, COLS + 4, 3 * COLS + 4, 3 * COLS + 4, 3 * COLS)]
         + [
-            pltpu.VMEM((PAY, NS), f32),
+            pltpu.VMEM((CHIPS * SLOTS * SLOT, 2 * K), f32),
+            pltpu.VMEM((2, CHIPS * SLOTS * SLOT, 2 * K), bf16),
+            pltpu.SemaphoreType.DMA((16,)),
+        ],
+        10**7,
+        HB,
+    )(core, mine, down, up, right, left, far)
+    bgt, bgc = call(
+        modes_kernel,
+        [SM] * 2 + [HB] * 5,
+        [shape(2 * ROWS16, NS, kind=bf16), shape(NS, 2 * K, kind=bf16)],
+        [pltpu.VMEM((tiles, SLOT, BLK), f32) for tiles in (NB, 4, 4, 4, 4)]
+        + [
+            pltpu.VMEM((ROWS16, NS), f32),
             pltpu.VMEM((256, NS), f32),
-            pltpu.VMEM((CHIPS * SLOTS * SLOT, 2 * K), f32),
-            pltpu.VMEM((2 * PAY, NS), bf16),
+            pltpu.VMEM((2 * ROWS16, NS), bf16),
             pltpu.VMEM((NS, 2 * K), bf16),
-            pltpu.VMEM((2, CHIPS * SLOTS * SLOT, 2 * K), bf16),
             pltpu.SemaphoreType.DMA((16,)),
         ],
         10**8,
         HB,
-    )(order, masks, core, modes, mine, down, up, right, left, far)
-    came = coarse_phase(pay, parts, core)
+    )(order, masks, modes, down, up, right, left)
+    (came,) = coarse_phase(pay, parts, core)
 
     matrix = schur_blocks[0, 0]
     residual, *faces, pay = call(
@@ -592,17 +630,26 @@
 
     state = ()
     for iteration in range(ITERS):
-        north, south = cyclic(faces[1], "row", 1), cyclic(faces[0], "row", -1)
-        west, east = cyclic(faces[3], "col", 1), cyclic(faces[2], "col", -1)
-        near = (north, south, west, east)
-        came = coarse_phase(pay, parts, core)
+        which = (1, 3) if iteration + 1 == ITERS else (0, 1, 2, 3)
+        moves = (("row", 1), ("row", -1), ("col", 1), ("col", -1))
+        near = [cyclic(faces[face ^ 1], *moves[face]) for face in which]
+        mine = [faces[face] for face in which]
+        (local,) = call(
+            functools.partial(image_kernel, which),
+            [SM] + [HB] * (2 * len(which)),
+            [shape(len(which), M, K)],
+            [pltpu.VMEM((len(which), M, K), f32)] * 2 + [pltpu.SemaphoreType.DMA((16,))],
+            COST,
+            HB,
+        )(masks, *mine, *near)
+        came, local = coarse_phase(pay, parts, core, local)
         if iteration + 1 == ITERS:
             break
         first = iteration == 0
-        given = (order, masks, matrix, bgt, bgc, came, residual, *near, *faces, *state)
+        given = (order, matrix, bgt, bgc, came, residual, local, *state)
         residual, along, moved, image, done, past, *faces, pay = call(
             functools.partial(step_kernel, first),
-            [SM, SM] + [HB] * (len(given) - 2),
+            [SM] + [HB] * (len(given) - 1),
             [shape(NS, K), shape(2 * M, K), shape(NS, K), shape(2 * M, K), shape(2 * M, K), shape(SLOT, K)]
             + FACES
             + [shape(ROWS, PAY, K)],
@@ -615,12 +662,12 @@
     past, along, moved, image, done = state
     done, residual = call(
         end_kernel,
-        [SM] + [HB] * 11,
+        [HB] * 8,
         [shape(2, K, M)] * 2,
         LAST,
         10**8,
         HB,
-    )(masks, bgc, came, residual, near[1], near[3], faces[1], faces[3], past, along, moved, done)
+    )(bgc, came, residual, local, past, along, moved, done)
     return (done[None, None], residual[None, None])
 
 

time: 198 us -> 186 us (0.939)
  blocking collectives: 49.7 us -> 35 us
  Pallas kernels: 44.9 us -> 52.8 us
  starting transfers between devices: 63.3 us -> 59.4 us
  waiting for transfers between devices: 27 us -> 24.1 us
    all_to_all x3 -> x0, blocking collectives: 36 us -> none  [coarse_phase(): own = lax.all_to_all(pay, 'row', 0, 0, tiled=True)]
    all_to_all x1 -> x3, blocking collectives: 13.8 us -> 35 us  [coarse_phase(): lax.all_to_all(terms, 'col', 0, 0, axis_index_groups=groups, tiled=True)]
    ppermute x16, waiting for transfers between devices: 23.1 us -> 4.64 us  [cyclic(): lax.ppermute(value, axis, [(s, (s + steps) % count) for s in range(count)])]
    all_to_all x1 -> x4, waiting for transfers between devices: 0.59 us -> 11.6 us  [coarse_phase(): own = lax.all_to_all(pay, 'row', 0, 0, tiled=True)]
    all_to_all x3 -> x1, starting transfers between devices: 15.9 us -> 5.27 us  [coarse_phase(): lax.all_to_all(terms, 'col', 0, 0, axis_index_groups=groups, tiled=True)]
    all_to_all x1 -> x4, starting transfers between devices: 5.56 us -> 15.9 us  [coarse_phase(): own = lax.all_to_all(pay, 'row', 0, 0, tiled=True)]
    pallas_call x4 -> x8, Pallas kernels: 28.4 us -> 37.5 us  [the longest x2 19.4 us: per_device(): call(functools.partial(step_kernel, first), [SM] + [HB] * (len(given) - 1...]
    all_to_all x3 -> x1, waiting for transfers between devices: 0.01 us -> 4.84 us  [coarse_phase(): lax.all_to_all(terms, 'col', 0, 0, axis_index_groups=groups, tiled=True)]
  transfers between devices with their start and end apart: 25 -> 26, of which waited for: 14 -> 13; matrix products, arithmetic and copies ran while one was open for 2% -> 2% of each run, Pallas kernels for 4% -> 10%
where the time goes in v2:
time: 186 us; the launch traced here: 185 us
  starting transfers between devices  59.4 us (32%)
  Pallas kernels  52.8 us (28%)
  blocking collectives  35 us (19%)
  waiting for transfers between devices  24.1 us (13%)
  local copies, waits for them, and re-layouts  9.62 us (5%)
  other arithmetic  2.52 us (1%)
    all_to_all x3, blocking collectives, coarse_phase(): lax.all_to_all(terms, 'col', 0, 0, axis_index_groups=groups, tiled=True)  35 us
    ppermute x16, starting transfers between devices, cyclic(): lax.ppermute(value, axis, [(s, (s + steps) % count) for s in range(count)])  21.4 us
    pallas_call x2, Pallas kernels, per_device(): call(functools.partial(step_kernel, first), [SM] + [HB] * (len(given) - 1...  19.4 us
    ppermute x5, starting transfers between devices, swapped(): return lax.ppermute(value, 'col', [(s, partner(s)) for s in range(COLS)])  16.8 us
    all_to_all x4, starting transfers between devices, coarse_phase(): own = lax.all_to_all(pay, 'row', 0, 0, tiled=True)  15.9 us
    all_to_all x4, waiting for transfers between devices, coarse_phase(): own = lax.all_to_all(pay, 'row', 0, 0, tiled=True)  11.6 us
    pallas_call x3, Pallas kernels, per_device(): call(functools.partial(image_kernel, which), [SM] + [HB] * (2 * len(which...  8.79 us
    pallas_call x1, Pallas kernels, per_device(): call(begin_kernel, [SM] + [HB] * 5, [shape(NS, K)] + FACES + [shape(ROWS,...  8.4 us
  transfers between devices with their start and end apart: 26, of which 13 were waited for; matrix products, arithmetic and copies ran while one was open for 2% of the time, Pallas kernels for 10%

profile of v2, /device:TPU:1, one launch (start us, length us, event | category | flops | bytes accessed | tf_op | source)
XLA Modules:
  0.0 185.3 jit_solution(15130789362215680064)
XLA Ops:
  0.6 1.1 slice_bitcast_fusion
  1.7 2.8 %collective-permute-start.3 = (f32[128,512]{1,0:T(8,128)S(1)}, f32[128,512]{1,0:T(8,128)S(1)}, u32[]{:S(2)}, u32[]{:S(2)}) collective-permute-start(f32[128,512]{1,0:T(8,128)S(1)} %get-tuple-element.86), channel_id=1, source_target_pairs={{0,1},{1,2},{2,3},{3,4},{4,5},{5,6},{6,7},{7,8},{8,9},{9,10},{10,1... | collective-permute-start | bytes 786440 | tf_op jit(solution)/shard_map/ppermute | solution.py:39
  4.5 1.6 collective-permute-start.2
  6.8 0.8 broadcast_multiply_fusion
  7.6 1.0 copy.13
  8.9 4.0 %collective-permute-start.1 = (f32[36,8,128]{2,1,0:T(8,128)S(1)}, f32[36,8,128]{2,1,0:T(8,128)S(1)}, u32[]{:S(2)}, u32[]{:S(2)}) collective-permute-start(f32[36,8,128]{2,1,0:T(8,128)S(1)} %get-tuple-element.90), channel_id=1, source_target_pairs={{0,224},{32,0},{64,32},{96,64},{128,96},{160,128},{192,160},{224,1... | collective-permute-start | bytes 442376 | tf_op jit(solution)/shard_map/ppermute | solution.py:39
  12.9 0.6 pad.8.own
  13.5 0.7 add_convert_fusion.masks.refs_0_
  14.2 1.5 collective-permute-done.2.from_n
  15.7 0.7 copy-done.9
  16.4 3.3 %shard_map.77 = (f32[2048,128]{1,0:T(8,128)}, f32[8,40,128]{2,1,0:T(8,128)}) custom-call(f32[4]{0:T(128)} %add_convert_fusion.masks.refs_0_, f32[16,8,128]{2,1,0:T(8,128)} %pad.8.own, f32[2,128,512]{2,1,0:T(8,128)} %bitcast.27, f32[128,512]{1,0:T(8,128)} %copy-done.9, f32[128,512]{1,0:T(8,128)} %copy-done.8), custom_call_target="tpu_custom_call" | custom-call | flops 100000000 | bytes 1048576 | tf_op jit(solution)/shard_map/pallas_call | solution.py:563
  20.0 1.7 collective-permute-start.4
  21.7 5.6 %all-to-all-start = ((f32[8,40,128]{2,1,0:T(8,128)}), f32[8,40,128]{2,1,0:T(8,128)S(1)}, u32[]{:S(2)}, u32[]{:S(2)}) async-start(f32[8,40,128]{2,1,0:T(8,128)} %get-tuple-element.49), calls=%async_computation | async-start | bytes 327680 | tf_op jit(solution)/shard_map/all_to_all | solution.py:531
  27.4 8.0 %collective-permute-start.6 = (f32[96,8,128]{2,1,0:T(8,128)S(1)}, f32[96,8,128]{2,1,0:T(8,128)S(1)}, u32[]{:S(2)}, u32[]{:S(2)}) collective-permute-start(f32[96,8,128]{2,1,0:T(8,128)S(1)} %slice_select_fusion), channel_id=1, source_target_pairs={{0,1},{1,0},{2,3},{3,2},{4,5},{5,4},{6,7},{7,6},{8,9},{9,8},{10,11... | collective-permute-start | bytes 1179656 | tf_op jit(solution)/shard_map/ppermute | solution.py:49
  35.6 3.6 %collective-permute-start.7 = (f32[8,40,128]{2,1,0:T(8,128)S(1)}, f32[8,40,128]{2,1,0:T(8,128)S(1)}, u32[]{:S(2)}, u32[]{:S(2)}) collective-permute-start(f32[8,40,128]{2,1,0:T(8,128)S(1)} %all-to-all-done.own_v), channel_id=1, source_target_pairs={{0,1},{1,0},{2,3},{3,2},{4,5},{5,4},{6,7},{7,6},{8,9},{9,8},{10,11... | collective-permute-start | bytes 491528 | tf_op jit(solution)/shard_map/ppermute | solution.py:49
  39.3 0.8 pad_maximum_fusion.6.mine
  40.0 0.7 copy-done.7
  40.8 2.8 %shard_map.79.parts = bf16[2,640,256]{2,1,0:T(8,128)(2,1)} custom-call(s32[1]{0:T(128)} %bitcast.14.core, f32[32,8,128]{2,1,0:T(8,128)} %pad_maximum_fusion.6.mine, f32[36,8,128]{2,1,0:T(8,128)} %copy-done.6, f32[36,8,128]{2,1,0:T(8,128)} %copy-done.5, f32[100,8,128]{2,1,0:T(8,128)} %copy-done.3, f32[100,8,128]{2,1,0:T(8,128)} %copy-done.2, ...), custom_call_target="tpu_custom_call" | custom-call | flops 10000000 | bytes 1048576 | tf_op jit(solution)/shard_map/pallas_call | solution.py:591
  43.6 1.1 copy-done
  44.7 1.4 shard_map.80
  46.1 5.3 %all-to-all-start.1 = ((f32[16,40,128]{2,1,0:T(8,128)}), f32[16,40,128]{2,1,0:T(8,128)S(1)}, u32[]{:S(2)}, u32[]{:S(2)}) async-start(f32[16,40,128]{2,1,0:T(8,128)} %shard_map.80), calls=%async_computation.1 | async-start | bytes 655360 | tf_op jit(solution)/shard_map/all_to_all | solution.py:549
  51.3 3.1 %shard_map.78 = (bf16[96,2048]{1,0:T(8,128)(2,1)}, bf16[2048,256]{1,0:T(8,128)(2,1)}) custom-call(s32[16]{0:T(128)} %bitcast.32, f32[4]{0:T(128)} %add_convert_fusion.masks.refs_0_, f32[16,8,128]{2,1,0:T(8,128)} %pad.8.own, f32[36,8,128]{2,1,0:T(8,128)} %copy-done.6, f32[36,8,128]{2,1,0:T(8,128)} %copy-done.5, f32[100,8,128]{2,1,0:T(8,128)} %copy-done.3, ...), custom_call_target="tpu_custom_call" | custom-call | flops 100000000 | bytes 1048576 | tf_op jit(solution)/shard_map/pallas_call | solution.py:604
  54.5 4.8 %all-to-all-done.1.came = f32[16,40,128]{2,1,0:T(8,128)S(1)} async-done(((f32[16,40,128]{2,1,0:T(8,128)}), f32[16,40,128]{2,1,0:T(8,128)S(1)}, u32[]{:S(2)}, u32[]{:S(2)}) %all-to-all-start.1) | async-done | bytes 327712 | tf_op jit(solution)/shard_map/all_to_all | solution.py:549
  59.3 0.7 copy-done.4
  60.1 8.4 %shard_map.81 = (f32[2048,128]{1,0:T(8,128)}, f32[512,128]{1,0:T(8,128)}, f32[512,128]{1,0:T(8,128)}, f32[512,128]{1,0:T(8,128)}, f32[512,128]{1,0:T(8,128)}, /*index=5*/f32[8,40,128]{2,1,0:T(8,128)}) custom-call(s32[16]{0:T(128)} %bitcast.33, bf16[2048,2048]{1,0:T(8,128)(2,1)} %bitcast.24, bf16[96,2048]{1,0:T(8,128)(2,1)} %get-tuple-element.48.bgt.refs_2_, ...), custom_call_target="tpu_custom_call" | custom-call | flops 2000000000 | bytes 1048576 | tf_op jit(solution)/shard_map/pallas_call | solution.py:622
  68.6 1.5 collective-permute-start.8
  70.0 2.7 %collective-permute-start.11 = (f32[512,128]{1,0:T(8,128)}, f32[512,128]{1,0:T(8,128)S(1)}, u32[]{:S(2)}, u32[]{:S(2)}) collective-permute-start(f32[512,128]{1,0:T(8,128)} %get-tuple-element.54.refs_3_), channel_id=1, source_target_pairs={{0,31},{1,0},{2,1},{3,2},{4,3},{5,4},{6,5},{7,6},{8,7},{9,8},{10,9... | collective-permute-start | bytes 786440 | tf_op jit(solution)/shard_map/ppermute | solution.py:39
  72.7 3.4 %all-to-all-start.2 = ((f32[8,40,128]{2,1,0:T(8,128)}), f32[8,40,128]{2,1,0:T(8,128)S(1)}, u32[]{:S(2)}, u32[]{:S(2)}) async-start(f32[8,40,128]{2,1,0:T(8,128)} %get-tuple-element.51), calls=%async_computation.2 | async-start | bytes 327680 | tf_op jit(solution)/shard_map/all_to_all | solution.py:531
  76.1 1.1 collective-permute-done.11.refs_8_
  77.2 0.7 copy-done.14
  77.9 0.7 copy-done.16
  78.6 3.0 %shard_map.82.refs_6_ = f32[4,512,128]{2,1,0:T(8,128)} custom-call(f32[4]{0:T(128)} %add_convert_fusion.masks.refs_0_, f32[512,128]{1,0:T(8,128)} %get-tuple-element.52.refs_1_, f32[512,128]{1,0:T(8,128)} %get-tuple-element.53.refs_2_, f32[512,128]{1,0:T(8,128)} %get-tuple-element.54.refs_3_, f32[512,128]{1,0:T(8,128)} %get-tuple-element.55.refs_4_, ...), custom_call_target="tpu_custom_call" | custom-call | flops 20000000000 | bytes 1048576 | tf_op jit(solution)/shard_map/pallas_call | solution.py:637
  81.6 3.3 %all-to-all-done.2.own_v = f32[8,40,128]{2,1,0:T(8,128)S(1)} async-done(((f32[8,40,128]{2,1,0:T(8,128)}), f32[8,40,128]{2,1,0:T(8,128)S(1)}, u32[]{:S(2)}, u32[]{:S(2)}) %all-to-all-start.2) | async-done | bytes 163872 | tf_op jit(solution)/shard_map/all_to_all | solution.py:531
  84.9 1.8 collective-permute-start.12
  86.7 1.0 collective-permute-done.12.other_v
  87.7 0.7 shard_map.83
  88.5 11.8 %all_to_all.40.refs_4_ = f32[16,40,128]{2,1,0:T(8,128)} all-to-all(f32[16,40,128]{2,1,0:T(8,128)S(1)} %shard_map.83), channel_id=1, replica_groups={{0,2,4,6,8,10,12,14,16,18,20,22,24,26,28,30},{1,3,5,7,9,11,13,15,17,19,..., dimensions={0} | all-to-all | bytes 655360 | tf_op jit(solution)/shard_map/all_to_all | solution.py:549
  100.3 9.3 %shard_map.84 = (f32[2048,128]{1,0:T(8,128)}, f32[1024,128]{1,0:T(8,128)}, f32[2048,128]{1,0:T(8,128)}, f32[1024,128]{1,0:T(8,128)}, f32[1024,128]{1,0:T(8,128)}...) custom-call(s32[16]{0:T(128)} %bitcast.34, ...), custom_call_target="tpu_custom_call" | custom-call | flops 2000000000 | bytes 1048576 | tf_op jit(solution)/shard_map/pallas_call | solution.py:650
  109.6 0.4 collective-permute-start.14
  110.1 1.1 collective-permute-start.13
  111.2 2.7 %collective-permute-start.16 = (f32[512,128]{1,0:T(8,128)}, f32[512,128]{1,0:T(8,128)S(1)}, u32[]{:S(2)}, u32[]{:S(2)}) collective-permute-start(f32[512,128]{1,0:T(8,128)} %get-tuple-element.62.refs_3_), channel_id=1, source_target_pairs={{0,31},{1,0},{2,1},{3,2},{4,3},{5,4},{6,5},{7,6},{8,7},{9,8},{10,9... | collective-permute-start | bytes 786440 | tf_op jit(solution)/shard_map/ppermute | solution.py:39
  113.9 3.4 %all-to-all-start.4 = ((f32[8,40,128]{2,1,0:T(8,128)}), f32[8,40,128]{2,1,0:T(8,128)S(1)}, u32[]{:S(2)}, u32[]{:S(2)}) async-start(f32[8,40,128]{2,1,0:T(8,128)} %get-tuple-element.59), calls=%async_computation.4 | async-start | bytes 327680 | tf_op jit(solution)/shard_map/all_to_all | solution.py:531
  117.3 1.1 collective-permute-done.16.refs_8_
  118.4 0.7 copy-done.15
  119.1 0.7 copy-done.17
  119.9 3.1 %shard_map.85.refs_6_ = f32[4,512,128]{2,1,0:T(8,128)} custom-call(f32[4]{0:T(128)} %add_convert_fusion.masks.refs_0_, f32[512,128]{1,0:T(8,128)} %get-tuple-element.60.refs_1_, f32[512,128]{1,0:T(8,128)} %get-tuple-element.61.refs_2_, f32[512,128]{1,0:T(8,128)} %get-tuple-element.62.refs_3_, f32[512,128]{1,0:T(8,128)} %get-tuple-element.63.refs_4_, ...), custom_call_target="tpu_custom_call" | custom-call | flops 20000000000 | bytes 1048576 | tf_op jit(solution)/shard_map/pallas_call | solution.py:637
  122.9 3.1 %all-to-all-done.4.own_v = f32[8,40,128]{2,1,0:T(8,128)S(1)} async-done(((f32[8,40,128]{2,1,0:T(8,128)}), f32[8,40,128]{2,1,0:T(8,128)S(1)}, u32[]{:S(2)}, u32[]{:S(2)}) %all-to-all-start.4) | async-done | bytes 163872 | tf_op jit(solution)/shard_map/all_to_all | solution.py:531
  126.0 1.9 %collective-permute-start.17 = (f32[8,40,128]{2,1,0:T(8,128)S(1)}, f32[8,40,128]{2,1,0:T(8,128)S(1)}, u32[]{:S(2)}, u32[]{:S(2)}) collective-permute-start(f32[8,40,128]{2,1,0:T(8,128)S(1)} %all-to-all-done.4.own_v), channel_id=1, source_target_pairs={{0,1},{1,0},{2,3},{3,2},{4,5},{5,4},{6,7},{7,6},{8,9},{9,8},{10,11... | collective-permute-start | bytes 491528 | tf_op jit(solution)/shard_map/ppermute | solution.py:49
  127.9 1.0 collective-permute-done.17.other_v
  129.0 0.7 shard_map.86
  129.7 11.9 %all_to_all.41.refs_4_ = f32[16,40,128]{2,1,0:T(8,128)} all-to-all(f32[16,40,128]{2,1,0:T(8,128)S(1)} %shard_map.86), channel_id=1, replica_groups={{0,2,4,6,8,10,12,14,16,18,20,22,24,26,28,30},{1,3,5,7,9,11,13,15,17,19,..., dimensions={0} | all-to-all | bytes 655360 | tf_op jit(solution)/shard_map/all_to_all | solution.py:549
  141.6 10.1 %shard_map.87 = (f32[2048,128]{1,0:T(8,128)}, f32[1024,128]{1,0:T(8,128)}, f32[2048,128]{1,0:T(8,128)}, f32[1024,128]{1,0:T(8,128)}, f32[1024,128]{1,0:T(8,128)}...) custom-call(s32[16]{0:T(128)} %bitcast.35, ...), custom_call_target="tpu_custom_call" | custom-call | flops 2000000000 | bytes 1048576 | tf_op jit(solution)/shard_map/pallas_call | solution.py:650
  151.7 0.5 collective-permute-start.18
  152.2 2.2 %collective-permute-start.19 = (f32[512,128]{1,0:T(8,128)}, f32[512,128]{1,0:T(8,128)S(1)}, u32[]{:S(2)}, u32[]{:S(2)}) collective-permute-start(f32[512,128]{1,0:T(8,128)} %get-tuple-element.76), channel_id=1, source_target_pairs={{0,31},{1,0},{2,1},{3,2},{4,3},{5,4},{6,5},{7,6},{8,7},{9,8},{10,9... | collective-permute-start | bytes 786440 | tf_op jit(solution)/shard_map/ppermute | solution.py:39
  154.4 3.6 %all-to-all-start.6 = ((f32[8,40,128]{2,1,0:T(8,128)}), f32[8,40,128]{2,1,0:T(8,128)S(1)}, u32[]{:S(2)}, u32[]{:S(2)}) async-start(f32[8,40,128]{2,1,0:T(8,128)} %get-tuple-element.72), calls=%async_computation.6 | async-start | bytes 327680 | tf_op jit(solution)/shard_map/all_to_all | solution.py:531
  158.0 0.9 collective-permute-done.19.refs_4_
  158.9 0.7 copy-done.19
  159.6 2.7 %shard_map.88.local = f32[2,512,128]{2,1,0:T(8,128)} custom-call(f32[4]{0:T(128)} %add_convert_fusion.masks.refs_0_, f32[512,128]{1,0:T(8,128)} %get-tuple-element.73.refs_1_, f32[512,128]{1,0:T(8,128)} %get-tuple-element.74.refs_2_, f32[512,128]{1,0:T(8,128)} %copy-done.18, f32[512,128]{1,0:T(8,128)} %copy-done.19), custom_call_target="tpu_custom_call" | custom-call | flops 20000000000 | bytes 1048576 | tf_op jit(solution)/shard_map/pallas_call | solution.py:637
  162.3 5.0 %all-to-all-done.6.own_v = f32[8,40,128]{2,1,0:T(8,128)S(1)} async-done(((f32[8,40,128]{2,1,0:T(8,128)}), f32[8,40,128]{2,1,0:T(8,128)S(1)}, u32[]{:S(2)}, u32[]{:S(2)}) %all-to-all-start.6) | async-done | bytes 163872 | tf_op jit(solution)/shard_map/all_to_all | solution.py:531
  167.3 1.4 collective-permute-start.20
  168.7 1.0 collective-permute-done.20.other_v
  169.7 0.7 shard_map.89
  170.5 11.3 %all_to_all.42.came = f32[16,40,128]{2,1,0:T(8,128)} all-to-all(f32[16,40,128]{2,1,0:T(8,128)S(1)} %shard_map.89), channel_id=1, replica_groups={{0,2,4,6,8,10,12,14,16,18,20,22,24,26,28,30},{1,3,5,7,9,11,13,15,17,19,..., dimensions={0} | all-to-all | bytes 655360 | tf_op jit(solution)/shard_map/all_to_all | solution.py:549
  181.8 3.4 %shard_map.90 = (f32[2,128,512]{2,1,0:T(8,128)}, f32[2,128,512]{2,1,0:T(8,128)}) custom-call(bf16[2048,256]{1,0:T(8,128)(2,1)} %get-tuple-element.47.bgc.refs_3_, f32[16,40,128]{2,1,0:T(8,128)} %all_to_all.42.came, f32[2048,128]{1,0:T(8,128)} %get-tuple-element.78.residual, f32[2,512,128]{2,1,0:T(8,128)} %shard_map.88.local, ...), custom_call_target="tpu_custom_call" | custom-call | flops 100000000 | bytes 1048576 | tf_op jit(solution)/shard_map/pallas_call | solution.py:663
  (60 shorter events, 1.1 us)
Async XLA Ops:
  1.7 12.5 %collective-permute-start.3 = (f32[128,512]{1,0:T(8,128)S(1)}, f32[128,512]{1,0:T(8,128)S(1)}, u32[]{:S(2)}, u32[]{:S(2)}) collective-permute-start(f32[128,512]{1,0:T(8,128)S(1)} %get-tuple-element.86), channel_id=1, source_target_pairs={{0,1},{1,2},{2,3},{3,4},{4,5},{5,6},{6,7},{7,8},{8,9},{9,10},{10,1... | collective-permute-start | bytes 786440 | tf_op jit(solution)/shard_map/ppermute | solution.py:39
  4.5 11.2 %collective-permute-start.2 = (f32[128,512]{1,0:T(8,128)S(1)}, f32[128,512]{1,0:T(8,128)S(1)}, u32[]{:S(2)}, u32[]{:S(2)}) collective-permute-start(f32[128,512]{1,0:T(8,128)S(1)} %get-tuple-element.87), channel_id=1, source_target_pairs={{0,32},{32,64},{64,96},{96,128},{128,160},{160,192},{192,224},{224... | collective-permute-start | bytes 786440 | tf_op jit(solution)/shard_map/ppermute | solution.py:39
  8.9 10.8 %collective-permute-start.1 = (f32[36,8,128]{2,1,0:T(8,128)S(1)}, f32[36,8,128]{2,1,0:T(8,128)S(1)}, u32[]{:S(2)}, u32[]{:S(2)}) collective-permute-start(f32[36,8,128]{2,1,0:T(8,128)S(1)} %get-tuple-element.90), channel_id=1, source_target_pairs={{0,224},{32,0},{64,32},{96,64},{128,96},{160,128},{192,160},{224,1... | collective-permute-start | bytes 442376 | tf_op jit(solution)/shard_map/ppermute | solution.py:39
  12.9 6.8 %collective-permute-start = (f32[36,8,128]{2,1,0:T(8,128)S(1)}, f32[36,8,128]{2,1,0:T(8,128)S(1)}, u32[]{:S(2)}, u32[]{:S(2)}) collective-permute-start(f32[36,8,128]{2,1,0:T(8,128)S(1)} %get-tuple-element.91), channel_id=1, source_target_pairs={{0,32},{32,64},{64,96},{96,128},{128,160},{160,192},{192,224},{224... | collective-permute-start | bytes 442376 | tf_op jit(solution)/shard_map/ppermute | solution.py:39
  14.2 1.5 copy-start.8
  15.7 0.7 copy-start.9
  19.7 20.3 %copy-start.5 = (f32[36,8,128]{2,1,0:T(8,128)}, f32[36,8,128]{2,1,0:T(8,128)S(1)}, u32[]{:S(2)}) copy-start(f32[36,8,128]{2,1,0:T(8,128)S(1)} %collective-permute-done.1.up) | copy-start | bytes 442372
  19.7 20.3 %copy-start.6 = (f32[36,8,128]{2,1,0:T(8,128)}, f32[36,8,128]{2,1,0:T(8,128)S(1)}, u32[]{:S(2)}) copy-start(f32[36,8,128]{2,1,0:T(8,128)S(1)} %collective-permute-done.down) | copy-start | bytes 442372
  19.9 7.5 %collective-permute-start.5 = (f32[100,8,128]{2,1,0:T(8,128)S(1)}, f32[100,8,128]{2,1,0:T(8,128)S(1)}, u32[]{:S(2)}, u32[]{:S(2)}) collective-permute-start(f32[100,8,128]{2,1,0:T(8,128)S(1)} %get-tuple-element.88), channel_id=1, source_target_pairs={{0,31},{1,0},{2,1},{3,2},{4,3},{5,4},{6,5},{7,6},{8,7},{9,8},{10,9... | collective-permute-start | bytes 1228808 | tf_op jit(solution)/shard_map/ppermute | solution.py:39
  20.0 7.4 %collective-permute-start.4 = (f32[100,8,128]{2,1,0:T(8,128)S(1)}, f32[100,8,128]{2,1,0:T(8,128)S(1)}, u32[]{:S(2)}, u32[]{:S(2)}) collective-permute-start(f32[100,8,128]{2,1,0:T(8,128)S(1)} %get-tuple-element.89), channel_id=1, source_target_pairs={{0,1},{1,2},{2,3},{3,4},{4,5},{5,6},{6,7},{7,8},{8,9},{9,10},{10,1... | collective-permute-start | bytes 1228808 | tf_op jit(solution)/shard_map/ppermute | solution.py:39
  21.7 13.9 %all-to-all-start = ((f32[8,40,128]{2,1,0:T(8,128)}), f32[8,40,128]{2,1,0:T(8,128)S(1)}, u32[]{:S(2)}, u32[]{:S(2)}) async-start(f32[8,40,128]{2,1,0:T(8,128)} %get-tuple-element.49), calls=%async_computation | async-start | bytes 327680 | tf_op jit(solution)/shard_map/all_to_all | solution.py:531
  27.3 12.7 %copy-start.2 = (f32[100,8,128]{2,1,0:T(8,128)}, f32[100,8,128]{2,1,0:T(8,128)S(1)}, u32[]{:S(2)}) copy-start(f32[100,8,128]{2,1,0:T(8,128)S(1)} %collective-permute-done.5.left) | copy-start | bytes 1228804
  27.3 12.7 %copy-start.3 = (f32[100,8,128]{2,1,0:T(8,128)}, f32[100,8,128]{2,1,0:T(8,128)S(1)}, u32[]{:S(2)}) copy-start(f32[100,8,128]{2,1,0:T(8,128)S(1)} %collective-permute-done.4.right) | copy-start | bytes 1228804
  27.4 12.6 %collective-permute-start.6 = (f32[96,8,128]{2,1,0:T(8,128)S(1)}, f32[96,8,128]{2,1,0:T(8,128)S(1)}, u32[]{:S(2)}, u32[]{:S(2)}) collective-permute-start(f32[96,8,128]{2,1,0:T(8,128)S(1)} %slice_select_fusion), channel_id=1, source_target_pairs={{0,1},{1,0},{2,3},{3,2},{4,5},{5,4},{6,7},{7,6},{8,9},{9,8},{10,11... | collective-permute-start | bytes 1179656 | tf_op jit(solution)/shard_map/ppermute | solution.py:49
  35.6 8.0 %collective-permute-start.7 = (f32[8,40,128]{2,1,0:T(8,128)S(1)}, f32[8,40,128]{2,1,0:T(8,128)S(1)}, u32[]{:S(2)}, u32[]{:S(2)}) collective-permute-start(f32[8,40,128]{2,1,0:T(8,128)S(1)} %all-to-all-done.own_v), channel_id=1, source_target_pairs={{0,1},{1,0},{2,3},{3,2},{4,5},{5,4},{6,7},{7,6},{8,9},{9,8},{10,11... | collective-permute-start | bytes 491528 | tf_op jit(solution)/shard_map/ppermute | solution.py:49
  40.0 0.8 copy-start.7
  43.6 1.1 copy-start
  46.1 13.3 %all-to-all-start.1 = ((f32[16,40,128]{2,1,0:T(8,128)}), f32[16,40,128]{2,1,0:T(8,128)S(1)}, u32[]{:S(2)}, u32[]{:S(2)}) async-start(f32[16,40,128]{2,1,0:T(8,128)} %shard_map.80), calls=%async_computation.1 | async-start | bytes 655360 | tf_op jit(solution)/shard_map/all_to_all | solution.py:549
  59.3 0.7 copy-start.4
  68.5 7.6 %collective-permute-start.9 = (f32[512,128]{1,0:T(8,128)}, f32[512,128]{1,0:T(8,128)S(1)}, u32[]{:S(2)}, u32[]{:S(2)}) collective-permute-start(f32[512,128]{1,0:T(8,128)} %get-tuple-element.52.refs_1_), channel_id=1, source_target_pairs={{0,224},{32,0},{64,32},{96,64},{128,96},{160,128},{192,160},{224,1... | collective-permute-start | bytes 786440 | tf_op jit(solution)/shard_map/ppermute | solution.py:39
  68.6 7.6 %collective-permute-start.8 = (f32[512,128]{1,0:T(8,128)}, f32[512,128]{1,0:T(8,128)S(1)}, u32[]{:S(2)}, u32[]{:S(2)}) collective-permute-start(f32[512,128]{1,0:T(8,128)} %get-tuple-element.53.refs_2_), channel_id=1, source_target_pairs={{0,32},{32,64},{64,96},{96,128},{128,160},{160,192},{192,224},{224... | collective-permute-start | bytes 786440 | tf_op jit(solution)/shard_map/ppermute | solution.py:39
  70.0 7.2 %collective-permute-start.11 = (f32[512,128]{1,0:T(8,128)}, f32[512,128]{1,0:T(8,128)S(1)}, u32[]{:S(2)}, u32[]{:S(2)}) collective-permute-start(f32[512,128]{1,0:T(8,128)} %get-tuple-element.54.refs_3_), channel_id=1, source_target_pairs={{0,31},{1,0},{2,1},{3,2},{4,3},{5,4},{6,5},{7,6},{8,7},{9,8},{10,9... | collective-permute-start | bytes 786440 | tf_op jit(solution)/shard_map/ppermute | solution.py:39
  72.7 4.5 %collective-permute-start.10 = (f32[512,128]{1,0:T(8,128)}, f32[512,128]{1,0:T(8,128)S(1)}, u32[]{:S(2)}, u32[]{:S(2)}) collective-permute-start(f32[512,128]{1,0:T(8,128)} %get-tuple-element.55.refs_4_), channel_id=1, source_target_pairs={{0,1},{1,2},{2,3},{3,4},{4,5},{5,6},{6,7},{7,8},{8,9},{9,10},{10,1... | collective-permute-start | bytes 786440 | tf_op jit(solution)/shard_map/ppermute | solution.py:39
  72.7 12.2 %all-to-all-start.2 = ((f32[8,40,128]{2,1,0:T(8,128)}), f32[8,40,128]{2,1,0:T(8,128)S(1)}, u32[]{:S(2)}, u32[]{:S(2)}) async-start(f32[8,40,128]{2,1,0:T(8,128)} %get-tuple-element.51), calls=%async_computation.2 | async-start | bytes 327680 | tf_op jit(solution)/shard_map/all_to_all | solution.py:531
  76.1 11.7 %copy-start.1 = (bf16[2,640,256]{2,1,0:T(8,128)(2,1)S(1)}, bf16[2,640,256]{2,1,0:T(8,128)(2,1)}, u32[]{:S(2)}) copy-start(bf16[2,640,256]{2,1,0:T(8,128)(2,1)} %shard_map.79.parts) | copy-start | bytes 1966084
  76.1 1.1 copy-start.10
  76.1 1.1 copy-start.12
  77.2 0.7 copy-start.14
  77.9 0.7 copy-start.16
  84.9 2.8 %collective-permute-start.12 = (f32[8,40,128]{2,1,0:T(8,128)S(1)}, f32[8,40,128]{2,1,0:T(8,128)S(1)}, u32[]{:S(2)}, u32[]{:S(2)}) collective-permute-start(f32[8,40,128]{2,1,0:T(8,128)S(1)} %all-to-all-done.2.own_v), channel_id=1, source_target_pairs={{0,1},{1,0},{2,3},{3,2},{4,5},{5,4},{6,7},{7,6},{8,9},{9,8},{10,11... | collective-permute-start | bytes 491528 | tf_op jit(solution)/shard_map/ppermute | solution.py:49
  109.6 7.7 %collective-permute-start.14 = (f32[512,128]{1,0:T(8,128)}, f32[512,128]{1,0:T(8,128)S(1)}, u32[]{:S(2)}, u32[]{:S(2)}) collective-permute-start(f32[512,128]{1,0:T(8,128)} %get-tuple-element.60.refs_1_), channel_id=1, source_target_pairs={{0,224},{32,0},{64,32},{96,64},{128,96},{160,128},{192,160},{224,1... | collective-permute-start | bytes 786440 | tf_op jit(solution)/shard_map/ppermute | solution.py:39
  110.1 7.2 %collective-permute-start.13 = (f32[512,128]{1,0:T(8,128)}, f32[512,128]{1,0:T(8,128)S(1)}, u32[]{:S(2)}, u32[]{:S(2)}) collective-permute-start(f32[512,128]{1,0:T(8,128)} %get-tuple-element.61.refs_2_), channel_id=1, source_target_pairs={{0,32},{32,64},{64,96},{96,128},{128,160},{160,192},{192,224},{224... | collective-permute-start | bytes 786440 | tf_op jit(solution)/shard_map/ppermute | solution.py:39
  111.2 7.2 %collective-permute-start.16 = (f32[512,128]{1,0:T(8,128)}, f32[512,128]{1,0:T(8,128)S(1)}, u32[]{:S(2)}, u32[]{:S(2)}) collective-permute-start(f32[512,128]{1,0:T(8,128)} %get-tuple-element.62.refs_3_), channel_id=1, source_target_pairs={{0,31},{1,0},{2,1},{3,2},{4,3},{5,4},{6,5},{7,6},{8,7},{9,8},{10,9... | collective-permute-start | bytes 786440 | tf_op jit(solution)/shard_map/ppermute | solution.py:39
  113.9 4.5 %collective-permute-start.15 = (f32[512,128]{1,0:T(8,128)}, f32[512,128]{1,0:T(8,128)S(1)}, u32[]{:S(2)}, u32[]{:S(2)}) collective-permute-start(f32[512,128]{1,0:T(8,128)} %get-tuple-element.63.refs_4_), channel_id=1, source_target_pairs={{0,1},{1,2},{2,3},{3,4},{4,5},{5,6},{6,7},{7,8},{8,9},{9,10},{10,1... | collective-permute-start | bytes 786440 | tf_op jit(solution)/shard_map/ppermute | solution.py:39
  113.9 12.1 %all-to-all-start.4 = ((f32[8,40,128]{2,1,0:T(8,128)}), f32[8,40,128]{2,1,0:T(8,128)S(1)}, u32[]{:S(2)}, u32[]{:S(2)}) async-start(f32[8,40,128]{2,1,0:T(8,128)} %get-tuple-element.59), calls=%async_computation.4 | async-start | bytes 327680 | tf_op jit(solution)/shard_map/all_to_all | solution.py:531
  117.3 1.1 copy-start.11
  117.3 1.1 copy-start.13
  118.4 0.7 copy-start.15
  119.1 0.7 copy-start.17
  126.0 2.9 %collective-permute-start.17 = (f32[8,40,128]{2,1,0:T(8,128)S(1)}, f32[8,40,128]{2,1,0:T(8,128)S(1)}, u32[]{:S(2)}, u32[]{:S(2)}) collective-permute-start(f32[8,40,128]{2,1,0:T(8,128)S(1)} %all-to-all-done.4.own_v), channel_id=1, source_target_pairs={{0,1},{1,0},{2,3},{3,2},{4,5},{5,4},{6,7},{7,6},{8,9},{9,8},{10,11... | collective-permute-start | bytes 491528 | tf_op jit(solution)/shard_map/ppermute | solution.py:49
  151.7 6.3 %collective-permute-start.18 = (f32[512,128]{1,0:T(8,128)}, f32[512,128]{1,0:T(8,128)S(1)}, u32[]{:S(2)}, u32[]{:S(2)}) collective-permute-start(f32[512,128]{1,0:T(8,128)} %get-tuple-element.75), channel_id=1, source_target_pairs={{0,224},{32,0},{64,32},{96,64},{128,96},{160,128},{192,160},{224,1... | collective-permute-start | bytes 786440 | tf_op jit(solution)/shard_map/ppermute | solution.py:39
  152.2 6.7 %collective-permute-start.19 = (f32[512,128]{1,0:T(8,128)}, f32[512,128]{1,0:T(8,128)S(1)}, u32[]{:S(2)}, u32[]{:S(2)}) collective-permute-start(f32[512,128]{1,0:T(8,128)} %get-tuple-element.76), channel_id=1, source_target_pairs={{0,31},{1,0},{2,1},{3,2},{4,3},{5,4},{6,5},{7,6},{8,7},{9,8},{10,9... | collective-permute-start | bytes 786440 | tf_op jit(solution)/shard_map/ppermute | solution.py:39
  154.4 12.9 %all-to-all-start.6 = ((f32[8,40,128]{2,1,0:T(8,128)}), f32[8,40,128]{2,1,0:T(8,128)S(1)}, u32[]{:S(2)}, u32[]{:S(2)}) async-start(f32[8,40,128]{2,1,0:T(8,128)} %get-tuple-element.72), calls=%async_computation.6 | async-start | bytes 327680 | tf_op jit(solution)/shard_map/all_to_all | solution.py:531
  158.0 0.9 copy-start.18
  158.9 0.7 copy-start.19
  167.3 2.5 %collective-permute-start.20 = (f32[8,40,128]{2,1,0:T(8,128)S(1)}, f32[8,40,128]{2,1,0:T(8,128)S(1)}, u32[]{:S(2)}, u32[]{:S(2)}) collective-permute-start(f32[8,40,128]{2,1,0:T(8,128)S(1)} %all-to-all-done.6.own_v), channel_id=1, source_target_pairs={{0,1},{1,0},{2,3},{3,2},{4,5},{5,4},{6,7},{7,6},{8,9},{9,8},{10,11... | collective-permute-start | bytes 491528 | tf_op jit(solution)/shard_map/ppermute | solution.py:49

commit v3 on v2

--- a/solution.py
+++ b/solution.py
@@ -23,6 +23,7 @@
 TERMS = ((0, 0), (0, 1), (1, 0), (1, 1), (0, 2), (2, 0))
 TALL = 1024
 CHIPS = 16
+HALF = COLS // 2
 COST = 2 * 10**10
 
 f32 = jnp.float32
@@ -89,52 +90,49 @@
 
 
 def start_kernel(
-    masks, own, side, from_n, from_w, local, pay,
-    own_v, side_v, near_v, local_v, full, halves, pay_v, sems,
+    masks, own, near_s, near_e, side, turned, pay,
+    own_v, near_v, side_v, turned_v, full, halves, pay_v, sems,
 ):
     copies = Copies(sems)
-    ready = [copies.start(own, own_v), copies.start(side.at[0], side_v.at[0]), copies.start(side.at[1], side_v.at[1])]
-    near = [copies.start(from_n, near_v.at[0]), copies.start(from_w, near_v.at[1])]
+    ready = [copies.start(own, own_v), copies.start(near_s, near_v.at[0]), copies.start(near_e, near_v.at[1])]
+    faces = [copies.start(side.at[index], side_v.at[index]) for index in range(2)]
     full[...] = jnp.zeros_like(full)
+    for index in range(2):
+        wait(faces[index : index + 1])
+        for block in range(M // BLK):
+            rows = slice(M * index + BLK * block, M * index + BLK * (block + 1))
+            value = side_v[index, :, BLK * block : BLK * (block + 1)].T
+            turned_v[index, BLK * block : BLK * (block + 1), :] = value
+            high, low = parts_of(value, 2)
+            halves[rows, :K] = high
+            halves[rows, K:] = low
+        copies.out(turned_v.at[index], turned.at[index])
     wait(ready)
-    own_modes(full, own_v, masks)
-    for pair in range(2):
-        wait(near[pair : pair + 1])
-        for kind in range(2):
-            face = 2 * pair + kind
-            for block in range(M // BLK):
-                inside = slice(BLK * block, BLK * (block + 1))
-                rows = slice(M * face + BLK * block, M * face + BLK * (block + 1))
-                if kind:
-                    turned = side_v[pair, :, inside].T
-                else:
-                    turned = near_v[pair, :, inside].T * -masks[face]
-                local_v[rows, :] = turned
-                high, low = parts_of(turned, 2)
-                halves[rows, :K] = high
-                halves[rows, K:] = low
-        wide = pl.ds(2 * M * pair, 2 * M)
-        copies.out(local_v.at[wide], local.at[wide])
+    for index in range(2):
+        rows = slice(SLOT * 2 * (index + 1), SLOT * (2 * index + 3))
+        for block in range(M // BLK):
+            lanes = slice(M * index + BLK * block, M * index + BLK * (block + 1))
+            full[0:SLOT, lanes] = own_v[M // BLK * (2 * index + 1) + block]
+            full[rows, lanes] = near_v[index, block] * -masks[2 * index + 1]
     pieces = jnp.concatenate(parts_of(full[...], 2), axis=0)
     d = jnp.dot(pieces, halves[...], preferred_element_type=f32)
-    value = d[0:16, :K] + d[0:16, K:] + d[16:32, :K] + d[16:32, K:]
-    pay_v[...] = jnp.zeros_like(pay_v)
-    pay_v[0:SLOT, :] = value[0:SLOT]
+    pay_v[...] = (d[:ROWS16, :K] + d[:ROWS16, K:] + d[ROWS16:, :K] + d[ROWS16:, K:])[0:PAY]
     for index in range(ROWS):
         copies.out(pay_v, pay.at[index])
     copies.close()
 
 
 def modes_kernel(
-    order, masks, own, down, up, right, left, bgt, bgc,
-    own_v, down_v, up_v, right_v, left_v, full, turned, bgt_v, bgc_v, sems,
+    order, masks, own, down, up, right, left, from_n, from_w, bgt, bgc, other,
+    own_v, down_v, up_v, right_v, left_v, full, turned, bgt_v, bgc_v, near_v, other_v, sems,
 ):
     copies = Copies(sems)
     ready = [copies.start(own, own_v)]
-    for source, target in ((down, down_v), (up, up_v)):
-        ready.append(copies.start(source.at[pl.ds(COLS, 4)], target))
-    for source, target in ((right, right_v), (left, left_v)):
-        ready.append(copies.start(source.at[pl.ds(3 * COLS, 4)], target))
+    for source, target in ((up, up_v), (left, left_v)):
+        ready.append(copies.start(source, target))
+    ready.append(copies.start(down.at[pl.ds(HALF, 4)], down_v))
+    ready.append(copies.start(right.at[pl.ds(3 * HALF, 4)], right_v))
+    sides = [copies.start(from_n, near_v.at[0]), copies.start(from_w, near_v.at[1])]
     full[...] = jnp.zeros_like(full)
     wait(ready)
     own_modes(full, own_v, masks)
@@ -157,6 +155,12 @@
         for index, piece in enumerate(parts_of(full[:, pl.ds(at, BLK)], 2)):
             bgt_v[ROWS16 * index : ROWS16 * (index + 1), BLK * block : BLK * (block + 1)] = piece
     copies.out(bgt_v, bgt)
+    for index in range(2):
+        wait(sides[index : index + 1])
+        for block in range(M // BLK):
+            inside = slice(BLK * block, BLK * (block + 1))
+            other_v[index, inside, :] = near_v[index, :, inside].T * -masks[2 * index]
+        copies.out(other_v.at[index], other.at[index])
     copies.close()
 
 
@@ -175,13 +179,22 @@
         at = 2 * target + core[0]
         picks = ((0, at), (1, at), (2, at), (0, jnp.maximum(at - 1, 0)), (0, jnp.minimum(at + 1, COLS - 1)))
         for slot, (line, column) in enumerate(picks):
-            w, e, f = (ref[COLS * line + column] for ref in (right_v, left_v, far_v))
-            m = (mine_v[column], down_v[column], up_v[column])[line]
-            inner = jnp.where(half, jnp.where(first, w, f), jnp.where(first, m, w))
-            outer = jnp.where(half, jnp.where(first, e, m), jnp.where(first, f, e))
+            two = lax.div(column, 2)
+            w, e, f = (ref[HALF * line + two] for ref in (right_v, left_v, far_v))
+            m = (mine_v[two], down_v[two], up_v[two])[line]
+            on_left = (core[0] == 0) == (slot < 3)
+            pairs = ((jnp.where(first, w, f), jnp.where(first, m, w)), (jnp.where(first, e, m), jnp.where(first, f, e)))
+            turned = [
+                jnp.where(
+                    half,
+                    jnp.where(on_left, a, pltpu.roll(a, SLOT * ROWS, 1)),
+                    jnp.where(on_left, pltpu.roll(b, SLOT * ROWS, 1), b),
+                )
+                for a, b in pairs
+            ]
             rows = pl.ds(pl.multiple_of((target * SLOTS + slot) * SLOT, SLOT), SLOT)
-            table[rows, :K] = inner
-            table[rows, K:] = outer
+            table[rows, :K] = turned[0]
+            table[rows, K:] = turned[1]
 
     for index, piece in enumerate(parts_of(table[...], 2)):
         parts_v[index] = piece
@@ -307,12 +320,12 @@
 
 
 def begin_kernel(
-    order, matrix, bgt, bgc, came, local, residual, yn, ys, yw, ye, pay,
-    inverse, held, bgt_v, bgc_v, came_v, r_v, halves, product, spread, stack, pay_v, sems, tall_sems,
+    order, matrix, bgt, bgc, came_v, own, other, residual, yn, ys, yw, ye, pay,
+    inverse, held, bgt_v, bgc_v, _, r_v, halves, product, spread, stack, pay_v, sems, tall_sems,
 ):
     copies, matrix = Copies(sems), Matrix(matrix, held, tall_sems)
-    head = [copies.start(came, came_v), copies.start(bgc, bgc_v)]
-    body = [copies.start(local.at[pl.ds(M * face, M)], r_v.at[pl.ds(M * face, M)]) for face in range(4)]
+    head = [copies.start(bgc, bgc_v)]
+    body = [copies.start((other, own)[face % 2].at[face // 2], r_v.at[pl.ds(M * face, M)]) for face in range(4)]
     matrix.start(0)
     turn = [copies.start(bgt, bgt_v)]
     invert(order, inverse)
@@ -369,26 +382,26 @@
     order, matrix, bgt, bgc, came, residual, local = refs[:7]
     refs = refs[7:]
     if not first:
-        past, along, moved, image, done = refs[:5]
-        refs = refs[5:]
-    new_residual, new_along, new_moved, new_image, new_done, new_past = refs[:6]
-    new_faces, pay, refs = refs[6:10], refs[10], refs[11:]
+        past, moved, image = refs[:3]
+        refs = refs[3:]
+    new_residual, new_moved, new_past = refs[:3]
+    new_faces, pay, refs = refs[3:7], refs[7], refs[8:]
     (inverse, held, bgt_v, bgc_v, came_v, r_v, halves, product, spread, stack, pay_v, sems, tall_sems,
-     local_v, moved_v, image_v, along_v, done_v, past_v, new_past_v) = refs
+     local_v, moved_v, image_v, past_v, new_past_v) = refs
 
     copies, matrix = Copies(sems), Matrix(matrix, held, tall_sems)
     head = [copies.start(came, came_v)]
     if not first:
         head.append(copies.start(past, past_v))
     head.append(copies.start(bgc, bgc_v))
+
     def fetch(pair):
-        wide, own = pl.ds(2 * M * pair, 2 * M), pl.ds(M * pair, M)
+        wide = pl.ds(2 * M * pair, 2 * M)
         part = [copies.start(residual.at[wide], r_v.at[wide])]
         part.append(copies.start(local.at[pl.ds(2 * pair, 2)], local_v.at[pl.ds(2 * pair, 2)]))
         if not first:
             part.append(copies.start(moved.at[wide], moved_v.at[wide]))
-            for source, target in ((image, image_v), (along, along_v), (done, done_v)):
-                part.append(copies.start(source.at[own], target.at[own]))
+            part.append(copies.start(image.at[2 * pair + 1], image_v.at[pl.ds(M * pair, M)]))
         return part
 
     body = [fetch(0)]
@@ -401,10 +414,16 @@
     new_past_v[...] = jnp.zeros_like(new_past_v)
     new_past_v[0:1, :] = norm
     new_past_v[1:2, :] = curvature
+    if first:
+        new_past_v[2:3, :] = step
+    else:
+        new_past_v[2:3, :] = past_v[2:3, :] + step * ratio
+        new_past_v[3:4, :] = step
+        new_past_v[4:5, :] = ratio
     copies.out(new_past_v, new_past)
     carry = (jnp.zeros((SLOT, K), f32), jnp.zeros((SLOT, K), f32))
     for pair in range(2):
-        wide, own = pl.ds(2 * M * pair, 2 * M), pl.ds(M * pair, M)
+        wide = pl.ds(2 * M * pair, 2 * M)
         spread[...] = jnp.dot(bgc_v[2 * M * pair : 2 * M * (pair + 1), :], stacked, preferred_element_type=f32)
         wait(body[pair])
         if pair == 0:
@@ -416,25 +435,15 @@
             for kind in range(2):
                 face = 2 * pair + kind
                 rows = pl.ds(pl.multiple_of(M * face + BLK * index, BLK), BLK)
-                mine = pl.ds(pl.multiple_of(M * pair + BLK * index, BLK), BLK)
                 q = local_v[face, pl.ds(pl.multiple_of(BLK * index, BLK), BLK), :]
-                if kind:
-                    f = q if first else q + ratio * image_v[mine, :]
-                    image_v[mine, :] = f
+                f = q
+                if kind and not first:
+                    f = q + ratio * image_v[pl.ds(pl.multiple_of(M * pair + BLK * index, BLK), BLK), :]
                 q = q - spread[pl.ds(pl.multiple_of(M * kind + BLK * index, BLK), BLK), :]
                 if not first:
                     q = q + ratio * moved_v[rows, :]
                 moved_v[rows, :] = q
-                r = r_v[rows, :]
-                if kind:
-                    if first:
-                        along_v[mine, :] = r
-                        done_v[mine, :] = step * r
-                    else:
-                        d = r + ratio * along_v[mine, :]
-                        along_v[mine, :] = d
-                        done_v[mine, :] = done_v[mine, :] + step * d
-                r = r - step * q
+                r = r_v[rows, :] - step * q
                 r_v[rows, :] = r
                 put_halves(r, halves, inverse[M // BLK * face + index])
                 if kind:
@@ -447,15 +456,13 @@
             matrix.start(1)
         for source, target in ((r_v, new_residual), (moved_v, new_moved)):
             copies.out(source.at[wide], target.at[wide])
-        for source, target in ((image_v, new_image), (along_v, new_along), (done_v, new_done)):
-            copies.out(source.at[own], target.at[own])
     value, energy = schur_product(order, copies, matrix, turn, bgt_v, r_v, halves, product)
     close_product(value, carry[0], energy, carry[1], product, pay, new_faces, copies, pay_v)
 
 
 def end_kernel(
-    bgc, came, residual, local, past, along, moved, done, out_done, out_residual,
-    stack, bgc_v, came_v, past_v, r_v, local_v, along_v, moved_v, done_v, x_v, s_v, sems,
+    bgc, came, residual, first, second, local, past, moved, out_done, out_residual,
+    stack, bgc_v, came_v, past_v, r_v, first_v, second_v, local_v, moved_v, x_v, s_v, sems,
 ):
     copies = Copies(sems)
     head = [copies.start(came, came_v), copies.start(past, past_v)]
@@ -463,12 +470,15 @@
     for pair in range(2):
         rows, own = pl.ds(M * (2 * pair + 1), M), pl.ds(M * pair, M)
         part = [copies.start(bgc.at[rows], bgc_v.at[own]), copies.start(local.at[pair], local_v.at[own])]
-        part.append(copies.start(residual.at[rows], r_v.at[own]))
-        part += [copies.start(moved.at[rows], moved_v.at[own]), copies.start(along.at[own], along_v.at[own])]
-        body.append(part + [copies.start(done.at[own], done_v.at[own])])
+        for source, target in ((residual, r_v), (moved, moved_v), (first, first_v), (second, second_v)):
+            part.append(copies.start(source.at[rows], target.at[own]))
+        body.append(part)
     wait(head)
     stacked, sums = take_values(came_v, stack)
     _, _, ratio, step = scalars(False, sums, past_v)
+    along = step * ratio
+    of_second = past_v[3:4, :] + along
+    of_first = past_v[2:3, :] + along * past_v[4:5, :]
     for pair in range(2):
         wait(body[pair])
         for block in range(M // BLK):
@@ -477,9 +487,8 @@
             q = local_v[own, :] - jnp.dot(bgc_v[own, :], stacked, preferred_element_type=f32)
             q = q + ratio * moved_v[own, :]
             r = r_v[own, :]
-            d = r + ratio * along_v[own, :]
             s_v[pair, :, inside] = (r - step * q).T
-            x_v[pair, :, inside] = (done_v[own, :] + step * d).T
+            x_v[pair, :, inside] = (of_first * first_v[own, :] + of_second * second_v[own, :] + step * r).T
         copies.out(s_v.at[pair], out_residual.at[pair])
         copies.out(x_v.at[pair], out_done.at[pair])
     copies.close()
@@ -504,7 +513,8 @@
     pltpu.SemaphoreType.DMA((64,)),
     pltpu.SemaphoreType.DMA((NS // TALL,)),
 ]
-MORE = [pltpu.VMEM((4, M, K), f32), pltpu.VMEM((NS, K), f32)] + [pltpu.VMEM((2 * M, K), f32)] * 3 + [pltpu.VMEM((SLOT, K), f32)] * 2
+MORE = [pltpu.VMEM((4, M, K), f32), pltpu.VMEM((NS, K), f32), pltpu.VMEM((2 * M, K), f32)]
+MORE += [pltpu.VMEM((SLOT, K), f32)] * 2
 LAST = (
     [pltpu.VMEM((256, K), f32), pltpu.VMEM((2 * M, 2 * K), bf16), pltpu.VMEM((CHIPS, SLOTS * SLOT, K), f32)]
     + [pltpu.VMEM((SLOT, K), f32)]
@@ -529,7 +539,7 @@
 
 def coarse_phase(pay, parts, core, *beside):
     own = lax.all_to_all(pay, "row", 0, 0, tiled=True)
-    own, *beside = lax.optimization_barrier((own, *beside))
+    own, parts, *beside = lax.optimization_barrier((own, parts, *beside))
     other = swapped(own, lambda c: c ^ 1)
     (terms,) = call(
         coarse_kernel,
@@ -556,79 +566,83 @@
     masks = jnp.stack([row > 0, row < ROWS - 1, col > 0, col < COLS - 1]).astype(f32)
     side = right_side[0, 0]
 
-    from_n = cyclic(side[0], "row", 1)
-    from_w = cyclic(side[1], "col", 1)
     modes = (rigid_modes[0, 0] * floating[0, 0].astype(f32)).reshape(MODES, NB, BLK)
     modes = jnp.pad(jnp.transpose(modes, (1, 0, 2)), ((0, 0), (0, SLOT - MODES), (0, 0)))
-    local, pay = call(
+    near_s = cyclic(modes[0:4], "row", -1)
+    near_e = cyclic(modes[8:12], "col", -1)
+    own, pay = call(
         start_kernel,
         [SM] + [HB] * 4,
-        [shape(NS, K), shape(ROWS, PAY, K)],
+        [shape(2, M, K), shape(ROWS, PAY, K)],
         [
             pltpu.VMEM((NB, SLOT, BLK), f32),
+            pltpu.VMEM((2, 4, SLOT, BLK), f32),
             pltpu.VMEM((2, K, M), f32),
-            pltpu.VMEM((2, K, M), f32),
-            pltpu.VMEM((NS, K), f32),
-            pltpu.VMEM((16, NS), f32),
-            pltpu.VMEM((NS, 2 * K), bf16),
+            pltpu.VMEM((2, M, K), f32),
+            pltpu.VMEM((ROWS16, 2 * M), f32),
+            pltpu.VMEM((2 * M, 2 * K), bf16),
             pltpu.VMEM((PAY, K), f32),
             pltpu.SemaphoreType.DMA((16,)),
         ],
         10**8,
         HB,
-    )(masks, modes, side, from_n, from_w)
-
+    )(masks, modes, near_s, near_e, side)
+    from_n = cyclic(side[0], "row", 1)
+    from_w = cyclic(side[1], "col", 1)
     mine = jnp.transpose(coarse_inverse[:, 0, :, :, :, 0], (1, 0, 3, 2))
-    mine = jnp.pad(mine, ((0, 0), (0, SLOT - MODES), (0, 0), (0, SLOT - MODES))).reshape(COLS, SLOT, SLOT * ROWS)
-    mine = jnp.concatenate([mine, mine], axis=2)
+    mine = jnp.pad(mine, ((0, 0), (0, SLOT - MODES), (0, 0), (0, SLOT - MODES))).reshape(HALF, 2, SLOT, SLOT * ROWS)
+    mine = jnp.concatenate([mine[:, 0], mine[:, 1]], axis=2)
     down = cyclic(jnp.concatenate([mine, modes[4:8]], axis=0), "row", 1)
-    up = cyclic(jnp.concatenate([mine, modes[0:4]], axis=0), "row", -1)
+    up = cyclic(mine, "row", -1)
     down, up, pay = lax.optimization_barrier((down, up, pay))
-    lines = jnp.concatenate([mine, down[:COLS], up[:COLS]], axis=0)
+    lines = jnp.concatenate([mine, down[:HALF], up], axis=0)
     right = cyclic(jnp.concatenate([lines, modes[12:16]], axis=0), "col", 1)
-    left = cyclic(jnp.concatenate([lines, modes[8:12]], axis=0), "col", -1)
-    far = swapped(jnp.where(core[0] == 0, right[: 3 * COLS], left[: 3 * COLS]), lambda c: c ^ 1)
+    left = cyclic(lines, "col", -1)
+    right, left, from_n, from_w = lax.optimization_barrier((right, left, from_n, from_w))
+    far = swapped(jnp.where(core[0] == 0, right[: 3 * HALF], left), lambda c: c ^ 1)
     (parts,) = call(
         table_kernel,
         [SM] + [HB] * 6,
         [shape(2, CHIPS * SLOTS * SLOT, 2 * K, kind=bf16)],
-        [pltpu.VMEM((tiles, SLOT, BLK), f32) for tiles in (COLS, COLS + 4, COLS + 4, 3 * COLS + 4, 3 * COLS + 4, 3 * COLS)]
+        [pltpu.VMEM((tiles, SLOT, BLK), f32) for tiles in (HALF, HALF + 4, HALF, 3 * HALF + 4, 3 * HALF, 3 * HALF)]
         + [
             pltpu.VMEM((CHIPS * SLOTS * SLOT, 2 * K), f32),
             pltpu.VMEM((2, CHIPS * SLOTS * SLOT, 2 * K), bf16),
             pltpu.SemaphoreType.DMA((16,)),
         ],
-        10**7,
+        10**6,
         HB,
     )(core, mine, down, up, right, left, far)
-    bgt, bgc = call(
+    bgt, bgc, other = call(
         modes_kernel,
-        [SM] * 2 + [HB] * 5,
-        [shape(2 * ROWS16, NS, kind=bf16), shape(NS, 2 * K, kind=bf16)],
+        [SM] * 2 + [HB] * 7,
+        [shape(2 * ROWS16, NS, kind=bf16), shape(NS, 2 * K, kind=bf16), shape(2, M, K)],
         [pltpu.VMEM((tiles, SLOT, BLK), f32) for tiles in (NB, 4, 4, 4, 4)]
         + [
             pltpu.VMEM((ROWS16, NS), f32),
             pltpu.VMEM((256, NS), f32),
             pltpu.VMEM((2 * ROWS16, NS), bf16),
             pltpu.VMEM((NS, 2 * K), bf16),
+            pltpu.VMEM((2, K, M), f32),
+            pltpu.VMEM((2, M, K), f32),
             pltpu.SemaphoreType.DMA((16,)),
         ],
-        10**8,
+        COST,
         HB,
-    )(order, masks, modes, down, up, right, left)
+    )(order, masks, modes, down, near_s, right, near_e, from_n, from_w)
     (came,) = coarse_phase(pay, parts, core)
 
     matrix = schur_blocks[0, 0]
     residual, *faces, pay = call(
         begin_kernel,
-        [SM] + [HB] * 5,
+        [SM] + [HB] * 3 + [VM] + [HB] * 2,
         [shape(NS, K)] + FACES + [shape(ROWS, PAY, K)],
         WORK,
         2 * 10**9,
         HB,
-    )(order, matrix, bgt, bgc, came, local)
-
-    state = ()
+    )(order, matrix, bgt, bgc, came, own, other)
+
+    state, residuals = (), [residual]
     for iteration in range(ITERS):
         which = (1, 3) if iteration + 1 == ITERS else (0, 1, 2, 3)
         moves = (("row", 1), ("row", -1), ("col", 1), ("col", -1))
@@ -646,20 +660,18 @@
         if iteration + 1 == ITERS:
             break
         first = iteration == 0
-        given = (order, matrix, bgt, bgc, came, residual, local, *state)
-        residual, along, moved, image, done, past, *faces, pay = call(
+        given = (order, matrix, bgt, bgc, came, residuals[-1], local, *state)
+        residual, moved, past, *faces, pay = call(
             functools.partial(step_kernel, first),
             [SM] + [HB] * (len(given) - 1),
-            [shape(NS, K), shape(2 * M, K), shape(NS, K), shape(2 * M, K), shape(2 * M, K), shape(SLOT, K)]
-            + FACES
-            + [shape(ROWS, PAY, K)],
+            [shape(NS, K), shape(NS, K), shape(SLOT, K)] + FACES + [shape(ROWS, PAY, K)],
             WORK + MORE,
             2 * 10**9,
             HB,
         )(*given)
-        state = (past, along, moved, image, done)
-
-    past, along, moved, image, done = state
+        state = (past, moved, local)
+        residuals.append(residual)
+
     done, residual = call(
         end_kernel,
         [HB] * 8,
@@ -667,7 +679,7 @@
         LAST,
         10**8,
         HB,
-    )(bgc, came, residual, local, past, along, moved, done)
+    )(bgc, came, residuals[2], residuals[0], residuals[1], local, past, moved)
     return (done[None, None], residual[None, None])
 
 

time: 186 us -> 186 us (level)
    ppermute x16 -> x18, starting transfers between devices: 21.4 us -> 25.3 us  [cyclic(): lax.ppermute(value, axis, [(s, (s + steps) % count) for s in range(count)])]
    ppermute x5, starting transfers between devices: 16.8 us -> 14.5 us  [swapped(): return lax.ppermute(value, 'col', [(s, partner(s)) for s in range(COLS)])]
    ppermute x5, waiting for transfers between devices: 3.09 us -> 5.18 us  [swapped(): return lax.ppermute(value, 'col', [(s, partner(s)) for s in range(COLS)])]
    ppermute x16 -> x18, waiting for transfers between devices: 4.64 us -> 2.6 us  [cyclic(): lax.ppermute(value, axis, [(s, (s + steps) % count) for s in range(count)])]
    unnamed x41 -> x47, local copies, waits for them, and re-layouts: 7.72 us -> 7.98 us
  transfers between devices with their start and end apart: 26 -> 28, of which waited for: 13 -> 14; matrix products, arithmetic and copies ran while one was open for 2% -> 2% of each run, Pallas kernels for 10% -> 10%
where the time goes in v3:
time: 186 us; the launch traced here: 185 us
  starting transfers between devices  58.6 us (32%)
  Pallas kernels  53 us (28%)
  blocking collectives  35.1 us (19%)
  waiting for transfers between devices  24.1 us (13%)
  local copies, waits for them, and re-layouts  10.1 us (5%)
  between operations  1.89 us (1%)
    all_to_all x3, blocking collectives, coarse_phase(): lax.all_to_all(terms, 'col', 0, 0, axis_index_groups=groups, tiled=True)  35.1 us
    ppermute x18, starting transfers between devices, cyclic(): lax.ppermute(value, axis, [(s, (s + steps) % count) for s in range(count)])  25.3 us
    pallas_call x2, Pallas kernels, per_device(): call(functools.partial(step_kernel, first), [SM] + [HB] * (len(given) - 1...  18.5 us
    all_to_all x4, starting transfers between devices, coarse_phase(): own = lax.all_to_all(pay, 'row', 0, 0, tiled=True)  15 us
    ppermute x5, starting transfers between devices, swapped(): return lax.ppermute(value, 'col', [(s, partner(s)) for s in range(COLS)])  14.5 us
    all_to_all x4, waiting for transfers between devices, coarse_phase(): own = lax.all_to_all(pay, 'row', 0, 0, tiled=True)  11.3 us
    pallas_call x3, Pallas kernels, per_device(): call(functools.partial(image_kernel, which), [SM] + [HB] * (2 * len(which...  8.81 us
    pallas_call x1, Pallas kernels, per_device(): call(begin_kernel, [SM] + [HB] * 3 + [VM] + [HB] * 2, [shape(NS, K)] + FA...  8.7 us
  transfers between devices with their start and end apart: 28, of which 14 were waited for; matrix products, arithmetic and copies ran while one was open for 2% of the time, Pallas kernels for 10%

profile of v3, /device:TPU:1, one launch (start us, length us, event | category | flops | bytes accessed | tf_op | source)
XLA Modules:
  0.0 184.7 jit_solution(1384805799159709574)
XLA Ops:
  1.3 0.8 broadcast_multiply_fusion
  2.2 6.5 %collective-permute-start.2 = (f32[4,8,128]{2,1,0:T(8,128)S(1)}, f32[4,8,128]{2,1,0:T(8,128)S(1)}, u32[]{:S(2)}, u32[]{:S(2)}) collective-permute-start(f32[4,8,128]{2,1,0:T(8,128)S(1)} %get-tuple-element.102), channel_id=1, source_target_pairs={{0,224},{32,0},{64,32},{96,64},{128,96},{160,128},{192,160},{224,1... | collective-permute-start | bytes 49160 | tf_op jit(solution)/shard_map/ppermute | solution.py:40
  8.6 1.0 collective-permute-start.3
  9.6 1.1 slice_bitcast_fusion
  10.7 1.3 collective-permute-start.7
  11.9 1.3 copy.14
  13.8 0.8 collective-permute-start.1
  14.7 0.8 collective-permute-start
  15.5 0.6 add_convert_fusion.masks.refs_0_
  16.1 0.6 pad.8.own
  16.8 0.6 copy-done.9
  17.4 3.0 %shard_map.77 = (f32[2,512,128]{2,1,0:T(8,128)}, f32[8,40,128]{2,1,0:T(8,128)}) custom-call(f32[4]{0:T(128)} %add_convert_fusion.masks.refs_0_, f32[16,8,128]{2,1,0:T(8,128)} %pad.8.own, f32[4,8,128]{2,1,0:T(8,128)} %copy-done.9, f32[4,8,128]{2,1,0:T(8,128)} %copy-done.10, f32[2,128,512]{2,1,0:T(8,128)} %bitcast.35), custom_call_target="tpu_custom_call" | custom-call | flops 100000000 | bytes 1048576 | tf_op jit(solution)/shard_map/pallas_call | solution.py:573
  20.5 1.7 collective-permute-start.4
  22.3 2.8 %collective-permute-start.5 = (f32[48,8,128]{2,1,0:T(8,128)S(1)}, f32[48,8,128]{2,1,0:T(8,128)S(1)}, u32[]{:S(2)}, u32[]{:S(2)}) collective-permute-start(f32[48,8,128]{2,1,0:T(8,128)S(1)} %pad_maximum_fusion.1), channel_id=1, source_target_pairs={{0,31},{1,0},{2,1},{3,2},{4,3},{5,4},{6,5},{7,6},{8,7},{9,8},{10,9... | collective-permute-start | bytes 589832 | tf_op jit(solution)/shard_map/ppermute | solution.py:40
  25.1 4.1 %all-to-all-start = ((f32[8,40,128]{2,1,0:T(8,128)}), f32[8,40,128]{2,1,0:T(8,128)S(1)}, u32[]{:S(2)}, u32[]{:S(2)}) async-start(f32[8,40,128]{2,1,0:T(8,128)} %get-tuple-element.57), calls=%async_computation | async-start | bytes 327680 | tf_op jit(solution)/shard_map/all_to_all | solution.py:541
  29.3 5.4 %collective-permute-start.8 = (f32[48,8,128]{2,1,0:T(8,128)S(1)}, f32[48,8,128]{2,1,0:T(8,128)S(1)}, u32[]{:S(2)}, u32[]{:S(2)}) collective-permute-start(f32[48,8,128]{2,1,0:T(8,128)S(1)} %slice_select_fusion), channel_id=1, source_target_pairs={{0,1},{1,0},{2,3},{3,2},{4,5},{5,4},{6,7},{7,6},{8,9},{9,8},{10,11... | collective-permute-start | bytes 589832 | tf_op jit(solution)/shard_map/ppermute | solution.py:50
  34.7 1.1 collective-permute-done.8.far
  35.8 0.7 copy-done.8
  36.5 3.8 %shard_map.79.parts = bf16[2,640,256]{2,1,0:T(8,128)(2,1)} custom-call(s32[1]{0:T(128)} %bitcast.15.core, f32[16,8,128]{2,1,0:T(8,128)} %copy-done.7, f32[20,8,128]{2,1,0:T(8,128)} %copy-done.6, f32[16,8,128]{2,1,0:T(8,128)} %copy-done.5, f32[52,8,128]{2,1,0:T(8,128)} %copy-done.3, f32[48,8,128]{2,1,0:T(8,128)} %copy-done.4, f32[48,8,128]{2,1,0:T(8,128)} %copy-done.8), custom_call_target="tpu_custom_call" | custom-call | flops 1000000 | bytes 1048576 | tf_op jit(solution)/shard_map/pallas_call | solution.py:603
  40.3 3.6 %collective-permute-start.9 = (f32[8,40,128]{2,1,0:T(8,128)S(1)}, f32[8,40,128]{2,1,0:T(8,128)S(1)}, u32[]{:S(2)}, u32[]{:S(2)}) collective-permute-start(f32[8,40,128]{2,1,0:T(8,128)S(1)} %all-to-all-done.own_v), channel_id=1, source_target_pairs={{0,1},{1,0},{2,3},{3,2},{4,5},{5,4},{6,7},{7,6},{8,9},{9,8},{10,11... | collective-permute-start | bytes 491528 | tf_op jit(solution)/shard_map/ppermute | solution.py:50
  44.0 1.0 collective-permute-done.9.other_v
  45.0 1.1 copy-done
  46.1 1.4 shard_map.80
  47.5 3.7 %all-to-all-start.1 = ((f32[16,40,128]{2,1,0:T(8,128)}), f32[16,40,128]{2,1,0:T(8,128)S(1)}, u32[]{:S(2)}, u32[]{:S(2)}) async-start(f32[16,40,128]{2,1,0:T(8,128)} %shard_map.80), calls=%async_computation.1 | async-start | bytes 655360 | tf_op jit(solution)/shard_map/all_to_all | solution.py:559
  51.3 3.3 %shard_map.78 = (bf16[96,2048]{1,0:T(8,128)(2,1)}, bf16[2048,256]{1,0:T(8,128)(2,1)}, f32[2,512,128]{2,1,0:T(8,128)}) custom-call(s32[16]{0:T(128)} %bitcast.40, f32[4]{0:T(128)} %add_convert_fusion.masks.refs_0_, f32[16,8,128]{2,1,0:T(8,128)} %pad.8.own, f32[20,8,128]{2,1,0:T(8,128)} %copy-done.6, f32[4,8,128]{2,1,0:T(8,128)} %copy-done.9, ...), custom_call_target="tpu_custom_call" | custom-call | flops 20000000000 | bytes 1048576 | tf_op jit(solution)/shard_map/pallas_call | solution.py:616
  54.6 5.1 %all-to-all-done.1.came_v = f32[16,40,128]{2,1,0:T(8,128)S(1)} async-done(((f32[16,40,128]{2,1,0:T(8,128)}), f32[16,40,128]{2,1,0:T(8,128)S(1)}, u32[]{:S(2)}, u32[]{:S(2)}) %all-to-all-start.1) | async-done | bytes 327712 | tf_op jit(solution)/shard_map/all_to_all | solution.py:559
  59.6 0.7 copy-done.2
  60.4 8.7 %shard_map.81 = (f32[2048,128]{1,0:T(8,128)}, f32[512,128]{1,0:T(8,128)}, f32[512,128]{1,0:T(8,128)}, f32[512,128]{1,0:T(8,128)}, f32[512,128]{1,0:T(8,128)}, /*index=5*/f32[8,40,128]{2,1,0:T(8,128)}) custom-call(s32[16]{0:T(128)} %bitcast.41, bf16[2048,2048]{1,0:T(8,128)(2,1)} %bitcast.32, bf16[96,2048]{1,0:T(8,128)(2,1)} %get-tuple-element.56.bgt.refs_2_, ...), custom_call_target="tpu_custom_call" | custom-call | flops 2000000000 | bytes 1048576 | tf_op jit(solution)/shard_map/pallas_call | solution.py:636
  69.1 0.6 collective-permute-start.11
  69.7 0.9 collective-permute-start.10
  70.6 2.0 %collective-permute-start.13 = (f32[512,128]{1,0:T(8,128)}, f32[512,128]{1,0:T(8,128)S(1)}, u32[]{:S(2)}, u32[]{:S(2)}) collective-permute-start(f32[512,128]{1,0:T(8,128)} %get-tuple-element.66.refs_3_), channel_id=1, source_target_pairs={{0,31},{1,0},{2,1},{3,2},{4,3},{5,4},{6,5},{7,6},{8,7},{9,8},{10,9... | collective-permute-start | bytes 786440 | tf_op jit(solution)/shard_map/ppermute | solution.py:40
  72.7 3.7 %all-to-all-start.2 = ((f32[8,40,128]{2,1,0:T(8,128)}), f32[8,40,128]{2,1,0:T(8,128)S(1)}, u32[]{:S(2)}, u32[]{:S(2)}) async-start(f32[8,40,128]{2,1,0:T(8,128)} %get-tuple-element.63), calls=%async_computation.2 | async-start | bytes 327680 | tf_op jit(solution)/shard_map/all_to_all | solution.py:541
  77.9 0.7 copy-done.19
  78.6 3.0 %shard_map.82.refs_6_.refs_9_ = f32[4,512,128]{2,1,0:T(8,128)} custom-call(f32[4]{0:T(128)} %add_convert_fusion.masks.refs_0_, f32[512,128]{1,0:T(8,128)} %get-tuple-element.64.refs_1_, f32[512,128]{1,0:T(8,128)} %get-tuple-element.65.refs_2_, f32[512,128]{1,0:T(8,128)} %get-tuple-element.66.refs_3_, f32[512,128]{1,0:T(8,128)} %get-tuple-element.67.refs_4_, ...), custom_call_target="tpu_custom_call" | custom-call | flops 20000000000 | bytes 1048576 | tf_op jit(solution)/shard_map/pallas_call | solution.py:651
  81.7 3.1 %all-to-all-done.2.own_v = f32[8,40,128]{2,1,0:T(8,128)S(1)} async-done(((f32[8,40,128]{2,1,0:T(8,128)}), f32[8,40,128]{2,1,0:T(8,128)S(1)}, u32[]{:S(2)}, u32[]{:S(2)}) %all-to-all-start.2) | async-done | bytes 163872 | tf_op jit(solution)/shard_map/all_to_all | solution.py:541
  84.8 2.3 %collective-permute-start.14 = (f32[8,40,128]{2,1,0:T(8,128)S(1)}, f32[8,40,128]{2,1,0:T(8,128)S(1)}, u32[]{:S(2)}, u32[]{:S(2)}) collective-permute-start(f32[8,40,128]{2,1,0:T(8,128)S(1)} %all-to-all-done.2.own_v), channel_id=1, source_target_pairs={{0,1},{1,0},{2,3},{3,2},{4,5},{5,4},{6,7},{7,6},{8,9},{9,8},{10,11... | collective-permute-start | bytes 491528 | tf_op jit(solution)/shard_map/ppermute | solution.py:50
  87.1 1.0 collective-permute-done.14.other_v
  88.2 0.7 shard_map.83
  88.9 11.8 %all_to_all.40.refs_4_ = f32[16,40,128]{2,1,0:T(8,128)} all-to-all(f32[16,40,128]{2,1,0:T(8,128)S(1)} %shard_map.83), channel_id=1, replica_groups={{0,2,4,6,8,10,12,14,16,18,20,22,24,26,28,30},{1,3,5,7,9,11,13,15,17,19,..., dimensions={0} | all-to-all | bytes 655360 | tf_op jit(solution)/shard_map/all_to_all | solution.py:559
  100.8 9.0 %shard_map.84 = (f32[2048,128]{1,0:T(8,128)}, f32[2048,128]{1,0:T(8,128)}, f32[8,128]{1,0:T(8,128)}, f32[512,128]{1,0:T(8,128)}, f32[512,128]{1,0:T(8,128)}, /*i...) custom-call(s32[16]{0:T(128)} %bitcast.42, bf16[2048,2048]{1,0:T(8,128)(2,1)} %bitcast.33, ...), custom_call_target="tpu_custom_call" | custom-call | flops 2000000000 | bytes 1048576 | tf_op jit(solution)/shard_map/pallas_call | solution.py:664
  109.8 1.1 collective-permute-start.16
  111.3 2.7 %collective-permute-start.18 = (f32[512,128]{1,0:T(8,128)}, f32[512,128]{1,0:T(8,128)S(1)}, u32[]{:S(2)}, u32[]{:S(2)}) collective-permute-start(f32[512,128]{1,0:T(8,128)} %get-tuple-element.75.refs_3_), channel_id=1, source_target_pairs={{0,31},{1,0},{2,1},{3,2},{4,3},{5,4},{6,5},{7,6},{8,7},{9,8},{10,9... | collective-permute-start | bytes 786440 | tf_op jit(solution)/shard_map/ppermute | solution.py:40
  114.0 3.6 %all-to-all-start.4 = ((f32[8,40,128]{2,1,0:T(8,128)}), f32[8,40,128]{2,1,0:T(8,128)S(1)}, u32[]{:S(2)}, u32[]{:S(2)}) async-start(f32[8,40,128]{2,1,0:T(8,128)} %get-tuple-element.72), calls=%async_computation.4 | async-start | bytes 327680 | tf_op jit(solution)/shard_map/all_to_all | solution.py:541
  117.6 0.7 collective-permute-done.15.refs_5_
  118.5 0.5 copy-done.16
  119.2 0.7 copy-done.20
  119.9 3.1 %shard_map.85.refs_6_ = f32[4,512,128]{2,1,0:T(8,128)} custom-call(f32[4]{0:T(128)} %add_convert_fusion.masks.refs_0_, f32[512,128]{1,0:T(8,128)} %get-tuple-element.73.refs_1_, f32[512,128]{1,0:T(8,128)} %get-tuple-element.74.refs_2_, f32[512,128]{1,0:T(8,128)} %get-tuple-element.75.refs_3_, f32[512,128]{1,0:T(8,128)} %get-tuple-element.76.refs_4_, ...), custom_call_target="tpu_custom_call" | custom-call | flops 20000000000 | bytes 1048576 | tf_op jit(solution)/shard_map/pallas_call | solution.py:651
  123.0 3.2 %all-to-all-done.4.own_v = f32[8,40,128]{2,1,0:T(8,128)S(1)} async-done(((f32[8,40,128]{2,1,0:T(8,128)}), f32[8,40,128]{2,1,0:T(8,128)S(1)}, u32[]{:S(2)}, u32[]{:S(2)}) %all-to-all-start.4) | async-done | bytes 163872 | tf_op jit(solution)/shard_map/all_to_all | solution.py:541
  126.2 1.7 collective-permute-start.19
  127.9 1.0 collective-permute-done.19.other_v
  128.9 0.7 shard_map.86
  129.7 12.0 %all_to_all.41.refs_4_ = f32[16,40,128]{2,1,0:T(8,128)} all-to-all(f32[16,40,128]{2,1,0:T(8,128)S(1)} %shard_map.86), channel_id=1, replica_groups={{0,2,4,6,8,10,12,14,16,18,20,22,24,26,28,30},{1,3,5,7,9,11,13,15,17,19,..., dimensions={0} | all-to-all | bytes 655360 | tf_op jit(solution)/shard_map/all_to_all | solution.py:559
  141.7 9.5 %shard_map.87 = (f32[2048,128]{1,0:T(8,128)}, f32[2048,128]{1,0:T(8,128)}, f32[8,128]{1,0:T(8,128)}, f32[512,128]{1,0:T(8,128)}, f32[512,128]{1,0:T(8,128)}, /*i...) custom-call(s32[16]{0:T(128)} %bitcast.43, bf16[2048,2048]{1,0:T(8,128)(2,1)} %bitcast.34, ...), custom_call_target="tpu_custom_call" | custom-call | flops 2000000000 | bytes 1048576 | tf_op jit(solution)/shard_map/pallas_call | solution.py:664
  151.6 2.2 %collective-permute-start.21 = (f32[512,128]{1,0:T(8,128)}, f32[512,128]{1,0:T(8,128)S(1)}, u32[]{:S(2)}, u32[]{:S(2)}) collective-permute-start(f32[512,128]{1,0:T(8,128)} %get-tuple-element.87), channel_id=1, source_target_pairs={{0,31},{1,0},{2,1},{3,2},{4,3},{5,4},{6,5},{7,6},{8,7},{9,8},{10,9... | collective-permute-start | bytes 786440 | tf_op jit(solution)/shard_map/ppermute | solution.py:40
  153.8 3.6 %all-to-all-start.6 = ((f32[8,40,128]{2,1,0:T(8,128)}), f32[8,40,128]{2,1,0:T(8,128)S(1)}, u32[]{:S(2)}, u32[]{:S(2)}) async-start(f32[8,40,128]{2,1,0:T(8,128)} %get-tuple-element.83), calls=%async_computation.6 | async-start | bytes 327680 | tf_op jit(solution)/shard_map/all_to_all | solution.py:541
  157.4 0.9 collective-permute-done.21.refs_4_
  158.3 0.7 copy-done.22
  159.0 2.7 %shard_map.88.local = f32[2,512,128]{2,1,0:T(8,128)} custom-call(f32[4]{0:T(128)} %add_convert_fusion.masks.refs_0_, f32[512,128]{1,0:T(8,128)} %get-tuple-element.84.refs_1_, f32[512,128]{1,0:T(8,128)} %get-tuple-element.85.refs_2_, f32[512,128]{1,0:T(8,128)} %copy-done.21, f32[512,128]{1,0:T(8,128)} %copy-done.22), custom_call_target="tpu_custom_call" | custom-call | flops 20000000000 | bytes 1048576 | tf_op jit(solution)/shard_map/pallas_call | solution.py:651
  161.8 4.9 %all-to-all-done.6.own_v = f32[8,40,128]{2,1,0:T(8,128)S(1)} async-done(((f32[8,40,128]{2,1,0:T(8,128)}), f32[8,40,128]{2,1,0:T(8,128)S(1)}, u32[]{:S(2)}, u32[]{:S(2)}) %all-to-all-start.6) | async-done | bytes 163872 | tf_op jit(solution)/shard_map/all_to_all | solution.py:541
  166.7 1.4 collective-permute-start.22
  168.1 1.0 collective-permute-done.22.other_v
  169.2 0.7 shard_map.89
  169.9 11.2 %all_to_all.42.came = f32[16,40,128]{2,1,0:T(8,128)} all-to-all(f32[16,40,128]{2,1,0:T(8,128)S(1)} %shard_map.89), channel_id=1, replica_groups={{0,2,4,6,8,10,12,14,16,18,20,22,24,26,28,30},{1,3,5,7,9,11,13,15,17,19,..., dimensions={0} | all-to-all | bytes 655360 | tf_op jit(solution)/shard_map/all_to_all | solution.py:559
  181.2 3.4 %shard_map.90 = (f32[2,128,512]{2,1,0:T(8,128)}, f32[2,128,512]{2,1,0:T(8,128)}) custom-call(bf16[2048,256]{1,0:T(8,128)(2,1)} %get-tuple-element.55.bgc.refs_3_, f32[16,40,128]{2,1,0:T(8,128)} %all_to_all.42.came, f32[2048,128]{1,0:T(8,128)} %get-tuple-element.90.residual, f32[2048,128]{1,0:T(8,128)} %get-tuple-element.70.refs_5_.first, ...), custom_call_target="tpu_custom_call" | custom-call | flops 100000000 | bytes 1048576 | tf_op jit(solution)/shard_map/pallas_call | solution.py:675
  (71 shorter events, 3.7 us)
Async XLA Ops:
  2.2 14.6 %collective-permute-start.2 = (f32[4,8,128]{2,1,0:T(8,128)S(1)}, f32[4,8,128]{2,1,0:T(8,128)S(1)}, u32[]{:S(2)}, u32[]{:S(2)}) collective-permute-start(f32[4,8,128]{2,1,0:T(8,128)S(1)} %get-tuple-element.102), channel_id=1, source_target_pairs={{0,224},{32,0},{64,32},{96,64},{128,96},{160,128},{192,160},{224,1... | collective-permute-start | bytes 49160 | tf_op jit(solution)/shard_map/ppermute | solution.py:40
  8.6 8.2 %collective-permute-start.3 = (f32[4,8,128]{2,1,0:T(8,128)S(1)}, f32[4,8,128]{2,1,0:T(8,128)S(1)}, u32[]{:S(2)}, u32[]{:S(2)}) collective-permute-start(f32[4,8,128]{2,1,0:T(8,128)S(1)} %get-tuple-element.103), channel_id=1, source_target_pairs={{0,31},{1,0},{2,1},{3,2},{4,3},{5,4},{6,5},{7,6},{8,7},{9,8},{10,9... | collective-permute-start | bytes 49160 | tf_op jit(solution)/shard_map/ppermute | solution.py:40
  10.7 18.6 %collective-permute-start.7 = (f32[128,512]{1,0:T(8,128)S(1)}, f32[128,512]{1,0:T(8,128)S(1)}, u32[]{:S(2)}, u32[]{:S(2)}) collective-permute-start(f32[128,512]{1,0:T(8,128)S(1)} %get-tuple-element.96), channel_id=1, source_target_pairs={{0,1},{1,2},{2,3},{3,4},{4,5},{5,6},{6,7},{7,8},{8,9},{9,10},{10,1... | collective-permute-start | bytes 786440 | tf_op jit(solution)/shard_map/ppermute | solution.py:40
  13.8 22.0 %copy-start.7 = (f32[16,8,128]{2,1,0:T(8,128)}, f32[16,8,128]{2,1,0:T(8,128)S(1)}, u32[]{:S(2)}) copy-start(f32[16,8,128]{2,1,0:T(8,128)S(1)} %pad_maximum_fusion.3.mine) | copy-start | bytes 196612
  13.8 6.6 %collective-permute-start.1 = (f32[16,8,128]{2,1,0:T(8,128)S(1)}, f32[16,8,128]{2,1,0:T(8,128)S(1)}, u32[]{:S(2)}, u32[]{:S(2)}) collective-permute-start(f32[16,8,128]{2,1,0:T(8,128)S(1)} %pad_maximum_fusion.3.mine), channel_id=1, source_target_pairs={{0,224},{32,0},{64,32},{96,64},{128,96},{160,128},{192,160},{224,1... | collective-permute-start | bytes 196616 | tf_op jit(solution)/shard_map/ppermute | solution.py:40
  14.7 5.7 %collective-permute-start = (f32[20,8,128]{2,1,0:T(8,128)S(1)}, f32[20,8,128]{2,1,0:T(8,128)S(1)}, u32[]{:S(2)}, u32[]{:S(2)}) collective-permute-start(f32[20,8,128]{2,1,0:T(8,128)S(1)} %pad_maximum_fusion.2), channel_id=1, source_target_pairs={{0,32},{32,64},{64,96},{96,128},{128,160},{160,192},{192,224},{224... | collective-permute-start | bytes 245768 | tf_op jit(solution)/shard_map/ppermute | solution.py:40
  16.8 0.6 copy-start.9
  16.8 12.5 %collective-permute-start.6 = (f32[128,512]{1,0:T(8,128)S(1)}, f32[128,512]{1,0:T(8,128)S(1)}, u32[]{:S(2)}, u32[]{:S(2)}) collective-permute-start(f32[128,512]{1,0:T(8,128)S(1)} %get-tuple-element.97), channel_id=1, source_target_pairs={{0,32},{32,64},{64,96},{96,128},{128,160},{160,192},{192,224},{224... | collective-permute-start | bytes 786440 | tf_op jit(solution)/shard_map/ppermute | solution.py:40
  16.8 0.6 copy-start.10
  20.4 15.4 %copy-start.5 = (f32[16,8,128]{2,1,0:T(8,128)}, f32[16,8,128]{2,1,0:T(8,128)S(1)}, u32[]{:S(2)}) copy-start(f32[16,8,128]{2,1,0:T(8,128)S(1)} %collective-permute-done.1.up) | copy-start | bytes 196612
  20.4 15.4 %copy-start.6 = (f32[20,8,128]{2,1,0:T(8,128)}, f32[20,8,128]{2,1,0:T(8,128)S(1)}, u32[]{:S(2)}) copy-start(f32[20,8,128]{2,1,0:T(8,128)S(1)} %collective-permute-done.down) | copy-start | bytes 245764
  20.5 8.7 %collective-permute-start.4 = (f32[52,8,128]{2,1,0:T(8,128)S(1)}, f32[52,8,128]{2,1,0:T(8,128)S(1)}, u32[]{:S(2)}, u32[]{:S(2)}) collective-permute-start(f32[52,8,128]{2,1,0:T(8,128)S(1)} %pad_maximum_fusion), channel_id=1, source_target_pairs={{0,1},{1,2},{2,3},{3,4},{4,5},{5,6},{6,7},{7,8},{8,9},{9,10},{10,1... | collective-permute-start | bytes 638984 | tf_op jit(solution)/shard_map/ppermute | solution.py:40
  22.3 6.9 %collective-permute-start.5 = (f32[48,8,128]{2,1,0:T(8,128)S(1)}, f32[48,8,128]{2,1,0:T(8,128)S(1)}, u32[]{:S(2)}, u32[]{:S(2)}) collective-permute-start(f32[48,8,128]{2,1,0:T(8,128)S(1)} %pad_maximum_fusion.1), channel_id=1, source_target_pairs={{0,31},{1,0},{2,1},{3,2},{4,3},{5,4},{6,5},{7,6},{8,7},{9,8},{10,9... | collective-permute-start | bytes 589832 | tf_op jit(solution)/shard_map/ppermute | solution.py:40
  25.1 15.2 %all-to-all-start = ((f32[8,40,128]{2,1,0:T(8,128)}), f32[8,40,128]{2,1,0:T(8,128)S(1)}, u32[]{:S(2)}, u32[]{:S(2)}) async-start(f32[8,40,128]{2,1,0:T(8,128)} %get-tuple-element.57), calls=%async_computation | async-start | bytes 327680 | tf_op jit(solution)/shard_map/all_to_all | solution.py:541
  29.2 22.0 %copy-start.11 = (f32[128,512]{1,0:T(8,128)}, f32[128,512]{1,0:T(8,128)S(1)}, u32[]{:S(2)}) copy-start(f32[128,512]{1,0:T(8,128)S(1)} %collective-permute-done.7.from_w) | copy-start | bytes 786436
  29.2 22.0 %copy-start.12 = (f32[128,512]{1,0:T(8,128)}, f32[128,512]{1,0:T(8,128)S(1)}, u32[]{:S(2)}) copy-start(f32[128,512]{1,0:T(8,128)S(1)} %collective-permute-done.6.from_n) | copy-start | bytes 786436
  29.3 6.6 %copy-start.4 = (f32[48,8,128]{2,1,0:T(8,128)}, f32[48,8,128]{2,1,0:T(8,128)S(1)}, u32[]{:S(2)}) copy-start(f32[48,8,128]{2,1,0:T(8,128)S(1)} %collective-permute-done.5.left) | copy-start | bytes 589828
  29.3 6.6 %copy-start.3 = (f32[52,8,128]{2,1,0:T(8,128)}, f32[52,8,128]{2,1,0:T(8,128)S(1)}, u32[]{:S(2)}) copy-start(f32[52,8,128]{2,1,0:T(8,128)S(1)} %collective-permute-done.4.right) | copy-start | bytes 638980
  29.3 6.5 %collective-permute-start.8 = (f32[48,8,128]{2,1,0:T(8,128)S(1)}, f32[48,8,128]{2,1,0:T(8,128)S(1)}, u32[]{:S(2)}, u32[]{:S(2)}) collective-permute-start(f32[48,8,128]{2,1,0:T(8,128)S(1)} %slice_select_fusion), channel_id=1, source_target_pairs={{0,1},{1,0},{2,3},{3,2},{4,5},{5,4},{6,7},{7,6},{8,9},{9,8},{10,11... | collective-permute-start | bytes 589832 | tf_op jit(solution)/shard_map/ppermute | solution.py:50
  35.8 0.7 copy-start.8
  40.3 4.7 %collective-permute-start.9 = (f32[8,40,128]{2,1,0:T(8,128)S(1)}, f32[8,40,128]{2,1,0:T(8,128)S(1)}, u32[]{:S(2)}, u32[]{:S(2)}) collective-permute-start(f32[8,40,128]{2,1,0:T(8,128)S(1)} %all-to-all-done.own_v), channel_id=1, source_target_pairs={{0,1},{1,0},{2,3},{3,2},{4,5},{5,4},{6,7},{7,6},{8,9},{9,8},{10,11... | collective-permute-start | bytes 491528 | tf_op jit(solution)/shard_map/ppermute | solution.py:50
  45.0 1.1 copy-start
  47.5 12.1 %all-to-all-start.1 = ((f32[16,40,128]{2,1,0:T(8,128)}), f32[16,40,128]{2,1,0:T(8,128)S(1)}, u32[]{:S(2)}, u32[]{:S(2)}) async-start(f32[16,40,128]{2,1,0:T(8,128)} %shard_map.80), calls=%async_computation.1 | async-start | bytes 655360 | tf_op jit(solution)/shard_map/all_to_all | solution.py:559
  59.6 0.7 copy-start.2
  69.1 7.3 %collective-permute-start.11 = (f32[512,128]{1,0:T(8,128)}, f32[512,128]{1,0:T(8,128)S(1)}, u32[]{:S(2)}, u32[]{:S(2)}) collective-permute-start(f32[512,128]{1,0:T(8,128)} %get-tuple-element.64.refs_1_), channel_id=1, source_target_pairs={{0,224},{32,0},{64,32},{96,64},{128,96},{160,128},{192,160},{224,1... | collective-permute-start | bytes 786440 | tf_op jit(solution)/shard_map/ppermute | solution.py:40
  69.7 7.0 %collective-permute-start.10 = (f32[512,128]{1,0:T(8,128)}, f32[512,128]{1,0:T(8,128)S(1)}, u32[]{:S(2)}, u32[]{:S(2)}) collective-permute-start(f32[512,128]{1,0:T(8,128)} %get-tuple-element.65.refs_2_), channel_id=1, source_target_pairs={{0,32},{32,64},{64,96},{96,128},{128,160},{160,192},{192,224},{224... | collective-permute-start | bytes 786440 | tf_op jit(solution)/shard_map/ppermute | solution.py:40
  70.6 6.6 %collective-permute-start.13 = (f32[512,128]{1,0:T(8,128)}, f32[512,128]{1,0:T(8,128)S(1)}, u32[]{:S(2)}, u32[]{:S(2)}) collective-permute-start(f32[512,128]{1,0:T(8,128)} %get-tuple-element.66.refs_3_), channel_id=1, source_target_pairs={{0,31},{1,0},{2,1},{3,2},{4,3},{5,4},{6,5},{7,6},{8,7},{9,8},{10,9... | collective-permute-start | bytes 786440 | tf_op jit(solution)/shard_map/ppermute | solution.py:40
  72.7 4.5 %collective-permute-start.12 = (f32[512,128]{1,0:T(8,128)}, f32[512,128]{1,0:T(8,128)S(1)}, u32[]{:S(2)}, u32[]{:S(2)}) collective-permute-start(f32[512,128]{1,0:T(8,128)} %get-tuple-element.67.refs_4_), channel_id=1, source_target_pairs={{0,1},{1,2},{2,3},{3,4},{4,5},{5,6},{6,7},{7,8},{8,9},{9,10},{10,1... | collective-permute-start | bytes 786440 | tf_op jit(solution)/shard_map/ppermute | solution.py:40
  72.7 12.1 %all-to-all-start.2 = ((f32[8,40,128]{2,1,0:T(8,128)}), f32[8,40,128]{2,1,0:T(8,128)S(1)}, u32[]{:S(2)}, u32[]{:S(2)}) async-start(f32[8,40,128]{2,1,0:T(8,128)} %get-tuple-element.63), calls=%async_computation.2 | async-start | bytes 327680 | tf_op jit(solution)/shard_map/all_to_all | solution.py:541
  76.4 11.8 %copy-start.1 = (bf16[2,640,256]{2,1,0:T(8,128)(2,1)S(1)}, bf16[2,640,256]{2,1,0:T(8,128)(2,1)}, u32[]{:S(2)}) copy-start(bf16[2,640,256]{2,1,0:T(8,128)(2,1)} %shard_map.79.parts) | copy-start | bytes 1966084
  76.4 0.8 copy-start.13
  76.7 0.7 copy-start.15
  77.2 0.7 copy-start.17
  77.9 0.7 copy-start.19
  84.8 3.4 %collective-permute-start.14 = (f32[8,40,128]{2,1,0:T(8,128)S(1)}, f32[8,40,128]{2,1,0:T(8,128)S(1)}, u32[]{:S(2)}, u32[]{:S(2)}) collective-permute-start(f32[8,40,128]{2,1,0:T(8,128)S(1)} %all-to-all-done.2.own_v), channel_id=1, source_target_pairs={{0,1},{1,0},{2,3},{3,2},{4,5},{5,4},{6,7},{7,6},{8,9},{9,8},{10,11... | collective-permute-start | bytes 491528 | tf_op jit(solution)/shard_map/ppermute | solution.py:50
  109.8 7.8 %collective-permute-start.16 = (f32[512,128]{1,0:T(8,128)}, f32[512,128]{1,0:T(8,128)S(1)}, u32[]{:S(2)}, u32[]{:S(2)}) collective-permute-start(f32[512,128]{1,0:T(8,128)} %get-tuple-element.73.refs_1_), channel_id=1, source_target_pairs={{0,224},{32,0},{64,32},{96,64},{128,96},{160,128},{192,160},{224,1... | collective-permute-start | bytes 786440 | tf_op jit(solution)/shard_map/ppermute | solution.py:40
  110.9 7.5 %collective-permute-start.15 = (f32[512,128]{1,0:T(8,128)}, f32[512,128]{1,0:T(8,128)S(1)}, u32[]{:S(2)}, u32[]{:S(2)}) collective-permute-start(f32[512,128]{1,0:T(8,128)} %get-tuple-element.74.refs_2_), channel_id=1, source_target_pairs={{0,32},{32,64},{64,96},{96,128},{128,160},{160,192},{192,224},{224... | collective-permute-start | bytes 786440 | tf_op jit(solution)/shard_map/ppermute | solution.py:40
  111.3 7.2 %collective-permute-start.18 = (f32[512,128]{1,0:T(8,128)}, f32[512,128]{1,0:T(8,128)S(1)}, u32[]{:S(2)}, u32[]{:S(2)}) collective-permute-start(f32[512,128]{1,0:T(8,128)} %get-tuple-element.75.refs_3_), channel_id=1, source_target_pairs={{0,31},{1,0},{2,1},{3,2},{4,3},{5,4},{6,5},{7,6},{8,7},{9,8},{10,9... | collective-permute-start | bytes 786440 | tf_op jit(solution)/shard_map/ppermute | solution.py:40
  114.0 4.5 %collective-permute-start.17 = (f32[512,128]{1,0:T(8,128)}, f32[512,128]{1,0:T(8,128)S(1)}, u32[]{:S(2)}, u32[]{:S(2)}) collective-permute-start(f32[512,128]{1,0:T(8,128)} %get-tuple-element.76.refs_4_), channel_id=1, source_target_pairs={{0,1},{1,2},{2,3},{3,4},{4,5},{5,6},{6,7},{7,8},{8,9},{9,10},{10,1... | collective-permute-start | bytes 786440 | tf_op jit(solution)/shard_map/ppermute | solution.py:40
  114.0 12.2 %all-to-all-start.4 = ((f32[8,40,128]{2,1,0:T(8,128)}), f32[8,40,128]{2,1,0:T(8,128)S(1)}, u32[]{:S(2)}, u32[]{:S(2)}) async-start(f32[8,40,128]{2,1,0:T(8,128)} %get-tuple-element.72), calls=%async_computation.4 | async-start | bytes 327680 | tf_op jit(solution)/shard_map/all_to_all | solution.py:541
  117.6 0.9 copy-start.14
  118.3 0.7 copy-start.16
  118.5 0.7 copy-start.18
  119.2 0.7 copy-start.20
  126.2 2.7 %collective-permute-start.19 = (f32[8,40,128]{2,1,0:T(8,128)S(1)}, f32[8,40,128]{2,1,0:T(8,128)S(1)}, u32[]{:S(2)}, u32[]{:S(2)}) collective-permute-start(f32[8,40,128]{2,1,0:T(8,128)S(1)} %all-to-all-done.4.own_v), channel_id=1, source_target_pairs={{0,1},{1,0},{2,3},{3,2},{4,5},{5,4},{6,7},{7,6},{8,9},{9,8},{10,11... | collective-permute-start | bytes 491528 | tf_op jit(solution)/shard_map/ppermute | solution.py:50
  151.2 6.2 %collective-permute-start.20 = (f32[512,128]{1,0:T(8,128)}, f32[512,128]{1,0:T(8,128)S(1)}, u32[]{:S(2)}, u32[]{:S(2)}) collective-permute-start(f32[512,128]{1,0:T(8,128)} %get-tuple-element.86), channel_id=1, source_target_pairs={{0,224},{32,0},{64,32},{96,64},{128,96},{160,128},{192,160},{224,1... | collective-permute-start | bytes 786440 | tf_op jit(solution)/shard_map/ppermute | solution.py:40
  151.6 6.7 %collective-permute-start.21 = (f32[512,128]{1,0:T(8,128)}, f32[512,128]{1,0:T(8,128)S(1)}, u32[]{:S(2)}, u32[]{:S(2)}) collective-permute-start(f32[512,128]{1,0:T(8,128)} %get-tuple-element.87), channel_id=1, source_target_pairs={{0,31},{1,0},{2,1},{3,2},{4,3},{5,4},{6,5},{7,6},{8,7},{9,8},{10,9... | collective-permute-start | bytes 786440 | tf_op jit(solution)/shard_map/ppermute | solution.py:40
  153.8 12.9 %all-to-all-start.6 = ((f32[8,40,128]{2,1,0:T(8,128)}), f32[8,40,128]{2,1,0:T(8,128)S(1)}, u32[]{:S(2)}, u32[]{:S(2)}) async-start(f32[8,40,128]{2,1,0:T(8,128)} %get-tuple-element.83), calls=%async_computation.6 | async-start | bytes 327680 | tf_op jit(solution)/shard_map/all_to_all | solution.py:541
  157.4 0.9 copy-start.21
  158.3 0.7 copy-start.22
  166.7 2.5 %collective-permute-start.22 = (f32[8,40,128]{2,1,0:T(8,128)S(1)}, f32[8,40,128]{2,1,0:T(8,128)S(1)}, u32[]{:S(2)}, u32[]{:S(2)}) collective-permute-start(f32[8,40,128]{2,1,0:T(8,128)S(1)} %all-to-all-done.6.own_v), channel_id=1, source_target_pairs={{0,1},{1,0},{2,3},{3,2},{4,5},{5,4},{6,7},{7,6},{8,9},{9,8},{10,11... | collective-permute-start | bytes 491528 | tf_op jit(solution)/shard_map/ppermute | solution.py:50

commit v4 on v3

--- a/solution.py
+++ b/solution.py
@@ -20,8 +20,9 @@
 SLOTS = 5
 PAY = 40
 ROWS16 = 48
-TERMS = ((0, 0), (0, 1), (1, 0), (1, 1), (0, 2), (2, 0))
+TERMS = ((0, 0), (0, 1), (1, 0))
 TALL = 1024
+PART = 512
 CHIPS = 16
 HALF = COLS // 2
 COST = 2 * 10**10
@@ -141,14 +142,13 @@
         for block in range(M // BLK):
             lanes = slice(M * slot + BLK * block, M * slot + BLK * (block + 1))
             full[rows, lanes] = near[block] * -masks[slot]
-    pieces = parts_of(full[...], 3)
+    pieces = parts_of(full[...], 2)
     for index, (which, _) in enumerate(TERMS):
         turned[40 * index : 40 * (index + 1), :] = pieces[which][0:40].astype(f32)
-    turned[240:256, :] = jnp.zeros((16, NS), f32)
+    turned[120:128, :] = jnp.zeros((8, NS), f32)
     for block in range(NB):
-        for half in range(2):
-            piece = turned[BLK * half : BLK * (half + 1), BLK * block : BLK * (block + 1)].T
-            bgc_v[BLK * block : BLK * (block + 1), BLK * half : BLK * (half + 1)] = piece.astype(bf16)
+        piece = turned[:, BLK * block : BLK * (block + 1)].T
+        bgc_v[BLK * block : BLK * (block + 1), :] = piece.astype(bf16)
     copies.out(bgc_v, bgc)
     for block in range(NB):
         at = pl.multiple_of(order[block] * BLK, BLK)
@@ -184,14 +184,10 @@
             m = (mine_v[two], down_v[two], up_v[two])[line]
             on_left = (core[0] == 0) == (slot < 3)
             pairs = ((jnp.where(first, w, f), jnp.where(first, m, w)), (jnp.where(first, e, m), jnp.where(first, f, e)))
-            turned = [
-                jnp.where(
-                    half,
-                    jnp.where(on_left, a, pltpu.roll(a, SLOT * ROWS, 1)),
-                    jnp.where(on_left, pltpu.roll(b, SLOT * ROWS, 1), b),
-                )
-                for a, b in pairs
-            ]
+            turned = []
+            for a, b in pairs:
+                across = pltpu.roll(jnp.where(on_left, b, a), SLOT * ROWS, 1)
+                turned.append(jnp.where(half, jnp.where(on_left, a, across), jnp.where(on_left, across, b)))
             rows = pl.ds(pl.multiple_of((target * SLOTS + slot) * SLOT, SLOT), SLOT)
             table[rows, :K] = turned[0]
             table[rows, K:] = turned[1]
@@ -245,10 +241,10 @@
     for index in range(1, CHIPS):
         value = value + came[index]
     spare = lax.broadcasted_iota(jnp.int32, (SLOT * SLOTS, K), 0) % SLOT >= MODES
-    pieces = parts_of(jnp.where(spare, 0.0, value), 3)
+    pieces = parts_of(jnp.where(spare, 0.0, value), 2)
     for index, (_, right) in enumerate(TERMS):
         stack[40 * index : 40 * (index + 1), :] = pieces[right].astype(f32)
-    stack[240:256, :] = jnp.zeros((16, K), f32)
+    stack[120:128, :] = jnp.zeros((8, K), f32)
     return stack[...].astype(bf16), (value[6:7], value[7:8], value[14:15])
 
 
@@ -285,15 +281,16 @@
     def __init__(self, source, held, sems):
         self.source, self.held, self.sems = source, held, sems
 
-    def copy(self, step):
-        rows = pl.ds(TALL * step if isinstance(step, int) else pl.multiple_of(step * TALL, TALL), TALL)
-        return pltpu.make_async_copy(self.source.at[rows], self.held.at[rows], self.sems.at[step])
-
-    def start(self, step):
-        self.copy(step).start()
+    def copy(self, part):
+        rows = pl.ds(PART * part if isinstance(part, int) else pl.multiple_of(part * PART, PART), PART)
+        return pltpu.make_async_copy(self.source.at[rows], self.held.at[rows], self.sems.at[part])
+
+    def start(self, part):
+        self.copy(part).start()
 
     def wait(self, step):
-        self.copy(step).wait()
+        for part in range(TALL // PART):
+            self.copy(step * (TALL // PART) + part).wait()
 
 
 def put_halves(value, halves, at):
@@ -320,17 +317,19 @@
 
 
 def begin_kernel(
-    order, matrix, bgt, bgc, came_v, own, other, residual, yn, ys, yw, ye, pay,
-    inverse, held, bgt_v, bgc_v, _, r_v, halves, product, spread, stack, pay_v, sems, tall_sems,
+    order, matrix, bgt, bgc, came, own, other, residual, yn, ys, yw, ye, pay,
+    inverse, held, bgt_v, bgc_v, came_v, r_v, halves, product, spread, stack, pay_v, sems, tall_sems,
 ):
     copies, matrix = Copies(sems), Matrix(matrix, held, tall_sems)
-    head = [copies.start(bgc, bgc_v)]
+    head = [copies.start(came, came_v), copies.start(bgc, bgc_v)]
     body = [copies.start((other, own)[face % 2].at[face // 2], r_v.at[pl.ds(M * face, M)]) for face in range(4)]
     matrix.start(0)
+    matrix.start(1)
     turn = [copies.start(bgt, bgt_v)]
     invert(order, inverse)
     wait(head)
-    matrix.start(1)
+    matrix.start(2)
+    matrix.start(3)
     stacked, _ = take_values(came_v, stack)
     norm = jnp.zeros((SLOT, K), f32)
     for face in range(4):
@@ -406,6 +405,7 @@
 
     body = [fetch(0)]
     matrix.start(0)
+    matrix.start(1)
     invert(order, inverse)
 
     wait(head)
@@ -453,7 +453,8 @@
 
         carry = lax.fori_loop(0, M // BLK, block, carry)
         if pair == 0:
-            matrix.start(1)
+            matrix.start(2)
+            matrix.start(3)
         for source, target in ((r_v, new_residual), (moved_v, new_moved)):
             copies.out(source.at[wide], target.at[wide])
     value, energy = schur_product(order, copies, matrix, turn, bgt_v, r_v, halves, product)
@@ -502,21 +503,21 @@
     pltpu.SMEM((NB,), jnp.int32),
     pltpu.VMEM((NS, NS), bf16),
     pltpu.VMEM((2 * ROWS16, NS), bf16),
-    pltpu.VMEM((NS, 2 * K), bf16),
+    pltpu.VMEM((NS, K), bf16),
     pltpu.VMEM((CHIPS, SLOTS * SLOT, K), f32),
     pltpu.VMEM((NS, K), f32),
     pltpu.VMEM((NS, 2 * K), bf16),
     pltpu.VMEM((NS, K), f32),
     pltpu.VMEM((2 * M, K), f32),
-    pltpu.VMEM((256, K), f32),
+    pltpu.VMEM((K, K), f32),
     pltpu.VMEM((PAY, K), f32),
     pltpu.SemaphoreType.DMA((64,)),
-    pltpu.SemaphoreType.DMA((NS // TALL,)),
+    pltpu.SemaphoreType.DMA((NS // PART,)),
 ]
 MORE = [pltpu.VMEM((4, M, K), f32), pltpu.VMEM((NS, K), f32), pltpu.VMEM((2 * M, K), f32)]
 MORE += [pltpu.VMEM((SLOT, K), f32)] * 2
 LAST = (
-    [pltpu.VMEM((256, K), f32), pltpu.VMEM((2 * M, 2 * K), bf16), pltpu.VMEM((CHIPS, SLOTS * SLOT, K), f32)]
+    [pltpu.VMEM((K, K), f32), pltpu.VMEM((2 * M, K), bf16), pltpu.VMEM((CHIPS, SLOTS * SLOT, K), f32)]
     + [pltpu.VMEM((SLOT, K), f32)]
     + [pltpu.VMEM((2 * M, K), f32)] * 5
     + [pltpu.VMEM((2, K, M), f32)] * 2
@@ -616,13 +617,13 @@
     bgt, bgc, other = call(
         modes_kernel,
         [SM] * 2 + [HB] * 7,
-        [shape(2 * ROWS16, NS, kind=bf16), shape(NS, 2 * K, kind=bf16), shape(2, M, K)],
+        [shape(2 * ROWS16, NS, kind=bf16), shape(NS, K, kind=bf16), shape(2, M, K)],
         [pltpu.VMEM((tiles, SLOT, BLK), f32) for tiles in (NB, 4, 4, 4, 4)]
         + [
             pltpu.VMEM((ROWS16, NS), f32),
-            pltpu.VMEM((256, NS), f32),
+            pltpu.VMEM((K, NS), f32),
             pltpu.VMEM((2 * ROWS16, NS), bf16),
-            pltpu.VMEM((NS, 2 * K), bf16),
+            pltpu.VMEM((NS, K), bf16),
             pltpu.VMEM((2, K, M), f32),
             pltpu.VMEM((2, M, K), f32),
             pltpu.SemaphoreType.DMA((16,)),
@@ -635,7 +636,7 @@
     matrix = schur_blocks[0, 0]
     residual, *faces, pay = call(
         begin_kernel,
-        [SM] + [HB] * 3 + [VM] + [HB] * 2,
+        [SM] + [HB] * 6,
         [shape(NS, K)] + FACES + [shape(ROWS, PAY, K)],
         WORK,
         2 * 10**9,

time: 186 us -> 186 us (level)
  no operation moved by 1% of the time
where the time goes in v4:
time: 186 us; the launch traced here: 185 us
  starting transfers between devices  59.4 us (32%)
  Pallas kernels  52.3 us (28%)
  blocking collectives  34.9 us (19%)
  waiting for transfers between devices  24.2 us (13%)
  local copies, waits for them, and re-layouts  10.1 us (5%)
  between operations  1.89 us (1%)
    all_to_all x3, blocking collectives, coarse_phase(): lax.all_to_all(terms, 'col', 0, 0, axis_index_groups=groups, tiled=True)  34.9 us
    ppermute x18, starting transfers between devices, cyclic(): lax.ppermute(value, axis, [(s, (s + steps) % count) for s in range(count)])  25.8 us
    pallas_call x2, Pallas kernels, per_device(): call(functools.partial(step_kernel, first), [SM] + [HB] * (len(given) - 1...  18.6 us
    ppermute x5, starting transfers between devices, swapped(): return lax.ppermute(value, 'col', [(s, partner(s)) for s in range(COLS)])  15.5 us
    all_to_all x4, starting transfers between devices, coarse_phase(): own = lax.all_to_all(pay, 'row', 0, 0, tiled=True)  14.6 us
    all_to_all x4, waiting for transfers between devices, coarse_phase(): own = lax.all_to_all(pay, 'row', 0, 0, tiled=True)  10.5 us
    pallas_call x3, Pallas kernels, per_device(): call(functools.partial(image_kernel, which), [SM] + [HB] * (2 * len(which...  8.79 us
    pallas_call x1, Pallas kernels, per_device(): call(begin_kernel, [SM] + [HB] * 6, [shape(NS, K)] + FACES + [shape(ROWS,...  8.37 us
  transfers between devices with their start and end apart: 28, of which 14 were waited for; matrix products, arithmetic and copies ran while one was open for 2% of the time, Pallas kernels for 10%

profile of v4, /device:TPU:1, one launch (start us, length us, event | category | flops | bytes accessed | tf_op | source)
XLA Modules:
  0.0 184.6 jit_solution(15187849151386131171)
XLA Ops:
  1.3 0.8 broadcast_multiply_fusion
  2.2 6.5 %collective-permute-start.2 = (f32[4,8,128]{2,1,0:T(8,128)S(1)}, f32[4,8,128]{2,1,0:T(8,128)S(1)}, u32[]{:S(2)}, u32[]{:S(2)}) collective-permute-start(f32[4,8,128]{2,1,0:T(8,128)S(1)} %get-tuple-element.102), channel_id=1, source_target_pairs={{0,224},{32,0},{64,32},{96,64},{128,96},{160,128},{192,160},{224,1... | collective-permute-start | bytes 49160 | tf_op jit(solution)/shard_map/ppermute | solution.py:41
  8.6 1.0 collective-permute-start.3
  9.6 1.1 slice_bitcast_fusion
  10.7 1.3 collective-permute-start.7
  11.9 1.3 copy.14
  13.8 0.8 collective-permute-start.1
  14.7 0.8 collective-permute-start
  16.1 0.6 pad.8.own
  17.4 3.0 %shard_map.77 = (f32[2,512,128]{2,1,0:T(8,128)}, f32[8,40,128]{2,1,0:T(8,128)}) custom-call(f32[4]{0:T(128)} %add_convert_fusion.masks.refs_0_, f32[16,8,128]{2,1,0:T(8,128)} %pad.8.own, f32[4,8,128]{2,1,0:T(8,128)} %copy-done.9, f32[4,8,128]{2,1,0:T(8,128)} %copy-done.10, f32[2,128,512]{2,1,0:T(8,128)} %bitcast.35), custom_call_target="tpu_custom_call" | custom-call | flops 100000000 | bytes 1048576 | tf_op jit(solution)/shard_map/pallas_call | solution.py:574
  20.5 1.7 collective-permute-start.4
  22.3 2.8 %collective-permute-start.5 = (f32[48,8,128]{2,1,0:T(8,128)S(1)}, f32[48,8,128]{2,1,0:T(8,128)S(1)}, u32[]{:S(2)}, u32[]{:S(2)}) collective-permute-start(f32[48,8,128]{2,1,0:T(8,128)S(1)} %pad_maximum_fusion.1), channel_id=1, source_target_pairs={{0,31},{1,0},{2,1},{3,2},{4,3},{5,4},{6,5},{7,6},{8,7},{9,8},{10,9... | collective-permute-start | bytes 589832 | tf_op jit(solution)/shard_map/ppermute | solution.py:41
  25.1 4.1 %all-to-all-start = ((f32[8,40,128]{2,1,0:T(8,128)}), f32[8,40,128]{2,1,0:T(8,128)S(1)}, u32[]{:S(2)}, u32[]{:S(2)}) async-start(f32[8,40,128]{2,1,0:T(8,128)} %get-tuple-element.57), calls=%async_computation | async-start | bytes 327680 | tf_op jit(solution)/shard_map/all_to_all | solution.py:542
  29.3 5.4 %collective-permute-start.8 = (f32[48,8,128]{2,1,0:T(8,128)S(1)}, f32[48,8,128]{2,1,0:T(8,128)S(1)}, u32[]{:S(2)}, u32[]{:S(2)}) collective-permute-start(f32[48,8,128]{2,1,0:T(8,128)S(1)} %slice_select_fusion), channel_id=1, source_target_pairs={{0,1},{1,0},{2,3},{3,2},{4,5},{5,4},{6,7},{7,6},{8,9},{9,8},{10,11... | collective-permute-start | bytes 589832 | tf_op jit(solution)/shard_map/ppermute | solution.py:51
  34.7 1.1 collective-permute-done.8.far
  35.8 0.6 copy-done.8
  36.4 3.7 %shard_map.79.parts = bf16[2,640,256]{2,1,0:T(8,128)(2,1)} custom-call(s32[1]{0:T(128)} %bitcast.15.core, f32[16,8,128]{2,1,0:T(8,128)} %copy-done.7, f32[20,8,128]{2,1,0:T(8,128)} %copy-done.6, f32[16,8,128]{2,1,0:T(8,128)} %copy-done.5, f32[52,8,128]{2,1,0:T(8,128)} %copy-done.3, f32[48,8,128]{2,1,0:T(8,128)} %copy-done.4, f32[48,8,128]{2,1,0:T(8,128)} %copy-done.8), custom_call_target="tpu_custom_call" | custom-call | flops 1000000 | bytes 1048576 | tf_op jit(solution)/shard_map/pallas_call | solution.py:604
  40.1 3.8 %collective-permute-start.9 = (f32[8,40,128]{2,1,0:T(8,128)S(1)}, f32[8,40,128]{2,1,0:T(8,128)S(1)}, u32[]{:S(2)}, u32[]{:S(2)}) collective-permute-start(f32[8,40,128]{2,1,0:T(8,128)S(1)} %all-to-all-done.own_v), channel_id=1, source_target_pairs={{0,1},{1,0},{2,3},{3,2},{4,5},{5,4},{6,7},{7,6},{8,9},{9,8},{10,11... | collective-permute-start | bytes 491528 | tf_op jit(solution)/shard_map/ppermute | solution.py:51
  43.9 1.0 collective-permute-done.9.other_v
  45.0 1.1 copy-done
  46.1 1.4 shard_map.80
  47.4 3.6 %all-to-all-start.1 = ((f32[16,40,128]{2,1,0:T(8,128)}), f32[16,40,128]{2,1,0:T(8,128)S(1)}, u32[]{:S(2)}, u32[]{:S(2)}) async-start(f32[16,40,128]{2,1,0:T(8,128)} %shard_map.80), calls=%async_computation.1 | async-start | bytes 655360 | tf_op jit(solution)/shard_map/all_to_all | solution.py:560
  51.0 3.0 %shard_map.78 = (bf16[96,2048]{1,0:T(8,128)(2,1)}, bf16[2048,128]{1,0:T(8,128)(2,1)}, f32[2,512,128]{2,1,0:T(8,128)}) custom-call(s32[16]{0:T(128)} %bitcast.40, f32[4]{0:T(128)} %add_convert_fusion.masks.refs_0_, f32[16,8,128]{2,1,0:T(8,128)} %pad.8.own, f32[20,8,128]{2,1,0:T(8,128)} %copy-done.6, f32[4,8,128]{2,1,0:T(8,128)} %copy-done.9, ...), custom_call_target="tpu_custom_call" | custom-call | flops 20000000000 | bytes 1048576 | tf_op jit(solution)/shard_map/pallas_call | solution.py:617
  54.0 5.6 %all-to-all-done.1.came = f32[16,40,128]{2,1,0:T(8,128)S(1)} async-done(((f32[16,40,128]{2,1,0:T(8,128)}), f32[16,40,128]{2,1,0:T(8,128)S(1)}, u32[]{:S(2)}, u32[]{:S(2)}) %all-to-all-start.1) | async-done | bytes 327712 | tf_op jit(solution)/shard_map/all_to_all | solution.py:560
  59.6 0.7 copy-done.2
  60.3 8.4 %shard_map.81 = (f32[2048,128]{1,0:T(8,128)}, f32[512,128]{1,0:T(8,128)}, f32[512,128]{1,0:T(8,128)}, f32[512,128]{1,0:T(8,128)}, f32[512,128]{1,0:T(8,128)}, /*index=5*/f32[8,40,128]{2,1,0:T(8,128)}) custom-call(s32[16]{0:T(128)} %bitcast.41, bf16[2048,2048]{1,0:T(8,128)(2,1)} %bitcast.32, bf16[96,2048]{1,0:T(8,128)(2,1)} %get-tuple-element.56.bgt.refs_2_, ...), custom_call_target="tpu_custom_call" | custom-call | flops 2000000000 | bytes 1048576 | tf_op jit(solution)/shard_map/pallas_call | solution.py:637
  68.7 0.7 collective-permute-start.11
  69.3 1.1 collective-permute-start.10
  70.4 2.0 %collective-permute-start.13 = (f32[512,128]{1,0:T(8,128)}, f32[512,128]{1,0:T(8,128)S(1)}, u32[]{:S(2)}, u32[]{:S(2)}) collective-permute-start(f32[512,128]{1,0:T(8,128)} %get-tuple-element.66.refs_3_), channel_id=1, source_target_pairs={{0,31},{1,0},{2,1},{3,2},{4,3},{5,4},{6,5},{7,6},{8,7},{9,8},{10,9... | collective-permute-start | bytes 786440 | tf_op jit(solution)/shard_map/ppermute | solution.py:41
  72.5 3.6 %all-to-all-start.2 = ((f32[8,40,128]{2,1,0:T(8,128)}), f32[8,40,128]{2,1,0:T(8,128)S(1)}, u32[]{:S(2)}, u32[]{:S(2)}) async-start(f32[8,40,128]{2,1,0:T(8,128)} %get-tuple-element.63), calls=%async_computation.2 | async-start | bytes 327680 | tf_op jit(solution)/shard_map/all_to_all | solution.py:542
  76.3 0.6 collective-permute-done.13.refs_8_
  77.0 0.7 copy-done.17
  77.7 0.7 copy-done.19
  78.4 3.0 %shard_map.82.refs_6_.refs_9_ = f32[4,512,128]{2,1,0:T(8,128)} custom-call(f32[4]{0:T(128)} %add_convert_fusion.masks.refs_0_, f32[512,128]{1,0:T(8,128)} %get-tuple-element.64.refs_1_, f32[512,128]{1,0:T(8,128)} %get-tuple-element.65.refs_2_, f32[512,128]{1,0:T(8,128)} %get-tuple-element.66.refs_3_, f32[512,128]{1,0:T(8,128)} %get-tuple-element.67.refs_4_, ...), custom_call_target="tpu_custom_call" | custom-call | flops 20000000000 | bytes 1048576 | tf_op jit(solution)/shard_map/pallas_call | solution.py:652
  81.5 2.9 %all-to-all-done.2.own_v = f32[8,40,128]{2,1,0:T(8,128)S(1)} async-done(((f32[8,40,128]{2,1,0:T(8,128)}), f32[8,40,128]{2,1,0:T(8,128)S(1)}, u32[]{:S(2)}, u32[]{:S(2)}) %all-to-all-start.2) | async-done | bytes 163872 | tf_op jit(solution)/shard_map/all_to_all | solution.py:542
  84.4 2.3 %collective-permute-start.14 = (f32[8,40,128]{2,1,0:T(8,128)S(1)}, f32[8,40,128]{2,1,0:T(8,128)S(1)}, u32[]{:S(2)}, u32[]{:S(2)}) collective-permute-start(f32[8,40,128]{2,1,0:T(8,128)S(1)} %all-to-all-done.2.own_v), channel_id=1, source_target_pairs={{0,1},{1,0},{2,3},{3,2},{4,5},{5,4},{6,7},{7,6},{8,9},{9,8},{10,11... | collective-permute-start | bytes 491528 | tf_op jit(solution)/shard_map/ppermute | solution.py:51
  86.7 1.0 collective-permute-done.14.other_v
  87.8 0.7 shard_map.83
  88.5 11.8 %all_to_all.40.refs_4_ = f32[16,40,128]{2,1,0:T(8,128)} all-to-all(f32[16,40,128]{2,1,0:T(8,128)S(1)} %shard_map.83), channel_id=1, replica_groups={{0,2,4,6,8,10,12,14,16,18,20,22,24,26,28,30},{1,3,5,7,9,11,13,15,17,19,..., dimensions={0} | all-to-all | bytes 655360 | tf_op jit(solution)/shard_map/all_to_all | solution.py:560
  100.4 9.3 %shard_map.84 = (f32[2048,128]{1,0:T(8,128)}, f32[2048,128]{1,0:T(8,128)}, f32[8,128]{1,0:T(8,128)}, f32[512,128]{1,0:T(8,128)}, f32[512,128]{1,0:T(8,128)}, /*i...) custom-call(s32[16]{0:T(128)} %bitcast.42, bf16[2048,2048]{1,0:T(8,128)(2,1)} %bitcast.33, ...), custom_call_target="tpu_custom_call" | custom-call | flops 2000000000 | bytes 1048576 | tf_op jit(solution)/shard_map/pallas_call | solution.py:665
  109.6 1.1 collective-permute-start.16
  111.2 2.7 %collective-permute-start.18 = (f32[512,128]{1,0:T(8,128)}, f32[512,128]{1,0:T(8,128)S(1)}, u32[]{:S(2)}, u32[]{:S(2)}) collective-permute-start(f32[512,128]{1,0:T(8,128)} %get-tuple-element.75.refs_3_), channel_id=1, source_target_pairs={{0,31},{1,0},{2,1},{3,2},{4,3},{5,4},{6,5},{7,6},{8,7},{9,8},{10,9... | collective-permute-start | bytes 786440 | tf_op jit(solution)/shard_map/ppermute | solution.py:41
  113.9 3.4 %all-to-all-start.4 = ((f32[8,40,128]{2,1,0:T(8,128)}), f32[8,40,128]{2,1,0:T(8,128)S(1)}, u32[]{:S(2)}, u32[]{:S(2)}) async-start(f32[8,40,128]{2,1,0:T(8,128)} %get-tuple-element.72), calls=%async_computation.4 | async-start | bytes 327680 | tf_op jit(solution)/shard_map/all_to_all | solution.py:542
  117.3 0.9 collective-permute-done.15.refs_5_
  119.1 0.7 copy-done.20
  119.8 3.1 %shard_map.85.refs_6_ = f32[4,512,128]{2,1,0:T(8,128)} custom-call(f32[4]{0:T(128)} %add_convert_fusion.masks.refs_0_, f32[512,128]{1,0:T(8,128)} %get-tuple-element.73.refs_1_, f32[512,128]{1,0:T(8,128)} %get-tuple-element.74.refs_2_, f32[512,128]{1,0:T(8,128)} %get-tuple-element.75.refs_3_, f32[512,128]{1,0:T(8,128)} %get-tuple-element.76.refs_4_, ...), custom_call_target="tpu_custom_call" | custom-call | flops 20000000000 | bytes 1048576 | tf_op jit(solution)/shard_map/pallas_call | solution.py:652
  122.9 2.6 %all-to-all-done.4.own_v = f32[8,40,128]{2,1,0:T(8,128)S(1)} async-done(((f32[8,40,128]{2,1,0:T(8,128)}), f32[8,40,128]{2,1,0:T(8,128)S(1)}, u32[]{:S(2)}, u32[]{:S(2)}) %all-to-all-start.4) | async-done | bytes 163872 | tf_op jit(solution)/shard_map/all_to_all | solution.py:542
  125.4 2.4 %collective-permute-start.19 = (f32[8,40,128]{2,1,0:T(8,128)S(1)}, f32[8,40,128]{2,1,0:T(8,128)S(1)}, u32[]{:S(2)}, u32[]{:S(2)}) collective-permute-start(f32[8,40,128]{2,1,0:T(8,128)S(1)} %all-to-all-done.4.own_v), channel_id=1, source_target_pairs={{0,1},{1,0},{2,3},{3,2},{4,5},{5,4},{6,7},{7,6},{8,9},{9,8},{10,11... | collective-permute-start | bytes 491528 | tf_op jit(solution)/shard_map/ppermute | solution.py:51
  127.9 1.0 collective-permute-done.19.other_v
  128.9 0.7 shard_map.86
  129.7 11.8 %all_to_all.41.refs_4_ = f32[16,40,128]{2,1,0:T(8,128)} all-to-all(f32[16,40,128]{2,1,0:T(8,128)S(1)} %shard_map.86), channel_id=1, replica_groups={{0,2,4,6,8,10,12,14,16,18,20,22,24,26,28,30},{1,3,5,7,9,11,13,15,17,19,..., dimensions={0} | all-to-all | bytes 655360 | tf_op jit(solution)/shard_map/all_to_all | solution.py:560
  141.5 9.4 %shard_map.87 = (f32[2048,128]{1,0:T(8,128)}, f32[2048,128]{1,0:T(8,128)}, f32[8,128]{1,0:T(8,128)}, f32[512,128]{1,0:T(8,128)}, f32[512,128]{1,0:T(8,128)}, /*i...) custom-call(s32[16]{0:T(128)} %bitcast.43, bf16[2048,2048]{1,0:T(8,128)(2,1)} %bitcast.34, ...), custom_call_target="tpu_custom_call" | custom-call | flops 2000000000 | bytes 1048576 | tf_op jit(solution)/shard_map/pallas_call | solution.py:665
  150.9 0.7 collective-permute-start.20
  151.6 2.2 %collective-permute-start.21 = (f32[512,128]{1,0:T(8,128)}, f32[512,128]{1,0:T(8,128)S(1)}, u32[]{:S(2)}, u32[]{:S(2)}) collective-permute-start(f32[512,128]{1,0:T(8,128)} %get-tuple-element.87), channel_id=1, source_target_pairs={{0,31},{1,0},{2,1},{3,2},{4,3},{5,4},{6,5},{7,6},{8,7},{9,8},{10,9... | collective-permute-start | bytes 786440 | tf_op jit(solution)/shard_map/ppermute | solution.py:41
  153.8 3.6 %all-to-all-start.6 = ((f32[8,40,128]{2,1,0:T(8,128)}), f32[8,40,128]{2,1,0:T(8,128)S(1)}, u32[]{:S(2)}, u32[]{:S(2)}) async-start(f32[8,40,128]{2,1,0:T(8,128)} %get-tuple-element.83), calls=%async_computation.6 | async-start | bytes 327680 | tf_op jit(solution)/shard_map/all_to_all | solution.py:542
  157.4 0.9 collective-permute-done.21.refs_4_
  158.3 0.7 copy-done.22
  159.0 2.7 %shard_map.88.local = f32[2,512,128]{2,1,0:T(8,128)} custom-call(f32[4]{0:T(128)} %add_convert_fusion.masks.refs_0_, f32[512,128]{1,0:T(8,128)} %get-tuple-element.84.refs_1_, f32[512,128]{1,0:T(8,128)} %get-tuple-element.85.refs_2_, f32[512,128]{1,0:T(8,128)} %copy-done.21, f32[512,128]{1,0:T(8,128)} %copy-done.22), custom_call_target="tpu_custom_call" | custom-call | flops 20000000000 | bytes 1048576 | tf_op jit(solution)/shard_map/pallas_call | solution.py:652
  161.7 4.9 %all-to-all-done.6.own_v = f32[8,40,128]{2,1,0:T(8,128)S(1)} async-done(((f32[8,40,128]{2,1,0:T(8,128)}), f32[8,40,128]{2,1,0:T(8,128)S(1)}, u32[]{:S(2)}, u32[]{:S(2)}) %all-to-all-start.6) | async-done | bytes 163872 | tf_op jit(solution)/shard_map/all_to_all | solution.py:542
  166.7 1.4 collective-permute-start.22
  168.1 1.0 collective-permute-done.22.other_v
  169.1 0.7 shard_map.89
  169.9 11.2 %all_to_all.42.came = f32[16,40,128]{2,1,0:T(8,128)} all-to-all(f32[16,40,128]{2,1,0:T(8,128)S(1)} %shard_map.89), channel_id=1, replica_groups={{0,2,4,6,8,10,12,14,16,18,20,22,24,26,28,30},{1,3,5,7,9,11,13,15,17,19,..., dimensions={0} | all-to-all | bytes 655360 | tf_op jit(solution)/shard_map/all_to_all | solution.py:560
  181.1 3.3 %shard_map.90 = (f32[2,128,512]{2,1,0:T(8,128)}, f32[2,128,512]{2,1,0:T(8,128)}) custom-call(bf16[2048,128]{1,0:T(8,128)(2,1)} %get-tuple-element.55.bgc.refs_3_, f32[16,40,128]{2,1,0:T(8,128)} %all_to_all.42.came, f32[2048,128]{1,0:T(8,128)} %get-tuple-element.90.residual, f32[2048,128]{1,0:T(8,128)} %get-tuple-element.70.refs_5_.first, ...), custom_call_target="tpu_custom_call" | custom-call | flops 100000000 | bytes 1048576 | tf_op jit(solution)/shard_map/pallas_call | solution.py:676
  (71 shorter events, 3.9 us)
Async XLA Ops:
  2.2 14.6 %collective-permute-start.2 = (f32[4,8,128]{2,1,0:T(8,128)S(1)}, f32[4,8,128]{2,1,0:T(8,128)S(1)}, u32[]{:S(2)}, u32[]{:S(2)}) collective-permute-start(f32[4,8,128]{2,1,0:T(8,128)S(1)} %get-tuple-element.102), channel_id=1, source_target_pairs={{0,224},{32,0},{64,32},{96,64},{128,96},{160,128},{192,160},{224,1... | collective-permute-start | bytes 49160 | tf_op jit(solution)/shard_map/ppermute | solution.py:41
  8.6 8.1 %collective-permute-start.3 = (f32[4,8,128]{2,1,0:T(8,128)S(1)}, f32[4,8,128]{2,1,0:T(8,128)S(1)}, u32[]{:S(2)}, u32[]{:S(2)}) collective-permute-start(f32[4,8,128]{2,1,0:T(8,128)S(1)} %get-tuple-element.103), channel_id=1, source_target_pairs={{0,31},{1,0},{2,1},{3,2},{4,3},{5,4},{6,5},{7,6},{8,7},{9,8},{10,9... | collective-permute-start | bytes 49160 | tf_op jit(solution)/shard_map/ppermute | solution.py:41
  10.7 18.5 %collective-permute-start.7 = (f32[128,512]{1,0:T(8,128)S(1)}, f32[128,512]{1,0:T(8,128)S(1)}, u32[]{:S(2)}, u32[]{:S(2)}) collective-permute-start(f32[128,512]{1,0:T(8,128)S(1)} %get-tuple-element.96), channel_id=1, source_target_pairs={{0,1},{1,2},{2,3},{3,4},{4,5},{5,6},{6,7},{7,8},{8,9},{9,10},{10,1... | collective-permute-start | bytes 786440 | tf_op jit(solution)/shard_map/ppermute | solution.py:41
  13.8 22.0 %copy-start.7 = (f32[16,8,128]{2,1,0:T(8,128)}, f32[16,8,128]{2,1,0:T(8,128)S(1)}, u32[]{:S(2)}) copy-start(f32[16,8,128]{2,1,0:T(8,128)S(1)} %pad_maximum_fusion.3.mine) | copy-start | bytes 196612
  13.8 6.5 %collective-permute-start.1 = (f32[16,8,128]{2,1,0:T(8,128)S(1)}, f32[16,8,128]{2,1,0:T(8,128)S(1)}, u32[]{:S(2)}, u32[]{:S(2)}) collective-permute-start(f32[16,8,128]{2,1,0:T(8,128)S(1)} %pad_maximum_fusion.3.mine), channel_id=1, source_target_pairs={{0,224},{32,0},{64,32},{96,64},{128,96},{160,128},{192,160},{224,1... | collective-permute-start | bytes 196616 | tf_op jit(solution)/shard_map/ppermute | solution.py:41
  14.7 5.7 %collective-permute-start = (f32[20,8,128]{2,1,0:T(8,128)S(1)}, f32[20,8,128]{2,1,0:T(8,128)S(1)}, u32[]{:S(2)}, u32[]{:S(2)}) collective-permute-start(f32[20,8,128]{2,1,0:T(8,128)S(1)} %pad_maximum_fusion.2), channel_id=1, source_target_pairs={{0,32},{32,64},{64,96},{96,128},{128,160},{160,192},{192,224},{224... | collective-permute-start | bytes 245768 | tf_op jit(solution)/shard_map/ppermute | solution.py:41
  16.7 0.6 copy-start.9
  16.7 12.4 %collective-permute-start.6 = (f32[128,512]{1,0:T(8,128)S(1)}, f32[128,512]{1,0:T(8,128)S(1)}, u32[]{:S(2)}, u32[]{:S(2)}) collective-permute-start(f32[128,512]{1,0:T(8,128)S(1)} %get-tuple-element.97), channel_id=1, source_target_pairs={{0,32},{32,64},{64,96},{96,128},{128,160},{160,192},{192,224},{224... | collective-permute-start | bytes 786440 | tf_op jit(solution)/shard_map/ppermute | solution.py:41
  16.8 0.6 copy-start.10
  20.4 15.4 %copy-start.5 = (f32[16,8,128]{2,1,0:T(8,128)}, f32[16,8,128]{2,1,0:T(8,128)S(1)}, u32[]{:S(2)}) copy-start(f32[16,8,128]{2,1,0:T(8,128)S(1)} %collective-permute-done.1.up) | copy-start | bytes 196612
  20.4 15.4 %copy-start.6 = (f32[20,8,128]{2,1,0:T(8,128)}, f32[20,8,128]{2,1,0:T(8,128)S(1)}, u32[]{:S(2)}) copy-start(f32[20,8,128]{2,1,0:T(8,128)S(1)} %collective-permute-done.down) | copy-start | bytes 245764
  20.5 8.7 %collective-permute-start.4 = (f32[52,8,128]{2,1,0:T(8,128)S(1)}, f32[52,8,128]{2,1,0:T(8,128)S(1)}, u32[]{:S(2)}, u32[]{:S(2)}) collective-permute-start(f32[52,8,128]{2,1,0:T(8,128)S(1)} %pad_maximum_fusion), channel_id=1, source_target_pairs={{0,1},{1,2},{2,3},{3,4},{4,5},{5,6},{6,7},{7,8},{8,9},{9,10},{10,1... | collective-permute-start | bytes 638984 | tf_op jit(solution)/shard_map/ppermute | solution.py:41
  22.3 6.9 %collective-permute-start.5 = (f32[48,8,128]{2,1,0:T(8,128)S(1)}, f32[48,8,128]{2,1,0:T(8,128)S(1)}, u32[]{:S(2)}, u32[]{:S(2)}) collective-permute-start(f32[48,8,128]{2,1,0:T(8,128)S(1)} %pad_maximum_fusion.1), channel_id=1, source_target_pairs={{0,31},{1,0},{2,1},{3,2},{4,3},{5,4},{6,5},{7,6},{8,7},{9,8},{10,9... | collective-permute-start | bytes 589832 | tf_op jit(solution)/shard_map/ppermute | solution.py:41
  25.1 15.0 %all-to-all-start = ((f32[8,40,128]{2,1,0:T(8,128)}), f32[8,40,128]{2,1,0:T(8,128)S(1)}, u32[]{:S(2)}, u32[]{:S(2)}) async-start(f32[8,40,128]{2,1,0:T(8,128)} %get-tuple-element.57), calls=%async_computation | async-start | bytes 327680 | tf_op jit(solution)/shard_map/all_to_all | solution.py:542
  29.2 21.8 %copy-start.11 = (f32[128,512]{1,0:T(8,128)}, f32[128,512]{1,0:T(8,128)S(1)}, u32[]{:S(2)}) copy-start(f32[128,512]{1,0:T(8,128)S(1)} %collective-permute-done.7.from_w) | copy-start | bytes 786436
  29.2 21.8 %copy-start.12 = (f32[128,512]{1,0:T(8,128)}, f32[128,512]{1,0:T(8,128)S(1)}, u32[]{:S(2)}) copy-start(f32[128,512]{1,0:T(8,128)S(1)} %collective-permute-done.6.from_n) | copy-start | bytes 786436
  29.2 6.6 %copy-start.4 = (f32[48,8,128]{2,1,0:T(8,128)}, f32[48,8,128]{2,1,0:T(8,128)S(1)}, u32[]{:S(2)}) copy-start(f32[48,8,128]{2,1,0:T(8,128)S(1)} %collective-permute-done.5.left) | copy-start | bytes 589828
  29.2 6.6 %copy-start.3 = (f32[52,8,128]{2,1,0:T(8,128)}, f32[52,8,128]{2,1,0:T(8,128)S(1)}, u32[]{:S(2)}) copy-start(f32[52,8,128]{2,1,0:T(8,128)S(1)} %collective-permute-done.4.right) | copy-start | bytes 638980
  29.3 6.5 %collective-permute-start.8 = (f32[48,8,128]{2,1,0:T(8,128)S(1)}, f32[48,8,128]{2,1,0:T(8,128)S(1)}, u32[]{:S(2)}, u32[]{:S(2)}) collective-permute-start(f32[48,8,128]{2,1,0:T(8,128)S(1)} %slice_select_fusion), channel_id=1, source_target_pairs={{0,1},{1,0},{2,3},{3,2},{4,5},{5,4},{6,7},{7,6},{8,9},{9,8},{10,11... | collective-permute-start | bytes 589832 | tf_op jit(solution)/shard_map/ppermute | solution.py:51
  35.8 0.7 copy-start.8
  40.1 4.8 %collective-permute-start.9 = (f32[8,40,128]{2,1,0:T(8,128)S(1)}, f32[8,40,128]{2,1,0:T(8,128)S(1)}, u32[]{:S(2)}, u32[]{:S(2)}) collective-permute-start(f32[8,40,128]{2,1,0:T(8,128)S(1)} %all-to-all-done.own_v), channel_id=1, source_target_pairs={{0,1},{1,0},{2,3},{3,2},{4,5},{5,4},{6,7},{7,6},{8,9},{9,8},{10,11... | collective-permute-start | bytes 491528 | tf_op jit(solution)/shard_map/ppermute | solution.py:51
  45.0 1.1 copy-start
  47.4 12.1 %all-to-all-start.1 = ((f32[16,40,128]{2,1,0:T(8,128)}), f32[16,40,128]{2,1,0:T(8,128)S(1)}, u32[]{:S(2)}, u32[]{:S(2)}) async-start(f32[16,40,128]{2,1,0:T(8,128)} %shard_map.80), calls=%async_computation.1 | async-start | bytes 655360 | tf_op jit(solution)/shard_map/all_to_all | solution.py:560
  59.6 0.7 copy-start.2
  68.7 7.3 %collective-permute-start.11 = (f32[512,128]{1,0:T(8,128)}, f32[512,128]{1,0:T(8,128)S(1)}, u32[]{:S(2)}, u32[]{:S(2)}) collective-permute-start(f32[512,128]{1,0:T(8,128)} %get-tuple-element.64.refs_1_), channel_id=1, source_target_pairs={{0,224},{32,0},{64,32},{96,64},{128,96},{160,128},{192,160},{224,1... | collective-permute-start | bytes 786440 | tf_op jit(solution)/shard_map/ppermute | solution.py:41
  69.3 7.0 %collective-permute-start.10 = (f32[512,128]{1,0:T(8,128)}, f32[512,128]{1,0:T(8,128)S(1)}, u32[]{:S(2)}, u32[]{:S(2)}) collective-permute-start(f32[512,128]{1,0:T(8,128)} %get-tuple-element.65.refs_2_), channel_id=1, source_target_pairs={{0,32},{32,64},{64,96},{96,128},{128,160},{160,192},{192,224},{224... | collective-permute-start | bytes 786440 | tf_op jit(solution)/shard_map/ppermute | solution.py:41
  70.4 6.6 %collective-permute-start.13 = (f32[512,128]{1,0:T(8,128)}, f32[512,128]{1,0:T(8,128)S(1)}, u32[]{:S(2)}, u32[]{:S(2)}) collective-permute-start(f32[512,128]{1,0:T(8,128)} %get-tuple-element.66.refs_3_), channel_id=1, source_target_pairs={{0,31},{1,0},{2,1},{3,2},{4,3},{5,4},{6,5},{7,6},{8,7},{9,8},{10,9... | collective-permute-start | bytes 786440 | tf_op jit(solution)/shard_map/ppermute | solution.py:41
  72.4 4.5 %collective-permute-start.12 = (f32[512,128]{1,0:T(8,128)}, f32[512,128]{1,0:T(8,128)S(1)}, u32[]{:S(2)}, u32[]{:S(2)}) collective-permute-start(f32[512,128]{1,0:T(8,128)} %get-tuple-element.67.refs_4_), channel_id=1, source_target_pairs={{0,1},{1,2},{2,3},{3,4},{4,5},{5,6},{6,7},{7,8},{8,9},{9,10},{10,1... | collective-permute-start | bytes 786440 | tf_op jit(solution)/shard_map/ppermute | solution.py:41
  72.5 11.9 %all-to-all-start.2 = ((f32[8,40,128]{2,1,0:T(8,128)}), f32[8,40,128]{2,1,0:T(8,128)S(1)}, u32[]{:S(2)}, u32[]{:S(2)}) async-start(f32[8,40,128]{2,1,0:T(8,128)} %get-tuple-element.63), calls=%async_computation.2 | async-start | bytes 327680 | tf_op jit(solution)/shard_map/all_to_all | solution.py:542
  76.0 11.8 %copy-start.1 = (bf16[2,640,256]{2,1,0:T(8,128)(2,1)S(1)}, bf16[2,640,256]{2,1,0:T(8,128)(2,1)}, u32[]{:S(2)}) copy-start(bf16[2,640,256]{2,1,0:T(8,128)(2,1)} %shard_map.79.parts) | copy-start | bytes 1966084
  76.0 1.0 copy-start.13
  76.3 0.7 copy-start.15
  77.0 0.7 copy-start.17
  77.7 0.7 copy-start.19
  84.4 3.4 %collective-permute-start.14 = (f32[8,40,128]{2,1,0:T(8,128)S(1)}, f32[8,40,128]{2,1,0:T(8,128)S(1)}, u32[]{:S(2)}, u32[]{:S(2)}) collective-permute-start(f32[8,40,128]{2,1,0:T(8,128)S(1)} %all-to-all-done.2.own_v), channel_id=1, source_target_pairs={{0,1},{1,0},{2,3},{3,2},{4,5},{5,4},{6,7},{7,6},{8,9},{9,8},{10,11... | collective-permute-start | bytes 491528 | tf_op jit(solution)/shard_map/ppermute | solution.py:51
  109.6 7.6 %collective-permute-start.16 = (f32[512,128]{1,0:T(8,128)}, f32[512,128]{1,0:T(8,128)S(1)}, u32[]{:S(2)}, u32[]{:S(2)}) collective-permute-start(f32[512,128]{1,0:T(8,128)} %get-tuple-element.73.refs_1_), channel_id=1, source_target_pairs={{0,224},{32,0},{64,32},{96,64},{128,96},{160,128},{192,160},{224,1... | collective-permute-start | bytes 786440 | tf_op jit(solution)/shard_map/ppermute | solution.py:41
  110.7 7.4 %collective-permute-start.15 = (f32[512,128]{1,0:T(8,128)}, f32[512,128]{1,0:T(8,128)S(1)}, u32[]{:S(2)}, u32[]{:S(2)}) collective-permute-start(f32[512,128]{1,0:T(8,128)} %get-tuple-element.74.refs_2_), channel_id=1, source_target_pairs={{0,32},{32,64},{64,96},{96,128},{128,160},{160,192},{192,224},{224... | collective-permute-start | bytes 786440 | tf_op jit(solution)/shard_map/ppermute | solution.py:41
  111.2 7.2 %collective-permute-start.18 = (f32[512,128]{1,0:T(8,128)}, f32[512,128]{1,0:T(8,128)S(1)}, u32[]{:S(2)}, u32[]{:S(2)}) collective-permute-start(f32[512,128]{1,0:T(8,128)} %get-tuple-element.75.refs_3_), channel_id=1, source_target_pairs={{0,31},{1,0},{2,1},{3,2},{4,3},{5,4},{6,5},{7,6},{8,7},{9,8},{10,9... | collective-permute-start | bytes 786440 | tf_op jit(solution)/shard_map/ppermute | solution.py:41
  113.9 4.5 %collective-permute-start.17 = (f32[512,128]{1,0:T(8,128)}, f32[512,128]{1,0:T(8,128)S(1)}, u32[]{:S(2)}, u32[]{:S(2)}) collective-permute-start(f32[512,128]{1,0:T(8,128)} %get-tuple-element.76.refs_4_), channel_id=1, source_target_pairs={{0,1},{1,2},{2,3},{3,4},{4,5},{5,6},{6,7},{7,8},{8,9},{9,10},{10,1... | collective-permute-start | bytes 786440 | tf_op jit(solution)/shard_map/ppermute | solution.py:41
  113.9 11.6 %all-to-all-start.4 = ((f32[8,40,128]{2,1,0:T(8,128)}), f32[8,40,128]{2,1,0:T(8,128)S(1)}, u32[]{:S(2)}, u32[]{:S(2)}) async-start(f32[8,40,128]{2,1,0:T(8,128)} %get-tuple-element.72), calls=%async_computation.4 | async-start | bytes 327680 | tf_op jit(solution)/shard_map/all_to_all | solution.py:542
  117.3 1.1 copy-start.14
  118.2 0.7 copy-start.16
  118.4 0.7 copy-start.18
  119.1 0.7 copy-start.20
  125.4 3.5 %collective-permute-start.19 = (f32[8,40,128]{2,1,0:T(8,128)S(1)}, f32[8,40,128]{2,1,0:T(8,128)S(1)}, u32[]{:S(2)}, u32[]{:S(2)}) collective-permute-start(f32[8,40,128]{2,1,0:T(8,128)S(1)} %all-to-all-done.4.own_v), channel_id=1, source_target_pairs={{0,1},{1,0},{2,3},{3,2},{4,5},{5,4},{6,7},{7,6},{8,9},{9,8},{10,11... | collective-permute-start | bytes 491528 | tf_op jit(solution)/shard_map/ppermute | solution.py:51
  150.9 6.5 %collective-permute-start.20 = (f32[512,128]{1,0:T(8,128)}, f32[512,128]{1,0:T(8,128)S(1)}, u32[]{:S(2)}, u32[]{:S(2)}) collective-permute-start(f32[512,128]{1,0:T(8,128)} %get-tuple-element.86), channel_id=1, source_target_pairs={{0,224},{32,0},{64,32},{96,64},{128,96},{160,128},{192,160},{224,1... | collective-permute-start | bytes 786440 | tf_op jit(solution)/shard_map/ppermute | solution.py:41
  151.6 6.7 %collective-permute-start.21 = (f32[512,128]{1,0:T(8,128)}, f32[512,128]{1,0:T(8,128)S(1)}, u32[]{:S(2)}, u32[]{:S(2)}) collective-permute-start(f32[512,128]{1,0:T(8,128)} %get-tuple-element.87), channel_id=1, source_target_pairs={{0,31},{1,0},{2,1},{3,2},{4,3},{5,4},{6,5},{7,6},{8,7},{9,8},{10,9... | collective-permute-start | bytes 786440 | tf_op jit(solution)/shard_map/ppermute | solution.py:41
  153.8 12.9 %all-to-all-start.6 = ((f32[8,40,128]{2,1,0:T(8,128)}), f32[8,40,128]{2,1,0:T(8,128)S(1)}, u32[]{:S(2)}, u32[]{:S(2)}) async-start(f32[8,40,128]{2,1,0:T(8,128)} %get-tuple-element.83), calls=%async_computation.6 | async-start | bytes 327680 | tf_op jit(solution)/shard_map/all_to_all | solution.py:542
  157.4 0.9 copy-start.21
  158.3 0.7 copy-start.22
  166.7 2.5 %collective-permute-start.22 = (f32[8,40,128]{2,1,0:T(8,128)S(1)}, f32[8,40,128]{2,1,0:T(8,128)S(1)}, u32[]{:S(2)}, u32[]{:S(2)}) collective-permute-start(f32[8,40,128]{2,1,0:T(8,128)S(1)} %all-to-all-done.6.own_v), channel_id=1, source_target_pairs={{0,1},{1,0},{2,3},{3,2},{4,5},{5,4},{6,7},{7,6},{8,9},{9,8},{10,11... | collective-permute-start | bytes 491528 | tf_op jit(solution)/shard_map/ppermute | solution.py:51

commit v5 on v4

--- a/solution.py
+++ b/solution.py
@@ -20,7 +20,7 @@
 SLOTS = 5
 PAY = 40
 ROWS16 = 48
-TERMS = ((0, 0), (0, 1), (1, 0))
+TERMS = ((0, 0), (0, 1), (1, 0), (1, 1), (0, 2), (2, 0))
 TALL = 1024
 PART = 512
 CHIPS = 16
@@ -142,13 +142,14 @@
         for block in range(M // BLK):
             lanes = slice(M * slot + BLK * block, M * slot + BLK * (block + 1))
             full[rows, lanes] = near[block] * -masks[slot]
-    pieces = parts_of(full[...], 2)
+    pieces = parts_of(full[...], 3)
     for index, (which, _) in enumerate(TERMS):
         turned[40 * index : 40 * (index + 1), :] = pieces[which][0:40].astype(f32)
-    turned[120:128, :] = jnp.zeros((8, NS), f32)
+    turned[240:256, :] = jnp.zeros((16, NS), f32)
     for block in range(NB):
-        piece = turned[:, BLK * block : BLK * (block + 1)].T
-        bgc_v[BLK * block : BLK * (block + 1), :] = piece.astype(bf16)
+        for half in range(2):
+            piece = turned[BLK * half : BLK * (half + 1), BLK * block : BLK * (block + 1)].T
+            bgc_v[BLK * block : BLK * (block + 1), BLK * half : BLK * (half + 1)] = piece.astype(bf16)
     copies.out(bgc_v, bgc)
     for block in range(NB):
         at = pl.multiple_of(order[block] * BLK, BLK)
@@ -241,10 +242,10 @@
     for index in range(1, CHIPS):
         value = value + came[index]
     spare = lax.broadcasted_iota(jnp.int32, (SLOT * SLOTS, K), 0) % SLOT >= MODES
-    pieces = parts_of(jnp.where(spare, 0.0, value), 2)
+    pieces = parts_of(jnp.where(spare, 0.0, value), 3)
     for index, (_, right) in enumerate(TERMS):
         stack[40 * index : 40 * (index + 1), :] = pieces[right].astype(f32)
-    stack[120:128, :] = jnp.zeros((8, K), f32)
+    stack[240:256, :] = jnp.zeros((16, K), f32)
     return stack[...].astype(bf16), (value[6:7], value[7:8], value[14:15])
 
 
@@ -503,13 +504,13 @@
     pltpu.SMEM((NB,), jnp.int32),
     pltpu.VMEM((NS, NS), bf16),
     pltpu.VMEM((2 * ROWS16, NS), bf16),
-    pltpu.VMEM((NS, K), bf16),
+    pltpu.VMEM((NS, 2 * K), bf16),
     pltpu.VMEM((CHIPS, SLOTS * SLOT, K), f32),
     pltpu.VMEM((NS, K), f32),
     pltpu.VMEM((NS, 2 * K), bf16),
     pltpu.VMEM((NS, K), f32),
     pltpu.VMEM((2 * M, K), f32),
-    pltpu.VMEM((K, K), f32),
+    pltpu.VMEM((256, K), f32),
     pltpu.VMEM((PAY, K), f32),
     pltpu.SemaphoreType.DMA((64,)),
     pltpu.SemaphoreType.DMA((NS // PART,)),
@@ -517,7 +518,7 @@
 MORE = [pltpu.VMEM((4, M, K), f32), pltpu.VMEM((NS, K), f32), pltpu.VMEM((2 * M, K), f32)]
 MORE += [pltpu.VMEM((SLOT, K), f32)] * 2
 LAST = (
-    [pltpu.VMEM((K, K), f32), pltpu.VMEM((2 * M, K), bf16), pltpu.VMEM((CHIPS, SLOTS * SLOT, K), f32)]
+    [pltpu.VMEM((256, K), f32), pltpu.VMEM((2 * M, 2 * K), bf16), pltpu.VMEM((CHIPS, SLOTS * SLOT, K), f32)]
     + [pltpu.VMEM((SLOT, K), f32)]
     + [pltpu.VMEM((2 * M, K), f32)] * 5
     + [pltpu.VMEM((2, K, M), f32)] * 2
@@ -617,13 +618,13 @@
     bgt, bgc, other = call(
         modes_kernel,
         [SM] * 2 + [HB] * 7,
-        [shape(2 * ROWS16, NS, kind=bf16), shape(NS, K, kind=bf16), shape(2, M, K)],
+        [shape(2 * ROWS16, NS, kind=bf16), shape(NS, 2 * K, kind=bf16), shape(2, M, K)],
         [pltpu.VMEM((tiles, SLOT, BLK), f32) for tiles in (NB, 4, 4, 4, 4)]
         + [
             pltpu.VMEM((ROWS16, NS), f32),
-            pltpu.VMEM((K, NS), f32),
+            pltpu.VMEM((256, NS), f32),
             pltpu.VMEM((2 * ROWS16, NS), bf16),
-            pltpu.VMEM((NS, K), bf16),
+            pltpu.VMEM((NS, 2 * K), bf16),
             pltpu.VMEM((2, K, M), f32),
             pltpu.VMEM((2, M, K), f32),
             pltpu.SemaphoreType.DMA((16,)),

time: 186 us -> 186 us (level)
  no operation moved by 1% of the time
where the time goes in v5:
time: 186 us; the launch traced here: 185 us
  starting transfers between devices  58.6 us (32%)
  Pallas kernels  53.2 us (29%)
  blocking collectives  35.1 us (19%)
  waiting for transfers between devices  24.1 us (13%)
  local copies, waits for them, and re-layouts  10.1 us (5%)
  between operations  1.89 us (1%)
    all_to_all x3, blocking collectives, coarse_phase(): lax.all_to_all(terms, 'col', 0, 0, axis_index_groups=groups, tiled=True)  35.1 us
    ppermute x18, starting transfers between devices, cyclic(): lax.ppermute(value, axis, [(s, (s + steps) % count) for s in range(count)])  25.3 us
    pallas_call x2, Pallas kernels, per_device(): call(functools.partial(step_kernel, first), [SM] + [HB] * (len(given) - 1...  18.9 us
    all_to_all x4, starting transfers between devices, coarse_phase(): own = lax.all_to_all(pay, 'row', 0, 0, tiled=True)  14.8 us
    ppermute x5, starting transfers between devices, swapped(): return lax.ppermute(value, 'col', [(s, partner(s)) for s in range(COLS)])  14.7 us
    all_to_all x4, waiting for transfers between devices, coarse_phase(): own = lax.all_to_all(pay, 'row', 0, 0, tiled=True)  11.1 us
    pallas_call x3, Pallas kernels, per_device(): call(functools.partial(image_kernel, which), [SM] + [HB] * (2 * len(which...  8.81 us
    pallas_call x1, Pallas kernels, per_device(): call(begin_kernel, [SM] + [HB] * 6, [shape(NS, K)] + FACES + [shape(ROWS,...  8.52 us
  transfers between devices with their start and end apart: 28, of which 14 were waited for; matrix products, arithmetic and copies ran while one was open for 2% of the time, Pallas kernels for 10%

profile of v5, /device:TPU:1, one launch (start us, length us, event | category | flops | bytes accessed | tf_op | source)
XLA Modules:
  0.0 184.8 jit_solution(2266003103587563685)
XLA Ops:
  1.3 0.8 broadcast_multiply_fusion
  2.2 6.5 %collective-permute-start.2 = (f32[4,8,128]{2,1,0:T(8,128)S(1)}, f32[4,8,128]{2,1,0:T(8,128)S(1)}, u32[]{:S(2)}, u32[]{:S(2)}) collective-permute-start(f32[4,8,128]{2,1,0:T(8,128)S(1)} %get-tuple-element.102), channel_id=1, source_target_pairs={{0,224},{32,0},{64,32},{96,64},{128,96},{160,128},{192,160},{224,1... | collective-permute-start | bytes 49160 | tf_op jit(solution)/shard_map/ppermute | solution.py:41
  8.6 1.0 collective-permute-start.3
  9.6 1.1 slice_bitcast_fusion
  10.7 1.3 collective-permute-start.7
  11.9 1.3 copy.14
  13.8 0.8 collective-permute-start.1
  14.7 0.8 collective-permute-start
  15.5 0.6 add_convert_fusion.masks.refs_0_
  16.1 0.6 pad.8.own
  16.8 0.6 copy-done.9
  17.4 3.0 %shard_map.77 = (f32[2,512,128]{2,1,0:T(8,128)}, f32[8,40,128]{2,1,0:T(8,128)}) custom-call(f32[4]{0:T(128)} %add_convert_fusion.masks.refs_0_, f32[16,8,128]{2,1,0:T(8,128)} %pad.8.own, f32[4,8,128]{2,1,0:T(8,128)} %copy-done.9, f32[4,8,128]{2,1,0:T(8,128)} %copy-done.10, f32[2,128,512]{2,1,0:T(8,128)} %bitcast.35), custom_call_target="tpu_custom_call" | custom-call | flops 100000000 | bytes 1048576 | tf_op jit(solution)/shard_map/pallas_call | solution.py:575
  20.5 1.7 collective-permute-start.4
  22.3 2.8 %collective-permute-start.5 = (f32[48,8,128]{2,1,0:T(8,128)S(1)}, f32[48,8,128]{2,1,0:T(8,128)S(1)}, u32[]{:S(2)}, u32[]{:S(2)}) collective-permute-start(f32[48,8,128]{2,1,0:T(8,128)S(1)} %pad_maximum_fusion.1), channel_id=1, source_target_pairs={{0,31},{1,0},{2,1},{3,2},{4,3},{5,4},{6,5},{7,6},{8,7},{9,8},{10,9... | collective-permute-start | bytes 589832 | tf_op jit(solution)/shard_map/ppermute | solution.py:41
  25.1 4.1 %all-to-all-start = ((f32[8,40,128]{2,1,0:T(8,128)}), f32[8,40,128]{2,1,0:T(8,128)S(1)}, u32[]{:S(2)}, u32[]{:S(2)}) async-start(f32[8,40,128]{2,1,0:T(8,128)} %get-tuple-element.57), calls=%async_computation | async-start | bytes 327680 | tf_op jit(solution)/shard_map/all_to_all | solution.py:543
  29.3 5.4 %collective-permute-start.8 = (f32[48,8,128]{2,1,0:T(8,128)S(1)}, f32[48,8,128]{2,1,0:T(8,128)S(1)}, u32[]{:S(2)}, u32[]{:S(2)}) collective-permute-start(f32[48,8,128]{2,1,0:T(8,128)S(1)} %slice_select_fusion), channel_id=1, source_target_pairs={{0,1},{1,0},{2,3},{3,2},{4,5},{5,4},{6,7},{7,6},{8,9},{9,8},{10,11... | collective-permute-start | bytes 589832 | tf_op jit(solution)/shard_map/ppermute | solution.py:51
  34.7 1.1 collective-permute-done.8.far
  35.8 0.7 copy-done.8
  36.5 3.7 %shard_map.79.parts = bf16[2,640,256]{2,1,0:T(8,128)(2,1)} custom-call(s32[1]{0:T(128)} %bitcast.15.core, f32[16,8,128]{2,1,0:T(8,128)} %copy-done.7, f32[20,8,128]{2,1,0:T(8,128)} %copy-done.6, f32[16,8,128]{2,1,0:T(8,128)} %copy-done.5, f32[52,8,128]{2,1,0:T(8,128)} %copy-done.3, f32[48,8,128]{2,1,0:T(8,128)} %copy-done.4, f32[48,8,128]{2,1,0:T(8,128)} %copy-done.8), custom_call_target="tpu_custom_call" | custom-call | flops 1000000 | bytes 1048576 | tf_op jit(solution)/shard_map/pallas_call | solution.py:605
  40.2 3.8 %collective-permute-start.9 = (f32[8,40,128]{2,1,0:T(8,128)S(1)}, f32[8,40,128]{2,1,0:T(8,128)S(1)}, u32[]{:S(2)}, u32[]{:S(2)}) collective-permute-start(f32[8,40,128]{2,1,0:T(8,128)S(1)} %all-to-all-done.own_v), channel_id=1, source_target_pairs={{0,1},{1,0},{2,3},{3,2},{4,5},{5,4},{6,7},{7,6},{8,9},{9,8},{10,11... | collective-permute-start | bytes 491528 | tf_op jit(solution)/shard_map/ppermute | solution.py:51
  44.0 1.0 collective-permute-done.9.other_v
  45.0 1.1 copy-done
  46.1 1.4 shard_map.80
  47.5 3.7 %all-to-all-start.1 = ((f32[16,40,128]{2,1,0:T(8,128)}), f32[16,40,128]{2,1,0:T(8,128)S(1)}, u32[]{:S(2)}, u32[]{:S(2)}) async-start(f32[16,40,128]{2,1,0:T(8,128)} %shard_map.80), calls=%async_computation.1 | async-start | bytes 655360 | tf_op jit(solution)/shard_map/all_to_all | solution.py:561
  51.3 3.3 %shard_map.78 = (bf16[96,2048]{1,0:T(8,128)(2,1)}, bf16[2048,256]{1,0:T(8,128)(2,1)}, f32[2,512,128]{2,1,0:T(8,128)}) custom-call(s32[16]{0:T(128)} %bitcast.40, f32[4]{0:T(128)} %add_convert_fusion.masks.refs_0_, f32[16,8,128]{2,1,0:T(8,128)} %pad.8.own, f32[20,8,128]{2,1,0:T(8,128)} %copy-done.6, f32[4,8,128]{2,1,0:T(8,128)} %copy-done.9, ...), custom_call_target="tpu_custom_call" | custom-call | flops 20000000000 | bytes 1048576 | tf_op jit(solution)/shard_map/pallas_call | solution.py:618
  54.6 5.1 %all-to-all-done.1.came = f32[16,40,128]{2,1,0:T(8,128)S(1)} async-done(((f32[16,40,128]{2,1,0:T(8,128)}), f32[16,40,128]{2,1,0:T(8,128)S(1)}, u32[]{:S(2)}, u32[]{:S(2)}) %all-to-all-start.1) | async-done | bytes 327712 | tf_op jit(solution)/shard_map/all_to_all | solution.py:561
  59.6 0.7 copy-done.2
  60.4 8.5 %shard_map.81 = (f32[2048,128]{1,0:T(8,128)}, f32[512,128]{1,0:T(8,128)}, f32[512,128]{1,0:T(8,128)}, f32[512,128]{1,0:T(8,128)}, f32[512,128]{1,0:T(8,128)}, /*index=5*/f32[8,40,128]{2,1,0:T(8,128)}) custom-call(s32[16]{0:T(128)} %bitcast.41, bf16[2048,2048]{1,0:T(8,128)(2,1)} %bitcast.32, bf16[96,2048]{1,0:T(8,128)(2,1)} %get-tuple-element.56.bgt.refs_2_, ...), custom_call_target="tpu_custom_call" | custom-call | flops 2000000000 | bytes 1048576 | tf_op jit(solution)/shard_map/pallas_call | solution.py:638
  69.4 1.0 collective-permute-start.10
  70.5 2.0 %collective-permute-start.13 = (f32[512,128]{1,0:T(8,128)}, f32[512,128]{1,0:T(8,128)S(1)}, u32[]{:S(2)}, u32[]{:S(2)}) collective-permute-start(f32[512,128]{1,0:T(8,128)} %get-tuple-element.66.refs_3_), channel_id=1, source_target_pairs={{0,31},{1,0},{2,1},{3,2},{4,3},{5,4},{6,5},{7,6},{8,7},{9,8},{10,9... | collective-permute-start | bytes 786440 | tf_op jit(solution)/shard_map/ppermute | solution.py:41
  72.5 3.6 %all-to-all-start.2 = ((f32[8,40,128]{2,1,0:T(8,128)}), f32[8,40,128]{2,1,0:T(8,128)S(1)}, u32[]{:S(2)}, u32[]{:S(2)}) async-start(f32[8,40,128]{2,1,0:T(8,128)} %get-tuple-element.63), calls=%async_computation.2 | async-start | bytes 327680 | tf_op jit(solution)/shard_map/all_to_all | solution.py:543
  76.4 0.6 collective-permute-done.13.refs_8_
  77.1 0.6 copy-done.17
  77.8 0.7 copy-done.19
  78.5 3.0 %shard_map.82.refs_6_.refs_9_ = f32[4,512,128]{2,1,0:T(8,128)} custom-call(f32[4]{0:T(128)} %add_convert_fusion.masks.refs_0_, f32[512,128]{1,0:T(8,128)} %get-tuple-element.64.refs_1_, f32[512,128]{1,0:T(8,128)} %get-tuple-element.65.refs_2_, f32[512,128]{1,0:T(8,128)} %get-tuple-element.66.refs_3_, f32[512,128]{1,0:T(8,128)} %get-tuple-element.67.refs_4_, ...), custom_call_target="tpu_custom_call" | custom-call | flops 20000000000 | bytes 1048576 | tf_op jit(solution)/shard_map/pallas_call | solution.py:653
  81.5 3.0 %all-to-all-done.2.own_v = f32[8,40,128]{2,1,0:T(8,128)S(1)} async-done(((f32[8,40,128]{2,1,0:T(8,128)}), f32[8,40,128]{2,1,0:T(8,128)S(1)}, u32[]{:S(2)}, u32[]{:S(2)}) %all-to-all-start.2) | async-done | bytes 163872 | tf_op jit(solution)/shard_map/all_to_all | solution.py:543
  84.5 2.3 %collective-permute-start.14 = (f32[8,40,128]{2,1,0:T(8,128)S(1)}, f32[8,40,128]{2,1,0:T(8,128)S(1)}, u32[]{:S(2)}, u32[]{:S(2)}) collective-permute-start(f32[8,40,128]{2,1,0:T(8,128)S(1)} %all-to-all-done.2.own_v), channel_id=1, source_target_pairs={{0,1},{1,0},{2,3},{3,2},{4,5},{5,4},{6,7},{7,6},{8,9},{9,8},{10,11... | collective-permute-start | bytes 491528 | tf_op jit(solution)/shard_map/ppermute | solution.py:51
  86.8 1.0 collective-permute-done.14.other_v
  87.9 0.7 shard_map.83
  88.6 11.8 %all_to_all.40.refs_4_ = f32[16,40,128]{2,1,0:T(8,128)} all-to-all(f32[16,40,128]{2,1,0:T(8,128)S(1)} %shard_map.83), channel_id=1, replica_groups={{0,2,4,6,8,10,12,14,16,18,20,22,24,26,28,30},{1,3,5,7,9,11,13,15,17,19,..., dimensions={0} | all-to-all | bytes 655360 | tf_op jit(solution)/shard_map/all_to_all | solution.py:561
  100.4 9.4 %shard_map.84 = (f32[2048,128]{1,0:T(8,128)}, f32[2048,128]{1,0:T(8,128)}, f32[8,128]{1,0:T(8,128)}, f32[512,128]{1,0:T(8,128)}, f32[512,128]{1,0:T(8,128)}, /*i...) custom-call(s32[16]{0:T(128)} %bitcast.42, bf16[2048,2048]{1,0:T(8,128)(2,1)} %bitcast.33, ...), custom_call_target="tpu_custom_call" | custom-call | flops 2000000000 | bytes 1048576 | tf_op jit(solution)/shard_map/pallas_call | solution.py:666
  109.9 1.1 collective-permute-start.16
  111.4 2.7 %collective-permute-start.18 = (f32[512,128]{1,0:T(8,128)}, f32[512,128]{1,0:T(8,128)S(1)}, u32[]{:S(2)}, u32[]{:S(2)}) collective-permute-start(f32[512,128]{1,0:T(8,128)} %get-tuple-element.75.refs_3_), channel_id=1, source_target_pairs={{0,31},{1,0},{2,1},{3,2},{4,3},{5,4},{6,5},{7,6},{8,7},{9,8},{10,9... | collective-permute-start | bytes 786440 | tf_op jit(solution)/shard_map/ppermute | solution.py:41
  114.1 3.6 %all-to-all-start.4 = ((f32[8,40,128]{2,1,0:T(8,128)}), f32[8,40,128]{2,1,0:T(8,128)S(1)}, u32[]{:S(2)}, u32[]{:S(2)}) async-start(f32[8,40,128]{2,1,0:T(8,128)} %get-tuple-element.72), calls=%async_computation.4 | async-start | bytes 327680 | tf_op jit(solution)/shard_map/all_to_all | solution.py:543
  117.7 0.7 collective-permute-done.15.refs_5_
  119.3 0.7 copy-done.20
  120.0 3.1 %shard_map.85.refs_6_ = f32[4,512,128]{2,1,0:T(8,128)} custom-call(f32[4]{0:T(128)} %add_convert_fusion.masks.refs_0_, f32[512,128]{1,0:T(8,128)} %get-tuple-element.73.refs_1_, f32[512,128]{1,0:T(8,128)} %get-tuple-element.74.refs_2_, f32[512,128]{1,0:T(8,128)} %get-tuple-element.75.refs_3_, f32[512,128]{1,0:T(8,128)} %get-tuple-element.76.refs_4_, ...), custom_call_target="tpu_custom_call" | custom-call | flops 20000000000 | bytes 1048576 | tf_op jit(solution)/shard_map/pallas_call | solution.py:653
  123.1 3.2 %all-to-all-done.4.own_v = f32[8,40,128]{2,1,0:T(8,128)S(1)} async-done(((f32[8,40,128]{2,1,0:T(8,128)}), f32[8,40,128]{2,1,0:T(8,128)S(1)}, u32[]{:S(2)}, u32[]{:S(2)}) %all-to-all-start.4) | async-done | bytes 163872 | tf_op jit(solution)/shard_map/all_to_all | solution.py:543
  126.3 1.7 collective-permute-start.19
  128.0 1.0 collective-permute-done.19.other_v
  129.0 0.7 shard_map.86
  129.8 12.0 %all_to_all.41.refs_4_ = f32[16,40,128]{2,1,0:T(8,128)} all-to-all(f32[16,40,128]{2,1,0:T(8,128)S(1)} %shard_map.86), channel_id=1, replica_groups={{0,2,4,6,8,10,12,14,16,18,20,22,24,26,28,30},{1,3,5,7,9,11,13,15,17,19,..., dimensions={0} | all-to-all | bytes 655360 | tf_op jit(solution)/shard_map/all_to_all | solution.py:561
  141.8 9.5 %shard_map.87 = (f32[2048,128]{1,0:T(8,128)}, f32[2048,128]{1,0:T(8,128)}, f32[8,128]{1,0:T(8,128)}, f32[512,128]{1,0:T(8,128)}, f32[512,128]{1,0:T(8,128)}, /*i...) custom-call(s32[16]{0:T(128)} %bitcast.43, bf16[2048,2048]{1,0:T(8,128)(2,1)} %bitcast.34, ...), custom_call_target="tpu_custom_call" | custom-call | flops 2000000000 | bytes 1048576 | tf_op jit(solution)/shard_map/pallas_call | solution.py:666
  151.7 2.2 %collective-permute-start.21 = (f32[512,128]{1,0:T(8,128)}, f32[512,128]{1,0:T(8,128)S(1)}, u32[]{:S(2)}, u32[]{:S(2)}) collective-permute-start(f32[512,128]{1,0:T(8,128)} %get-tuple-element.87), channel_id=1, source_target_pairs={{0,31},{1,0},{2,1},{3,2},{4,3},{5,4},{6,5},{7,6},{8,7},{9,8},{10,9... | collective-permute-start | bytes 786440 | tf_op jit(solution)/shard_map/ppermute | solution.py:41
  153.9 3.6 %all-to-all-start.6 = ((f32[8,40,128]{2,1,0:T(8,128)}), f32[8,40,128]{2,1,0:T(8,128)S(1)}, u32[]{:S(2)}, u32[]{:S(2)}) async-start(f32[8,40,128]{2,1,0:T(8,128)} %get-tuple-element.83), calls=%async_computation.6 | async-start | bytes 327680 | tf_op jit(solution)/shard_map/all_to_all | solution.py:543
  157.6 0.9 collective-permute-done.21.refs_4_
  158.5 0.7 copy-done.22
  159.2 2.7 %shard_map.88.local = f32[2,512,128]{2,1,0:T(8,128)} custom-call(f32[4]{0:T(128)} %add_convert_fusion.masks.refs_0_, f32[512,128]{1,0:T(8,128)} %get-tuple-element.84.refs_1_, f32[512,128]{1,0:T(8,128)} %get-tuple-element.85.refs_2_, f32[512,128]{1,0:T(8,128)} %copy-done.21, f32[512,128]{1,0:T(8,128)} %copy-done.22), custom_call_target="tpu_custom_call" | custom-call | flops 20000000000 | bytes 1048576 | tf_op jit(solution)/shard_map/pallas_call | solution.py:653
  161.9 4.9 %all-to-all-done.6.own_v = f32[8,40,128]{2,1,0:T(8,128)S(1)} async-done(((f32[8,40,128]{2,1,0:T(8,128)}), f32[8,40,128]{2,1,0:T(8,128)S(1)}, u32[]{:S(2)}, u32[]{:S(2)}) %all-to-all-start.6) | async-done | bytes 163872 | tf_op jit(solution)/shard_map/all_to_all | solution.py:543
  166.8 1.4 collective-permute-start.22
  168.3 1.0 collective-permute-done.22.other_v
  169.3 0.7 shard_map.89
  170.0 11.2 %all_to_all.42.came = f32[16,40,128]{2,1,0:T(8,128)} all-to-all(f32[16,40,128]{2,1,0:T(8,128)S(1)} %shard_map.89), channel_id=1, replica_groups={{0,2,4,6,8,10,12,14,16,18,20,22,24,26,28,30},{1,3,5,7,9,11,13,15,17,19,..., dimensions={0} | all-to-all | bytes 655360 | tf_op jit(solution)/shard_map/all_to_all | solution.py:561
  181.3 3.4 %shard_map.90 = (f32[2,128,512]{2,1,0:T(8,128)}, f32[2,128,512]{2,1,0:T(8,128)}) custom-call(bf16[2048,256]{1,0:T(8,128)(2,1)} %get-tuple-element.55.bgc.refs_3_, f32[16,40,128]{2,1,0:T(8,128)} %all_to_all.42.came, f32[2048,128]{1,0:T(8,128)} %get-tuple-element.90.residual, f32[2048,128]{1,0:T(8,128)} %get-tuple-element.70.refs_5_.first, ...), custom_call_target="tpu_custom_call" | custom-call | flops 100000000 | bytes 1048576 | tf_op jit(solution)/shard_map/pallas_call | solution.py:677
  (71 shorter events, 3.6 us)
Async XLA Ops:
  2.2 14.6 %collective-permute-start.2 = (f32[4,8,128]{2,1,0:T(8,128)S(1)}, f32[4,8,128]{2,1,0:T(8,128)S(1)}, u32[]{:S(2)}, u32[]{:S(2)}) collective-permute-start(f32[4,8,128]{2,1,0:T(8,128)S(1)} %get-tuple-element.102), channel_id=1, source_target_pairs={{0,224},{32,0},{64,32},{96,64},{128,96},{160,128},{192,160},{224,1... | collective-permute-start | bytes 49160 | tf_op jit(solution)/shard_map/ppermute | solution.py:41
  8.6 8.2 %collective-permute-start.3 = (f32[4,8,128]{2,1,0:T(8,128)S(1)}, f32[4,8,128]{2,1,0:T(8,128)S(1)}, u32[]{:S(2)}, u32[]{:S(2)}) collective-permute-start(f32[4,8,128]{2,1,0:T(8,128)S(1)} %get-tuple-element.103), channel_id=1, source_target_pairs={{0,31},{1,0},{2,1},{3,2},{4,3},{5,4},{6,5},{7,6},{8,7},{9,8},{10,9... | collective-permute-start | bytes 49160 | tf_op jit(solution)/shard_map/ppermute | solution.py:41
  10.7 18.6 %collective-permute-start.7 = (f32[128,512]{1,0:T(8,128)S(1)}, f32[128,512]{1,0:T(8,128)S(1)}, u32[]{:S(2)}, u32[]{:S(2)}) collective-permute-start(f32[128,512]{1,0:T(8,128)S(1)} %get-tuple-element.96), channel_id=1, source_target_pairs={{0,1},{1,2},{2,3},{3,4},{4,5},{5,6},{6,7},{7,8},{8,9},{9,10},{10,1... | collective-permute-start | bytes 786440 | tf_op jit(solution)/shard_map/ppermute | solution.py:41
  13.8 22.0 %copy-start.7 = (f32[16,8,128]{2,1,0:T(8,128)}, f32[16,8,128]{2,1,0:T(8,128)S(1)}, u32[]{:S(2)}) copy-start(f32[16,8,128]{2,1,0:T(8,128)S(1)} %pad_maximum_fusion.3.mine) | copy-start | bytes 196612
  13.8 6.6 %collective-permute-start.1 = (f32[16,8,128]{2,1,0:T(8,128)S(1)}, f32[16,8,128]{2,1,0:T(8,128)S(1)}, u32[]{:S(2)}, u32[]{:S(2)}) collective-permute-start(f32[16,8,128]{2,1,0:T(8,128)S(1)} %pad_maximum_fusion.3.mine), channel_id=1, source_target_pairs={{0,224},{32,0},{64,32},{96,64},{128,96},{160,128},{192,160},{224,1... | collective-permute-start | bytes 196616 | tf_op jit(solution)/shard_map/ppermute | solution.py:41
  14.7 5.7 %collective-permute-start = (f32[20,8,128]{2,1,0:T(8,128)S(1)}, f32[20,8,128]{2,1,0:T(8,128)S(1)}, u32[]{:S(2)}, u32[]{:S(2)}) collective-permute-start(f32[20,8,128]{2,1,0:T(8,128)S(1)} %pad_maximum_fusion.2), channel_id=1, source_target_pairs={{0,32},{32,64},{64,96},{96,128},{128,160},{160,192},{192,224},{224... | collective-permute-start | bytes 245768 | tf_op jit(solution)/shard_map/ppermute | solution.py:41
  16.8 0.6 copy-start.9
  16.8 12.5 %collective-permute-start.6 = (f32[128,512]{1,0:T(8,128)S(1)}, f32[128,512]{1,0:T(8,128)S(1)}, u32[]{:S(2)}, u32[]{:S(2)}) collective-permute-start(f32[128,512]{1,0:T(8,128)S(1)} %get-tuple-element.97), channel_id=1, source_target_pairs={{0,32},{32,64},{64,96},{96,128},{128,160},{160,192},{192,224},{224... | collective-permute-start | bytes 786440 | tf_op jit(solution)/shard_map/ppermute | solution.py:41
  16.8 0.6 copy-start.10
  20.4 15.4 %copy-start.5 = (f32[16,8,128]{2,1,0:T(8,128)}, f32[16,8,128]{2,1,0:T(8,128)S(1)}, u32[]{:S(2)}) copy-start(f32[16,8,128]{2,1,0:T(8,128)S(1)} %collective-permute-done.1.up) | copy-start | bytes 196612
  20.4 15.4 %copy-start.6 = (f32[20,8,128]{2,1,0:T(8,128)}, f32[20,8,128]{2,1,0:T(8,128)S(1)}, u32[]{:S(2)}) copy-start(f32[20,8,128]{2,1,0:T(8,128)S(1)} %collective-permute-done.down) | copy-start | bytes 245764
  20.5 8.7 %collective-permute-start.4 = (f32[52,8,128]{2,1,0:T(8,128)S(1)}, f32[52,8,128]{2,1,0:T(8,128)S(1)}, u32[]{:S(2)}, u32[]{:S(2)}) collective-permute-start(f32[52,8,128]{2,1,0:T(8,128)S(1)} %pad_maximum_fusion), channel_id=1, source_target_pairs={{0,1},{1,2},{2,3},{3,4},{4,5},{5,6},{6,7},{7,8},{8,9},{9,10},{10,1... | collective-permute-start | bytes 638984 | tf_op jit(solution)/shard_map/ppermute | solution.py:41
  22.3 6.9 %collective-permute-start.5 = (f32[48,8,128]{2,1,0:T(8,128)S(1)}, f32[48,8,128]{2,1,0:T(8,128)S(1)}, u32[]{:S(2)}, u32[]{:S(2)}) collective-permute-start(f32[48,8,128]{2,1,0:T(8,128)S(1)} %pad_maximum_fusion.1), channel_id=1, source_target_pairs={{0,31},{1,0},{2,1},{3,2},{4,3},{5,4},{6,5},{7,6},{8,7},{9,8},{10,9... | collective-permute-start | bytes 589832 | tf_op jit(solution)/shard_map/ppermute | solution.py:41
  25.1 15.0 %all-to-all-start = ((f32[8,40,128]{2,1,0:T(8,128)}), f32[8,40,128]{2,1,0:T(8,128)S(1)}, u32[]{:S(2)}, u32[]{:S(2)}) async-start(f32[8,40,128]{2,1,0:T(8,128)} %get-tuple-element.57), calls=%async_computation | async-start | bytes 327680 | tf_op jit(solution)/shard_map/all_to_all | solution.py:543
  29.2 22.0 %copy-start.11 = (f32[128,512]{1,0:T(8,128)}, f32[128,512]{1,0:T(8,128)S(1)}, u32[]{:S(2)}) copy-start(f32[128,512]{1,0:T(8,128)S(1)} %collective-permute-done.7.from_w) | copy-start | bytes 786436
  29.2 22.0 %copy-start.12 = (f32[128,512]{1,0:T(8,128)}, f32[128,512]{1,0:T(8,128)S(1)}, u32[]{:S(2)}) copy-start(f32[128,512]{1,0:T(8,128)S(1)} %collective-permute-done.6.from_n) | copy-start | bytes 786436
  29.3 6.6 %copy-start.4 = (f32[48,8,128]{2,1,0:T(8,128)}, f32[48,8,128]{2,1,0:T(8,128)S(1)}, u32[]{:S(2)}) copy-start(f32[48,8,128]{2,1,0:T(8,128)S(1)} %collective-permute-done.5.left) | copy-start | bytes 589828
  29.3 6.6 %copy-start.3 = (f32[52,8,128]{2,1,0:T(8,128)}, f32[52,8,128]{2,1,0:T(8,128)S(1)}, u32[]{:S(2)}) copy-start(f32[52,8,128]{2,1,0:T(8,128)S(1)} %collective-permute-done.4.right) | copy-start | bytes 638980
  29.3 6.5 %collective-permute-start.8 = (f32[48,8,128]{2,1,0:T(8,128)S(1)}, f32[48,8,128]{2,1,0:T(8,128)S(1)}, u32[]{:S(2)}, u32[]{:S(2)}) collective-permute-start(f32[48,8,128]{2,1,0:T(8,128)S(1)} %slice_select_fusion), channel_id=1, source_target_pairs={{0,1},{1,0},{2,3},{3,2},{4,5},{5,4},{6,7},{7,6},{8,9},{9,8},{10,11... | collective-permute-start | bytes 589832 | tf_op jit(solution)/shard_map/ppermute | solution.py:51
  35.8 0.7 copy-start.8
  40.2 4.8 %collective-permute-start.9 = (f32[8,40,128]{2,1,0:T(8,128)S(1)}, f32[8,40,128]{2,1,0:T(8,128)S(1)}, u32[]{:S(2)}, u32[]{:S(2)}) collective-permute-start(f32[8,40,128]{2,1,0:T(8,128)S(1)} %all-to-all-done.own_v), channel_id=1, source_target_pairs={{0,1},{1,0},{2,3},{3,2},{4,5},{5,4},{6,7},{7,6},{8,9},{9,8},{10,11... | collective-permute-start | bytes 491528 | tf_op jit(solution)/shard_map/ppermute | solution.py:51
  45.0 1.1 copy-start
  47.5 12.1 %all-to-all-start.1 = ((f32[16,40,128]{2,1,0:T(8,128)}), f32[16,40,128]{2,1,0:T(8,128)S(1)}, u32[]{:S(2)}, u32[]{:S(2)}) async-start(f32[16,40,128]{2,1,0:T(8,128)} %shard_map.80), calls=%async_computation.1 | async-start | bytes 655360 | tf_op jit(solution)/shard_map/all_to_all | solution.py:561
  59.6 0.7 copy-start.2
  68.9 7.2 %collective-permute-start.11 = (f32[512,128]{1,0:T(8,128)}, f32[512,128]{1,0:T(8,128)S(1)}, u32[]{:S(2)}, u32[]{:S(2)}) collective-permute-start(f32[512,128]{1,0:T(8,128)} %get-tuple-element.64.refs_1_), channel_id=1, source_target_pairs={{0,224},{32,0},{64,32},{96,64},{128,96},{160,128},{192,160},{224,1... | collective-permute-start | bytes 786440 | tf_op jit(solution)/shard_map/ppermute | solution.py:41
  69.4 7.0 %collective-permute-start.10 = (f32[512,128]{1,0:T(8,128)}, f32[512,128]{1,0:T(8,128)S(1)}, u32[]{:S(2)}, u32[]{:S(2)}) collective-permute-start(f32[512,128]{1,0:T(8,128)} %get-tuple-element.65.refs_2_), channel_id=1, source_target_pairs={{0,32},{32,64},{64,96},{96,128},{128,160},{160,192},{192,224},{224... | collective-permute-start | bytes 786440 | tf_op jit(solution)/shard_map/ppermute | solution.py:41
  70.5 6.6 %collective-permute-start.13 = (f32[512,128]{1,0:T(8,128)}, f32[512,128]{1,0:T(8,128)S(1)}, u32[]{:S(2)}, u32[]{:S(2)}) collective-permute-start(f32[512,128]{1,0:T(8,128)} %get-tuple-element.66.refs_3_), channel_id=1, source_target_pairs={{0,31},{1,0},{2,1},{3,2},{4,3},{5,4},{6,5},{7,6},{8,7},{9,8},{10,9... | collective-permute-start | bytes 786440 | tf_op jit(solution)/shard_map/ppermute | solution.py:41
  72.5 4.5 %collective-permute-start.12 = (f32[512,128]{1,0:T(8,128)}, f32[512,128]{1,0:T(8,128)S(1)}, u32[]{:S(2)}, u32[]{:S(2)}) collective-permute-start(f32[512,128]{1,0:T(8,128)} %get-tuple-element.67.refs_4_), channel_id=1, source_target_pairs={{0,1},{1,2},{2,3},{3,4},{4,5},{5,6},{6,7},{7,8},{8,9},{9,10},{10,1... | collective-permute-start | bytes 786440 | tf_op jit(solution)/shard_map/ppermute | solution.py:41
  72.5 12.0 %all-to-all-start.2 = ((f32[8,40,128]{2,1,0:T(8,128)}), f32[8,40,128]{2,1,0:T(8,128)S(1)}, u32[]{:S(2)}, u32[]{:S(2)}) async-start(f32[8,40,128]{2,1,0:T(8,128)} %get-tuple-element.63), calls=%async_computation.2 | async-start | bytes 327680 | tf_op jit(solution)/shard_map/all_to_all | solution.py:543
  76.1 11.8 %copy-start.1 = (bf16[2,640,256]{2,1,0:T(8,128)(2,1)S(1)}, bf16[2,640,256]{2,1,0:T(8,128)(2,1)}, u32[]{:S(2)}) copy-start(bf16[2,640,256]{2,1,0:T(8,128)(2,1)} %shard_map.79.parts) | copy-start | bytes 1966084
  76.1 0.9 copy-start.13
  76.4 0.7 copy-start.15
  77.0 0.7 copy-start.17
  77.8 0.7 copy-start.19
  84.5 3.4 %collective-permute-start.14 = (f32[8,40,128]{2,1,0:T(8,128)S(1)}, f32[8,40,128]{2,1,0:T(8,128)S(1)}, u32[]{:S(2)}, u32[]{:S(2)}) collective-permute-start(f32[8,40,128]{2,1,0:T(8,128)S(1)} %all-to-all-done.2.own_v), channel_id=1, source_target_pairs={{0,1},{1,0},{2,3},{3,2},{4,5},{5,4},{6,7},{7,6},{8,9},{9,8},{10,11... | collective-permute-start | bytes 491528 | tf_op jit(solution)/shard_map/ppermute | solution.py:51
  109.9 7.9 %collective-permute-start.16 = (f32[512,128]{1,0:T(8,128)}, f32[512,128]{1,0:T(8,128)S(1)}, u32[]{:S(2)}, u32[]{:S(2)}) collective-permute-start(f32[512,128]{1,0:T(8,128)} %get-tuple-element.73.refs_1_), channel_id=1, source_target_pairs={{0,224},{32,0},{64,32},{96,64},{128,96},{160,128},{192,160},{224,1... | collective-permute-start | bytes 786440 | tf_op jit(solution)/shard_map/ppermute | solution.py:41
  110.9 7.5 %collective-permute-start.15 = (f32[512,128]{1,0:T(8,128)}, f32[512,128]{1,0:T(8,128)S(1)}, u32[]{:S(2)}, u32[]{:S(2)}) collective-permute-start(f32[512,128]{1,0:T(8,128)} %get-tuple-element.74.refs_2_), channel_id=1, source_target_pairs={{0,32},{32,64},{64,96},{96,128},{128,160},{160,192},{192,224},{224... | collective-permute-start | bytes 786440 | tf_op jit(solution)/shard_map/ppermute | solution.py:41
  111.4 7.2 %collective-permute-start.18 = (f32[512,128]{1,0:T(8,128)}, f32[512,128]{1,0:T(8,128)S(1)}, u32[]{:S(2)}, u32[]{:S(2)}) collective-permute-start(f32[512,128]{1,0:T(8,128)} %get-tuple-element.75.refs_3_), channel_id=1, source_target_pairs={{0,31},{1,0},{2,1},{3,2},{4,3},{5,4},{6,5},{7,6},{8,7},{9,8},{10,9... | collective-permute-start | bytes 786440 | tf_op jit(solution)/shard_map/ppermute | solution.py:41
  114.1 4.5 %collective-permute-start.17 = (f32[512,128]{1,0:T(8,128)}, f32[512,128]{1,0:T(8,128)S(1)}, u32[]{:S(2)}, u32[]{:S(2)}) collective-permute-start(f32[512,128]{1,0:T(8,128)} %get-tuple-element.76.refs_4_), channel_id=1, source_target_pairs={{0,1},{1,2},{2,3},{3,4},{4,5},{5,6},{6,7},{7,8},{8,9},{9,10},{10,1... | collective-permute-start | bytes 786440 | tf_op jit(solution)/shard_map/ppermute | solution.py:41
  114.1 12.2 %all-to-all-start.4 = ((f32[8,40,128]{2,1,0:T(8,128)}), f32[8,40,128]{2,1,0:T(8,128)S(1)}, u32[]{:S(2)}, u32[]{:S(2)}) async-start(f32[8,40,128]{2,1,0:T(8,128)} %get-tuple-element.72), calls=%async_computation.4 | async-start | bytes 327680 | tf_op jit(solution)/shard_map/all_to_all | solution.py:543
  117.7 0.9 copy-start.14
  118.4 0.7 copy-start.16
  118.6 0.7 copy-start.18
  119.3 0.7 copy-start.20
  126.3 2.8 %collective-permute-start.19 = (f32[8,40,128]{2,1,0:T(8,128)S(1)}, f32[8,40,128]{2,1,0:T(8,128)S(1)}, u32[]{:S(2)}, u32[]{:S(2)}) collective-permute-start(f32[8,40,128]{2,1,0:T(8,128)S(1)} %all-to-all-done.4.own_v), channel_id=1, source_target_pairs={{0,1},{1,0},{2,3},{3,2},{4,5},{5,4},{6,7},{7,6},{8,9},{9,8},{10,11... | collective-permute-start | bytes 491528 | tf_op jit(solution)/shard_map/ppermute | solution.py:51
  151.3 6.2 %collective-permute-start.20 = (f32[512,128]{1,0:T(8,128)}, f32[512,128]{1,0:T(8,128)S(1)}, u32[]{:S(2)}, u32[]{:S(2)}) collective-permute-start(f32[512,128]{1,0:T(8,128)} %get-tuple-element.86), channel_id=1, source_target_pairs={{0,224},{32,0},{64,32},{96,64},{128,96},{160,128},{192,160},{224,1... | collective-permute-start | bytes 786440 | tf_op jit(solution)/shard_map/ppermute | solution.py:41
  151.7 6.7 %collective-permute-start.21 = (f32[512,128]{1,0:T(8,128)}, f32[512,128]{1,0:T(8,128)S(1)}, u32[]{:S(2)}, u32[]{:S(2)}) collective-permute-start(f32[512,128]{1,0:T(8,128)} %get-tuple-element.87), channel_id=1, source_target_pairs={{0,31},{1,0},{2,1},{3,2},{4,3},{5,4},{6,5},{7,6},{8,7},{9,8},{10,9... | collective-permute-start | bytes 786440 | tf_op jit(solution)/shard_map/ppermute | solution.py:41
  153.9 12.9 %all-to-all-start.6 = ((f32[8,40,128]{2,1,0:T(8,128)}), f32[8,40,128]{2,1,0:T(8,128)S(1)}, u32[]{:S(2)}, u32[]{:S(2)}) async-start(f32[8,40,128]{2,1,0:T(8,128)} %get-tuple-element.83), calls=%async_computation.6 | async-start | bytes 327680 | tf_op jit(solution)/shard_map/all_to_all | solution.py:543
  157.5 0.9 copy-start.21
  158.5 0.7 copy-start.22
  166.8 2.5 %collective-permute-start.22 = (f32[8,40,128]{2,1,0:T(8,128)S(1)}, f32[8,40,128]{2,1,0:T(8,128)S(1)}, u32[]{:S(2)}, u32[]{:S(2)}) collective-permute-start(f32[8,40,128]{2,1,0:T(8,128)S(1)} %all-to-all-done.6.own_v), channel_id=1, source_target_pairs={{0,1},{1,0},{2,3},{3,2},{4,5},{5,4},{6,7},{7,6},{8,9},{9,8},{10,11... | collective-permute-start | bytes 491528 | tf_op jit(solution)/shard_map/ppermute | solution.py:51
